TPU v7x, 512 devices: a whole 4x8x8 slice. The times are simulated.
512 devices in a mesh: dom: 128 (over z, y, core), mp: 4 (over x).
Axes of the slice: x: 4, y: 8, z: 8, core: 2. Of those that a mesh axis runs over, the one named last changes fastest.
Arguments:
- vertex_embeddings: bfloat16 [32768, 512], P('dom', 'mp'), may hold values from -6 to 6
- upstream_sensitivity: bfloat16 [32768, 512], P('dom', 'mp'), may hold values from -6 to 6
- asking_projector_matrix: bfloat16 [512, 512], P(None, 'mp'), may hold values from -0.25 to 0.25
- lookup_projector_matrix: bfloat16 [512, 512], P(None, 'mp'), may hold values from -0.25 to 0.25
- content_projector_matrix: bfloat16 [512, 512], P(None, 'mp'), may hold values from -0.25 to 0.25
- channel_logit_scales: float32 [8], P('mp'), may hold values from 2 to 8
- adjacent_block_table: int32 [256, 8], P('dom'), may hold values from 0 to 255, as said below
- compressed_link_bitmap: int32 [256, 9, 1024], P('dom'), may hold values from 0 to 65535, as said below
Outputs:
- attended: bfloat16 [32768, 512], P('dom', 'mp')
- input_grad: bfloat16 [32768, 512], P('dom', 'mp')
- grad_query: float32 [512, 512], P(None, 'mp')
- grad_key: float32 [512, 512], P(None, 'mp')
- grad_value: float32 [512, 512], P(None, 'mp')
Inputs may be any that keep to these rules, and one draw needn't show every extreme that they name: `adjacent_block_table`: consecutive groups of 2 blocks form partitions. Every block listed for a block lies in its own partition or in the partition just before or just after it. All blocks of one partition that list blocks of the partition before (after) it list the same block of it. The first listed block lies in the partition before and the second in the partition after, where those exist, else in the own partition. `compressed_link_bitmap`: each word holds 16 edge bits of one tile in its lowest bits. Tile 0 of each block has every diagonal edge. For each block, the tiles of its first two or more listed neighbours may hold edges and the tiles after them have none.
All inputs are finite; a program needn't handle non-finite values.
Results may differ from a plain program's by a relative error of at most 0.017.
Values may be sent and summed in bfloat16 or wider, within the bound.
No kernel may reach another device: no remote copies, remote signals or barrier semaphores. Data moves between devices by JAX's collectives and lax.ppermute only.
A program may use at most 64 MiB of HBM per device.

v0:
```python
import jax
import jax.numpy as jnp
from jax import lax
from jax.sharding import PartitionSpec as P

epsilon = 1e-06


def extended_2(cells, sides, width):
    for axis, dim in sides:
        count = lax.axis_size(axis)
        ends = count - 1
        head = lax.slice_in_dim(cells, 0, width, axis=dim)
        tail = lax.slice_in_dim(cells, cells.shape[dim] - width, cells.shape[dim], axis=dim)
        cells = jnp.concatenate(
            [
                lax.ppermute(tail, axis, [(i, (i + 1) % count) for i in range(ends)]),
                cells,
                lax.ppermute(head, axis, [((i + 1) % count, i) for i in range(ends)]),
            ],
            axis=dim,
        )
    return cells


def from_behind(value, axis, steps):
    count = lax.axis_size(axis)
    leading, last = (max(0, -steps), min(count, count - steps))
    return lax.ppermute(value, axis, [(source, source + steps) for source in range(leading, last)])


def head_norm(projected, resident_channels):
    head_split = projected.reshape(projected.shape[0], resident_channels, -1)
    scale_rows = lax.rsqrt(jnp.mean(head_split * head_split, axis=-1, keepdims=True) + epsilon)
    return (head_split * scale_rows, scale_rows)


def norm_back(upstream, unit_vec, scale_rows):
    return scale_rows * (
        upstream - unit_vec * jnp.mean(upstream * unit_vec, axis=-1, keepdims=True)
    )


def shards(
    vertex_embeddings,
    upstream_sensitivity,
    asking_projector_matrix,
    lookup_projector_matrix,
    content_projector_matrix,
    channel_logit_scales,
    adjacent_block_table,
    compressed_link_bitmap,
):
    blocks_here, slot_count = adjacent_block_table.shape
    row_count = upstream_sensitivity.shape[0]
    block_len = row_count // blocks_here
    feat_width = asking_projector_matrix.shape[1]
    resident_channels = channel_logit_scales.shape[0]
    channel_extent = feat_width // resident_channels
    part_count = lax.axis_size("dom")
    my_part = lax.axis_index("dom")
    gathered = lax.all_gather(vertex_embeddings, "mp", axis=1, tiled=True)
    w_joint = jnp.concatenate(
        [asking_projector_matrix, lookup_projector_matrix, content_projector_matrix], axis=1
    )
    projected = jnp.dot(gathered, w_joint, preferred_element_type=jnp.float32)
    query_unit, query_scale = head_norm(projected[:, :feat_width], resident_channels)
    key_unit, key_scale = head_norm(projected[:, feat_width : 2 * feat_width], resident_channels)
    query_round = query_unit.astype(jnp.bfloat16).reshape(
        blocks_here, block_len, resident_channels, channel_extent
    )
    own_kv = jnp.concatenate(
        [
            key_unit.reshape(row_count, feat_width).astype(jnp.bfloat16),
            projected[:, 2 * feat_width :].astype(jnp.bfloat16),
        ],
        axis=1,
    )
    logit_scaling_factor = channel_logit_scales / channel_extent
    offset = adjacent_block_table // blocks_here - my_part
    within = adjacent_block_table % blocks_here
    local_order = jnp.arange(blocks_here, dtype=jnp.int32)
    extended = extended_2(own_kv, (("dom", 0),), row_count)
    extended = extended.reshape(3 * blocks_here, block_len, 2 * feat_width)
    position = (offset + 1) * blocks_here + within
    own_position = blocks_here + local_order
    tile_pos = jnp.concatenate([own_position[:, None], position], axis=1)
    tile_data = jnp.take(extended, tile_pos.reshape(-1), axis=0).reshape(
        blocks_here, slot_count + 1, block_len, 2 * feat_width
    )
    key_tiles = tile_data[..., :feat_width].reshape(
        blocks_here, slot_count + 1, block_len, resident_channels, channel_extent
    )
    value_tiles = tile_data[..., feat_width:].reshape(
        blocks_here, slot_count + 1, block_len, resident_channels, channel_extent
    )
    bit_place = jnp.arange(16, dtype=jnp.int32)
    edge_bits = jnp.right_shift(compressed_link_bitmap[..., None], bit_place) & 1
    edge_bits = edge_bits.reshape(blocks_here, slot_count + 1, block_len, block_len)
    scores = jnp.einsum(
        "bqhd,btkhd->bhtqk", query_round, key_tiles, preferred_element_type=jnp.float32
    )
    scores = scores * logit_scaling_factor[None, :, None, None, None]
    live_mask = (edge_bits != 0)[:, None]
    exp_scores = jnp.where(live_mask, jnp.exp(scores), 0.0)
    row_total = jnp.sum(exp_scores, axis=(2, 4), keepdims=True)
    weights = exp_scores / row_total
    weights_round = weights.astype(jnp.bfloat16)
    attended = jnp.einsum(
        "bhtqk,btkhd->bqhd", weights_round, value_tiles, preferred_element_type=jnp.float32
    )
    attended = attended.astype(jnp.bfloat16).reshape(row_count, feat_width)
    grad_attn = upstream_sensitivity.reshape(
        blocks_here, block_len, resident_channels, channel_extent
    )
    grad_weights = jnp.einsum(
        "bqhd,btkhd->bhtqk", grad_attn, value_tiles, preferred_element_type=jnp.float32
    )
    row_delta = jnp.sum(weights * grad_weights, axis=(2, 4), keepdims=True)
    grad_scores = (weights * (grad_weights - row_delta)).astype(jnp.bfloat16)
    grad_qn = jnp.einsum(
        "bhtqk,btkhd->bqhd", grad_scores, key_tiles, preferred_element_type=jnp.float32
    )
    grad_qn = grad_qn * logit_scaling_factor[None, None, :, None]
    grad_kn = jnp.einsum(
        "bhtqk,bqhd->btkhd", grad_scores, query_round, preferred_element_type=jnp.float32
    )
    grad_kn = grad_kn * logit_scaling_factor[None, None, None, :, None]
    grad_value = jnp.einsum(
        "bhtqk,bqhd->btkhd", weights_round, grad_attn, preferred_element_type=jnp.float32
    )
    tile_grads = jnp.concatenate(
        [
            grad_kn.reshape(blocks_here, slot_count + 1, block_len, feat_width),
            grad_value.reshape(blocks_here, slot_count + 1, block_len, feat_width),
        ],
        axis=-1,
    )
    tile_grads = tile_grads.reshape(blocks_here * (slot_count + 1), block_len * 2 * feat_width)
    ext_grads = (
        jnp.zeros((extended.shape[0], block_len * 2 * feat_width), jnp.float32)
        .at[tile_pos.reshape(-1)]
        .add(tile_grads)
    )
    own_grads = ext_grads[blocks_here : 2 * blocks_here]
    for facing in (-1, 1):
        rim_piece = ext_grads[:blocks_here] if facing == -1 else ext_grads[2 * blocks_here :]
        own_grads = own_grads + from_behind(rim_piece.astype(jnp.bfloat16), "dom", facing).astype(
            rim_piece.dtype
        )
    summed = own_grads.reshape(row_count, 2 * feat_width)
    grad_q = norm_back(
        grad_qn.reshape(row_count, resident_channels, channel_extent), query_unit, query_scale
    ).reshape(row_count, feat_width)
    grad_k = norm_back(
        summed[:, :feat_width].reshape(row_count, resident_channels, channel_extent),
        key_unit,
        key_scale,
    ).reshape(row_count, feat_width)
    grads_joint = jnp.concatenate([grad_q, grad_k, summed[:, feat_width:]], axis=1).astype(
        jnp.bfloat16
    )
    input_part = jnp.einsum("rc,dc->rd", grads_joint, w_joint, preferred_element_type=jnp.float32)
    input_grad = lax.psum_scatter(
        input_part.astype(jnp.bfloat16), "mp", scatter_dimension=1, tiled=True
    )
    grad_scale = (part_count * row_count) ** (-0.5)
    weight_term = jnp.einsum("rd,rc->dc", gathered, grads_joint, preferred_element_type=jnp.float32)
    weight_total = lax.psum(weight_term, "dom") * grad_scale
    grad_query = weight_total[:, :feat_width]
    grad_key = weight_total[:, feat_width : 2 * feat_width]
    grad_value_out = weight_total[:, 2 * feat_width :]
    return (attended, input_grad, grad_query, grad_key, grad_value_out)


def solution(mesh):
    in_specs = (
        P("dom", "mp"),
        P("dom", "mp"),
        P(None, "mp"),
        P(None, "mp"),
        P(None, "mp"),
        P("mp"),
        P("dom", None),
        P("dom", None, None),
    )
    out_specs = (P("dom", "mp"), P("dom", "mp"), P(None, "mp"), P(None, "mp"), P(None, "mp"))
    return jax.shard_map(shards, mesh=mesh, in_specs=in_specs, out_specs=out_specs, check_vma=False)
```

profile of v0, /device:TPU:1, one launch (start us, length us, event | category | flops | bytes accessed | tf_op | source)
XLA Modules:
  0.0 292.0 jit_solution(1266042511014244479)
XLA Ops:
  8.1 0.9 constant_dynamic-update-slice_fusion.2
  9.0 10.5 %all_gather.3 = bf16[256,512]{1,0:T(8,128)(2,1)S(1)} all-gather(bf16[256,128]{1,0:T(8,128)(2,1)} %param.8), channel_id=1, replica_groups=mesh['dom'=128,'mp'=4] {'mp'}, dimensions={1}, use_global_device_ids=true | all-gather | bytes 327680 | tf_op jit(solution)/shard_map/all_gather | solution.py:62
  19.5 0.9 constant_dynamic-update-slice_fusion.1
  20.4 0.9 constant_dynamic-update-slice_fusion
  22.6 6.4 %collective-permute-start = (bf16[256,256]{0,1:T(8,128)(2,1)S(1)}, bf16[256,256]{0,1:T(8,128)(2,1)S(1)}, u32[]{:S(2)}, u32[]{:S(2)}) collective-permute-start(bf16[256,256]{0,1:T(8,128)(2,1)S(1)} %pad_maximum_fusion.3), channel_id=1, source_target_pairs={{0,4},{4,8},{8,12},{12,16},{16,20},{20,24},{24,28},{28,32},{32,36}... | collective-permute-start | bytes 393224 | tf_op jit(solution)/shard_map/ppermute | solution.py:17
  28.9 4.5 %collective-permute-start.1 = (bf16[256,256]{0,1:T(8,128)(2,1)S(1)}, bf16[256,256]{0,1:T(8,128)(2,1)S(1)}, u32[]{:S(2)}, u32[]{:S(2)}) collective-permute-start(bf16[256,256]{0,1:T(8,128)(2,1)S(1)} %pad_maximum_fusion.3), channel_id=1, source_target_pairs={{4,0},{8,4},{12,8},{16,12},{20,16},{24,20},{28,24},{32,28},{36,32}... | collective-permute-start | bytes 393224 | tf_op jit(solution)/shard_map/ppermute | solution.py:19
  33.8 7.3 %shift_right_arithmetic.24 = s32[2,9,1024,16]{3,2,1,0:T(8,128)} broadcast(s32[2,9,1024]{2,1,0:T(8,128)S(1)} %copy.82), dimensions={0,1,2} | broadcast | bytes 1253376 | tf_op jit(solution)/shard_map/shift_right_arithmetic | solution.py:98
  41.1 6.2 %shift_right_arithmetic.25 = s32[2,9,128,128]{3,2,1,0:T(8,128)S(1)} reshape(s32[2,9,1024,16]{3,2,1,0:T(8,128)} %shift_right_arithmetic.24) | data formatting | bytes 2359296 | tf_op jit(solution)/shard_map/shift_right_arithmetic | solution.py:98
  50.5 0.9 fusion.4
  51.3 0.9 convolution_bitcast_fusion
  52.2 0.9 fusion
  53.2 0.8 fusion.2
  55.2 2.0 copy.101
  57.2 2.0 pad.14
  59.2 3.5 %copy.127 = f32[3,8,128,256]{3,1,2,0:T(8,128)} copy(f32[3,8,128,256]{3,2,1,0:T(8,128)S(1)} %bitcast.132) | data formatting | bytes 6291456
  62.6 4.9 %scatter_custom_fusion = f32[6,32768]{1,0:T(8,128)S(1)} fusion(s32[18]{0:T(128)S(1)} %fusion.34, f32[18,32768]{1,0:T(8,128)} %bitcast.138, f32[]{:T(128)} %constant.64.clone.1), kind=kCustom, calls=%fused_computation.27 | custom fusion | flops 589824 | bytes 786944 | tf_op jit(solution)/shard_map/scatter-add | solution.py:143
  67.8 1.9 collective-permute-start.2
  69.7 3.6 %collective-permute-start.3 = (bf16[2,32768]{1,0:T(2,128)(2,1)S(1)}, bf16[2,32768]{1,0:T(2,128)(2,1)S(1)}, u32[]{:S(2)}, u32[]{:S(2)}) collective-permute-start(bf16[2,32768]{1,0:T(2,128)(2,1)S(1)} %get-tuple-element.35), channel_id=1, source_target_pairs={{0,4},{4,8},{8,12},{12,16},{16,20},{20,24},{24,28},{28,32},{32,36}... | collective-permute-start | bytes 393224 | tf_op jit(solution)/shard_map/ppermute | solution.py:29
  73.4 0.8 copy.95
  74.1 1.2 collective-permute-done.3
  76.6 1.1 copy.126
  77.7 1.0 fusion.24
  79.3 1.1 convolution_bitcast_fusion.1
  80.5 2.2 convolution_convert_fusion
  82.7 1.8 copy.122
  84.5 0.9 fusion.9
  86.3 192.9 %all-reduce.2.cloned.1.call-done = f32[512,384]{0,1:T(8,128)} async-done(((f32[512,384]{0,1:T(8,128)}), f32[512,384]{0,1:T(8,128)}) %all-reduce.2.cloned.1.call-update) | async-done | bytes 786448 | tf_op jit(solution)/shard_map/psum | solution.py:169
  279.2 1.2 broadcast_multiply_fusion
  280.5 0.8 copy.105
  281.4 0.8 copy.106
  282.2 0.8 copy.107
  283.0 1.6 copy.123
  (76 shorter events, 8.8 us)
Async XLA Ops:
  8.0 25.5 %copy-start.9 = (s32[2,8]{1,0:T(2,128)S(1)}, s32[2,8]{1,0:T(2,128)}, u32[]{:S(2)}) copy-start(s32[2,8]{1,0:T(2,128)} %param.14) | copy-start | bytes 196
  8.0 25.7 %copy-start.7 = (s32[2,9,1024]{2,0,1:T(2,128)S(1)}, s32[2,9,1024]{2,0,1:T(2,128)}, u32[]{:S(2)}) copy-start(s32[2,9,1024]{2,0,1:T(2,128)} %param.15) | copy-start | bytes 221188
  8.0 271.2 %all-reduce.2.cloned.1.call-start = ((), (), s32[]{:S(2)}) async-start(), calls=%async_computation.1 | async-start | bytes 1572864 | tf_op jit(solution)/shard_map/psum | solution.py:169
  21.4 0.7 copy-start.2
  22.6 25.9 %collective-permute-start = (bf16[256,256]{0,1:T(8,128)(2,1)S(1)}, bf16[256,256]{0,1:T(8,128)(2,1)S(1)}, u32[]{:S(2)}, u32[]{:S(2)}) collective-permute-start(bf16[256,256]{0,1:T(8,128)(2,1)S(1)} %pad_maximum_fusion.3), channel_id=1, source_target_pairs={{0,4},{4,8},{8,12},{12,16},{16,20},{20,24},{24,28},{28,32},{32,36}... | collective-permute-start | bytes 393224 | tf_op jit(solution)/shard_map/ppermute | solution.py:17
  28.9 19.5 %collective-permute-start.1 = (bf16[256,256]{0,1:T(8,128)(2,1)S(1)}, bf16[256,256]{0,1:T(8,128)(2,1)S(1)}, u32[]{:S(2)}, u32[]{:S(2)}) collective-permute-start(bf16[256,256]{0,1:T(8,128)(2,1)S(1)} %pad_maximum_fusion.3), channel_id=1, source_target_pairs={{4,0},{8,4},{12,8},{16,12},{20,16},{24,20},{28,24},{32,28},{36,32}... | collective-permute-start | bytes 393224 | tf_op jit(solution)/shard_map/ppermute | solution.py:19
  41.1 6.6 %copy-start.10 = (f32[2]{0:T(128)S(1)}, f32[2]{0:T(128)}, u32[]{:S(2)}) copy-start(f32[2]{0:T(128)} %param.13) | copy-start | bytes 28
  47.3 0.9 copy-start.8
  50.5 1.7 copy-start.3
  51.3 1.8 copy-start
  67.8 6.3 %collective-permute-start.2 = (bf16[2,32768]{1,0:T(2,128)(2,1)S(1)}, bf16[2,32768]{1,0:T(2,128)(2,1)S(1)}, u32[]{:S(2)}, u32[]{:S(2)}) collective-permute-start(bf16[2,32768]{1,0:T(2,128)(2,1)S(1)} %get-tuple-element.34), channel_id=1, source_target_pairs={{4,0},{8,4},{12,8},{16,12},{20,16},{24,20},{28,24},{32,28},{36,32}... | collective-permute-start | bytes 393224 | tf_op jit(solution)/shard_map/ppermute | solution.py:29
  69.7 5.6 %collective-permute-start.3 = (bf16[2,32768]{1,0:T(2,128)(2,1)S(1)}, bf16[2,32768]{1,0:T(2,128)(2,1)S(1)}, u32[]{:S(2)}, u32[]{:S(2)}) collective-permute-start(bf16[2,32768]{1,0:T(2,128)(2,1)S(1)} %get-tuple-element.35), channel_id=1, source_target_pairs={{0,4},{4,8},{8,12},{12,16},{16,20},{20,24},{24,28},{28,32},{32,36}... | collective-permute-start | bytes 393224 | tf_op jit(solution)/shard_map/ppermute | solution.py:29
  76.6 7.9 %copy-start.1 = (f32[2,2,9,128,128]{4,3,2,1,0:T(8,128)S(1)}, f32[2,2,9,128,128]{4,3,2,1,0:T(8,128)}, u32[]{:S(2)}) copy-start(f32[2,2,9,128,128]{4,3,2,1,0:T(8,128)} %copy-done) | copy-start | bytes 7077892
  78.7 0.6 copy-start.5
  78.7 0.6 copy-start.6
  80.5 4.1 %copy-start.4 = (bf16[2,9,128,128]{2,3,1,0:T(8,128)(2,1)S(1)}, bf16[2,9,128,128]{2,3,1,0:T(8,128)(2,1)}, u32[]{:S(2)}) copy-start(bf16[2,9,128,128]{2,3,1,0:T(8,128)(2,1)} %copy-done.3) | copy-start | bytes 1769476
  80.5 202.5 %reduce-scatter.4.cloned.1.call-start = ((), (), s32[]{:S(2)}) async-start(), calls=%async_computation.2 | async-start | bytes 327680
Sparse Core Ops, SparseCore 0:
  80.6 198.5 all-reduce.1
Sparse Core Ops, SparseCore 1:
  84.6 28.7 reduce-scatter.3
where the time goes:
time: 293 us; the launch traced here: 292 us
  waiting for transfers between devices  194 us (66%)
  local copies, waits for them, and re-layouts  37.8 us (13%)
  starting transfers between devices  16.6 us (6%)
  between operations  16 us (5%)
  blocking collectives  10.5 us (4%)
  other arithmetic  8.96 us (3%)
  matrix products  8.14 us (3%)
    psum x1, waiting for transfers between devices, shards(): weight_total = lax.psum(weight_term, 'dom') * grad_scale  193 us
    unnamed x37, local copies, waits for them, and re-layouts  16.8 us
    shift_right_arithmetic x4, local copies, waits for them, and re-layouts, shards(): jnp.right_shift(compressed_link_bitmap[..., None], bit_place) & 1  13.7 us
    all_gather x1, blocking collectives, shards(): gathered = lax.all_gather(vertex_embeddings, 'mp', axis=1, tiled=True)  10.5 us
    ppermute x1, starting transfers between devices, extended_2(): lax.ppermute(tail, axis, [(i, (i + 1) % count) for i in range(ends)])  6.37 us
  transfers between devices with their start and end apart: 6, of which 2 were waited for; matrix products, arithmetic and copies ran while one was open for 9% of the time, Pallas kernels for 0%

commit v1 on v0

--- a/solution.py
+++ b/solution.py
@@ -39,6 +39,34 @@
     return scale_rows * (
         upstream - unit_vec * jnp.mean(upstream * unit_vec, axis=-1, keepdims=True)
     )
+
+
+def spread(value, axis, groups, count):
+    copies = jnp.broadcast_to(value[None], (count,) + value.shape)
+    return lax.all_to_all(copies, axis, 0, 0, tiled=True, axis_index_groups=groups)
+
+
+def sum_over_dom(term, part_count):
+    rows, columns = term.shape
+    half, peers = rows // 2, part_count // 2
+    core = lax.axis_index("dom") % 2
+    pairs = [(i, i ^ 1) for i in range(part_count)]
+    groups = [[2 * i + c for i in range(peers)] for c in range(2)]
+    away = lax.dynamic_slice_in_dim(term, (1 - core) * half, half, axis=0).astype(jnp.bfloat16)
+    keep = lax.dynamic_slice_in_dim(term, core * half, half, axis=0)
+    keep = keep + lax.ppermute(away, "dom", pairs).astype(jnp.float32)
+    tall = jnp.concatenate([keep[:, i : i + 128] for i in range(0, columns, 128)], axis=0)
+    pieces = tall.astype(jnp.bfloat16).reshape(peers, -1, 128)
+    got = lax.all_to_all(pieces, "dom", 0, 0, tiled=True, axis_index_groups=groups)
+    mine = jnp.sum(got.astype(jnp.float32), axis=0).astype(jnp.bfloat16)
+    tall = spread(mine, "dom", groups, peers).reshape(-1, 128)
+    keep = jnp.concatenate(
+        [tall[i * half : (i + 1) * half] for i in range(columns // 128)], axis=1
+    )
+    other = lax.ppermute(keep, "dom", pairs)
+    low = jnp.where(core == 0, keep, other)
+    high = jnp.where(core == 0, other, keep)
+    return jnp.concatenate([low, high], axis=0).astype(jnp.float32)
 
 
 def shards(
@@ -59,7 +87,8 @@
     channel_extent = feat_width // resident_channels
     part_count = lax.axis_size("dom")
     my_part = lax.axis_index("dom")
-    gathered = lax.all_gather(vertex_embeddings, "mp", axis=1, tiled=True)
+    gathered = spread(vertex_embeddings, "mp", None, lax.axis_size("mp"))
+    gathered = jnp.concatenate([gathered[i] for i in range(gathered.shape[0])], axis=1)
     w_joint = jnp.concatenate(
         [asking_projector_matrix, lookup_projector_matrix, content_projector_matrix], axis=1
     )
@@ -166,7 +195,7 @@
     )
     grad_scale = (part_count * row_count) ** (-0.5)
     weight_term = jnp.einsum("rd,rc->dc", gathered, grads_joint, preferred_element_type=jnp.float32)
-    weight_total = lax.psum(weight_term, "dom") * grad_scale
+    weight_total = sum_over_dom(weight_term, part_count) * grad_scale
     grad_query = weight_total[:, :feat_width]
     grad_key = weight_total[:, feat_width : 2 * feat_width]
     grad_value_out = weight_total[:, 2 * feat_width :]

time: 293 us -> 158 us (0.54)
  waiting for transfers between devices: 194 us -> 22.9 us
  blocking collectives: 10.5 us -> 34.8 us
  starting transfers between devices: 16.6 us -> 32.1 us
    psum x1 -> x0, waiting for transfers between devices: 193 us -> none  [shards(): weight_total = lax.psum(weight_term, 'dom') * grad_scale]
    all_to_all x0 -> x1, blocking collectives: none -> 34.8 us  [sum_over_dom(): lax.all_to_all(pieces, 'dom', 0, 0, tiled=True, axis_index_groups=groups)]
    all_gather x1 -> x0, blocking collectives: 10.5 us -> none  [shards(): gathered = lax.all_gather(vertex_embeddings, 'mp', axis=1, tiled=True)]
    all_to_all x0 -> x2, waiting for transfers between devices: none -> 10.4 us  [spread(): lax.all_to_all(copies, axis, 0, 0, tiled=True, axis_index_groups=groups)]
    all_to_all x0 -> x2, starting transfers between devices: none -> 10.3 us  [spread(): lax.all_to_all(copies, axis, 0, 0, tiled=True, axis_index_groups=groups)]
    unnamed x3 -> x2, waiting for transfers between devices: 0.03 us -> 9.71 us
    ppermute x0 -> x2, starting transfers between devices: none -> 7.12 us  [the longest x1 5.2 us: sum_over_dom(): other = lax.ppermute(keep, 'dom', pairs)]
    unnamed x37 -> x40, local copies, waits for them, and re-layouts: 16.8 us -> 11.5 us
  transfers between devices with their start and end apart: 6 -> 9, of which waited for: 2 -> 5; matrix products, arithmetic and copies ran while one was open for 9% -> 16% of each run, Pallas kernels for 0% -> 0%
where the time goes in v1:
time: 158 us; the launch traced here: 156 us
  local copies, waits for them, and re-layouts  35.2 us (22%)
  blocking collectives  34.8 us (22%)
  starting transfers between devices  32.1 us (20%)
  waiting for transfers between devices  22.9 us (14%)
  between operations  14.8 us (9%)
  matrix products  8.4 us (5%)
  other arithmetic  7.72 us (5%)
    all_to_all x1, blocking collectives, sum_over_dom(): lax.all_to_all(pieces, 'dom', 0, 0, tiled=True, axis_index_groups=groups)  34.8 us
    shift_right_arithmetic x4, local copies, waits for them, and re-layouts, shards(): jnp.right_shift(compressed_link_bitmap[..., None], bit_place) & 1  13.7 us
    unnamed x40, local copies, waits for them, and re-layouts  11.5 us
    all_to_all x2, waiting for transfers between devices, spread(): lax.all_to_all(copies, axis, 0, 0, tiled=True, axis_index_groups=groups)  10.4 us
    all_to_all x2, starting transfers between devices, spread(): lax.all_to_all(copies, axis, 0, 0, tiled=True, axis_index_groups=groups)  10.3 us
    unnamed x2, waiting for transfers between devices  9.71 us
    ppermute x2, starting transfers between devices, from_behind(): lax.ppermute(value, axis, [(source, source + steps) for source in range(l...  5.78 us
    ppermute x1, starting transfers between devices, sum_over_dom(): other = lax.ppermute(keep, 'dom', pairs)  5.2 us
  transfers between devices with their start and end apart: 9, of which 5 were waited for; matrix products, arithmetic and copies ran while one was open for 16% of the time, Pallas kernels for 0%

profile of v1, /device:TPU:1, one launch (start us, length us, event | category | flops | bytes accessed | tf_op | source)
XLA Modules:
  0.0 156.1 jit_solution(3679031822251290715)
XLA Ops:
  7.2 1.6 %broadcast_in_dim.29 = bf16[4,256,128]{2,1,0:T(8,128)(2,1)} broadcast(bf16[256,128]{1,0:T(8,128)(2,1)} %param.8), dimensions={1,2} | broadcast | bytes 327680 | tf_op jit(solution)/shard_map/broadcast_in_dim | solution.py:45
  8.7 4.8 %all-to-all-start = ((bf16[4,256,128]{2,1,0:T(8,128)(2,1)}), bf16[4,256,128]{2,1,0:T(8,128)(2,1)S(1)}, u32[]{:S(2)}, u32[]{:S(2)}) async-start(bf16[4,256,128]{2,1,0:T(8,128)(2,1)} %broadcast_in_dim.29), calls=%async_computation | async-start | bytes 524288 | tf_op jit(solution)/shard_map/all_to_all | solution.py:46
  13.6 0.9 constant_dynamic-update-slice_fusion.2
  15.4 0.9 copy.88
  16.3 7.4 %shift_right_arithmetic.24 = s32[2,9,1024,16]{3,2,1,0:T(8,128)} broadcast(s32[2,9,1024]{2,1,0:T(8,128)S(1)} %copy.88), dimensions={0,1,2} | broadcast | bytes 1253376 | tf_op jit(solution)/shard_map/shift_right_arithmetic | solution.py:127
  23.7 6.3 %shift_right_arithmetic.25 = s32[2,9,128,128]{3,2,1,0:T(8,128)S(1)} reshape(s32[2,9,1024,16]{3,2,1,0:T(8,128)} %shift_right_arithmetic.24) | data formatting | bytes 2359296 | tf_op jit(solution)/shard_map/shift_right_arithmetic | solution.py:127
  32.6 4.0 %collective-permute-start = (bf16[256,256]{1,0:T(8,128)(2,1)S(1)}, bf16[256,256]{1,0:T(8,128)(2,1)S(1)}, u32[]{:S(2)}, u32[]{:S(2)}) collective-permute-start(bf16[256,256]{1,0:T(8,128)(2,1)S(1)} %pad_maximum_fusion.6), channel_id=1, source_target_pairs={{0,4},{4,8},{8,12},{12,16},{16,20},{20,24},{24,28},{28,32},{32,36}... | collective-permute-start | bytes 393224 | tf_op jit(solution)/shard_map/ppermute | solution.py:17
  36.6 4.8 %collective-permute-start.1 = (bf16[256,256]{1,0:T(8,128)(2,1)S(1)}, bf16[256,256]{1,0:T(8,128)(2,1)S(1)}, u32[]{:S(2)}, u32[]{:S(2)}) collective-permute-start(bf16[256,256]{1,0:T(8,128)(2,1)S(1)} %pad_maximum_fusion.6), channel_id=1, source_target_pairs={{4,0},{8,4},{12,8},{16,12},{20,16},{24,20},{28,24},{32,28},{36,32}... | collective-permute-start | bytes 393224 | tf_op jit(solution)/shard_map/ppermute | solution.py:19
  44.6 0.9 fusion.4
  45.4 0.9 convolution_bitcast_fusion
  46.3 0.9 fusion
  47.3 0.8 fusion.2
  49.3 2.0 %copy.112 = f32[2,9,128,256]{3,2,1,0:T(8,128)} copy(f32[2,9,128,256]{2,3,1,0:T(8,128)S(1)} %pad_maximum_fusion) | data formatting | bytes 4718592 | tf_op jit(solution)/shard_map/concatenate | solution.py:161
  51.3 2.0 %pad.26 = f32[24,128,256]{2,1,0:T(8,128)S(1)} pad(f32[18,128,256]{2,1,0:T(8,128)} %bitcast.103, f32[]{:T(128)} %constant.75.clone.1), padding=0_6x0_0x0_0 | pad | bytes 5505028
  53.3 3.5 %copy.138 = f32[3,8,128,256]{3,1,2,0:T(8,128)} copy(f32[3,8,128,256]{3,2,1,0:T(8,128)S(1)} %bitcast.102) | data formatting | bytes 6291456
  56.8 4.7 %scatter_custom_fusion = f32[6,32768]{1,0:T(8,128)S(1)} fusion(s32[18]{0:T(128)S(1)} %fusion.29, f32[18,32768]{1,0:T(8,128)} %bitcast.108, f32[]{:T(128)} %constant.75.clone.1), kind=kCustom, calls=%fused_computation.26 | custom fusion | flops 589824 | bytes 786944 | tf_op jit(solution)/shard_map/scatter-add | solution.py:172
  61.7 1.9 %collective-permute-start.2 = (bf16[2,32768]{1,0:T(2,128)(2,1)S(1)}, bf16[2,32768]{1,0:T(2,128)(2,1)S(1)}, u32[]{:S(2)}, u32[]{:S(2)}) collective-permute-start(bf16[2,32768]{1,0:T(2,128)(2,1)S(1)} %get-tuple-element.27), channel_id=1, source_target_pairs={{4,0},{8,4},{12,8},{16,12},{20,16},{24,20},{28,24},{32,28},{36,32}... | collective-permute-start | bytes 393224 | tf_op jit(solution)/shard_map/ppermute | solution.py:29
  63.7 3.9 %collective-permute-start.3 = (bf16[2,32768]{1,0:T(2,128)(2,1)S(1)}, bf16[2,32768]{1,0:T(2,128)(2,1)S(1)}, u32[]{:S(2)}, u32[]{:S(2)}) collective-permute-start(bf16[2,32768]{1,0:T(2,128)(2,1)S(1)} %get-tuple-element.28), channel_id=1, source_target_pairs={{0,4},{4,8},{8,12},{12,16},{16,20},{20,24},{24,28},{28,32},{32,36}... | collective-permute-start | bytes 393224 | tf_op jit(solution)/shard_map/ppermute | solution.py:29
  68.0 1.2 collective-permute-done.3
  70.1 1.2 fusion.21
  71.4 1.9 %collective-permute-start.4 = (bf16[256,384]{1,0:T(8,128)(2,1)S(1)}, bf16[256,384]{1,0:T(8,128)(2,1)S(1)}, u32[]{:S(2)}, u32[]{:S(2)}) collective-permute-start(bf16[256,384]{1,0:T(8,128)(2,1)S(1)} %dynamic-slice_convert_fusion), channel_id=1, source_target_pairs={{0,4},{4,0},{8,12},{12,8},{16,20},{20,16},{24,28},{28,24},{32,36},... | collective-permute-start | bytes 589832 | tf_op jit(solution)/shard_map/ppermute | solution.py:57
  73.3 1.4 collective-permute-done.4
  74.9 34.8 %all_to_all.15 = bf16[64,12,128]{2,1,0:T(8,128)(2,1)S(1)} all-to-all(bf16[64,12,128]{2,1,0:T(8,128)(2,1)S(1)} %convert_element_type.59), channel_id=1, replica_groups={{0,8,16,24,32,40,48,56,64,72,80,88,96,104,112,120,128,136,144,152,160,1..., dimensions={0} | all-to-all | bytes 393216 | tf_op jit(solution)/shard_map/all_to_all | solution.py:60
  110.5 5.5 %all-to-all-start.2 = ((bf16[64,12,128]{2,1,0:T(8,128)(2,1)}), bf16[64,12,128]{2,1,0:T(8,128)(2,1)S(1)}, u32[]{:S(2)}, u32[]{:S(2)}) async-start(bf16[64,12,128]{2,1,0:T(8,128)(2,1)} %broadcast_in_dim.34), calls=%async_computation.2 | async-start | bytes 524288 | tf_op jit(solution)/shard_map/all_to_all | solution.py:46
  116.1 1.3 convolution_convert_fusion
  117.4 0.8 copy.134
  118.3 10.4 %all-to-all-done.2 = bf16[64,12,128]{2,1,0:T(8,128)(2,1)S(1)} async-done(((bf16[64,12,128]{2,1,0:T(8,128)(2,1)}), bf16[64,12,128]{2,1,0:T(8,128)(2,1)S(1)}, u32[]{:S(2)}, u32[]{:S(2)}) %all-to-all-start.2) | async-done | bytes 196640 | tf_op jit(solution)/shard_map/all_to_all | solution.py:46
  128.8 5.2 %collective-permute-start.5 = (bf16[256,384]{1,0:T(8,128)(2,1)S(1)}, bf16[256,384]{1,0:T(8,128)(2,1)S(1)}, u32[]{:S(2)}, u32[]{:S(2)}) collective-permute-start(bf16[256,384]{1,0:T(8,128)(2,1)S(1)} %pad_maximum_fusion.5), channel_id=1, source_target_pairs={{0,4},{4,0},{8,12},{12,8},{16,20},{20,16},{24,28},{28,24},{32,36},... | collective-permute-start | bytes 589832 | tf_op jit(solution)/shard_map/ppermute | solution.py:66
  134.0 2.0 %fusion.9 = bf16[2,128,2,64]{1,3,2,0:T(8,128)(2,1)S(1)} fusion(bf16[2,9,128,2,64]{2,4,3,1,0:T(8,128)(2,1)} %bitcast.113, f32[2,2,9,128,128]{4,3,2,1,0:T(8,128)S(1)} %copy-done.1, f32[2,2,128]{2,1,0:T(2,128)S(1)} %get-tuple-element.48, f32[2]{0:T(128)S(1)} %broadcast_multiply_fusion.1, pred[2,9,128,128]{2,3,1,0:T(8,128)(4,1)S(1)} %copy.89), kind=kOutput, calls=%fused_computation.22 | convolution fusion | flops 77889536 | bytes 3311624 | tf_op jit(solution)/shard_map/bhtqk,btkhd->bqhd/dot_general | solution.py:138
  136.9 9.7 %reduce-scatter.4.cloned.1.call-done = bf16[128,256]{1,0:T(8,128)(2,1)} async-done(((bf16[512,256]{1,0:T(8,128)(2,1)}), bf16[128,256]{1,0:T(8,128)(2,1)}) %reduce-scatter.4.cloned.1.call-update) | async-done | bytes 65552
  146.6 1.6 %copy.135 = bf16[256,128]{1,0:T(8,128)(2,1)} copy(bf16[256,128]{0,1:T(8,128)(2,1)} %bitcast.120) | data formatting | bytes 131072
  148.3 0.9 fusion.38
  (111 shorter events, 11.2 us)
Async XLA Ops:
  8.7 22.4 %all-to-all-start = ((bf16[4,256,128]{2,1,0:T(8,128)(2,1)}), bf16[4,256,128]{2,1,0:T(8,128)(2,1)S(1)}, u32[]{:S(2)}, u32[]{:S(2)}) async-start(bf16[4,256,128]{2,1,0:T(8,128)(2,1)} %broadcast_in_dim.29), calls=%async_computation | async-start | bytes 524288 | tf_op jit(solution)/shard_map/all_to_all | solution.py:46
  23.7 7.1 %copy-start.6 = (bf16[256,128]{1,0:T(8,128)(2,1)S(1)}, bf16[256,128]{1,0:T(8,128)(2,1)}, u32[]{:S(2)}) copy-start(bf16[256,128]{1,0:T(8,128)(2,1)} %param.9) | copy-start | bytes 196612
  30.0 1.0 copy-start.4
  30.0 1.1 copy-start.5
  30.0 1.1 copy-start.14
  31.1 10.7 %copy-start.13 = (bf16[512,384]{1,0:T(8,128)(2,1)}, bf16[512,384]{1,0:T(8,128)(2,1)S(1)}, u32[]{:S(2)}) copy-start(bf16[512,384]{1,0:T(8,128)(2,1)S(1)} %constant_dynamic-update-slice_fusion) | copy-start | bytes 1179652
  31.2 0.7 copy-start.7
  31.2 0.7 copy-start.9
  31.2 1.0 copy-start.11
  31.2 1.0 copy-start.12
  32.6 10.1 %collective-permute-start = (bf16[256,256]{1,0:T(8,128)(2,1)S(1)}, bf16[256,256]{1,0:T(8,128)(2,1)S(1)}, u32[]{:S(2)}, u32[]{:S(2)}) collective-permute-start(bf16[256,256]{1,0:T(8,128)(2,1)S(1)} %pad_maximum_fusion.6), channel_id=1, source_target_pairs={{0,4},{4,8},{8,12},{12,16},{16,20},{20,24},{24,28},{28,32},{32,36}... | collective-permute-start | bytes 393224 | tf_op jit(solution)/shard_map/ppermute | solution.py:17
  36.6 6.3 %collective-permute-start.1 = (bf16[256,256]{1,0:T(8,128)(2,1)S(1)}, bf16[256,256]{1,0:T(8,128)(2,1)S(1)}, u32[]{:S(2)}, u32[]{:S(2)}) collective-permute-start(bf16[256,256]{1,0:T(8,128)(2,1)S(1)} %pad_maximum_fusion.6), channel_id=1, source_target_pairs={{4,0},{8,4},{12,8},{16,12},{20,16},{24,20},{28,24},{32,28},{36,32}... | collective-permute-start | bytes 393224 | tf_op jit(solution)/shard_map/ppermute | solution.py:19
  44.6 1.7 %copy-start.2 = (bf16[2,9,128,128]{2,3,1,0:T(8,128)(2,1)}, bf16[2,9,128,128]{2,3,1,0:T(8,128)(2,1)S(1)}, u32[]{:S(2)}) copy-start(bf16[2,9,128,128]{2,3,1,0:T(8,128)(2,1)S(1)} %get-tuple-element.23) | copy-start | bytes 1769476
  45.4 1.8 %copy-start = (f32[2,2,9,128,128]{4,3,2,1,0:T(8,128)}, f32[2,2,9,128,128]{4,3,2,1,0:T(8,128)S(1)}, u32[]{:S(2)}) copy-start(f32[2,2,9,128,128]{4,3,2,1,0:T(8,128)S(1)} %get-tuple-element.49) | copy-start | bytes 7077892
  61.5 8.5 %copy-start.3 = (f32[256,128]{1,0:T(8,128)S(1)}, f32[256,128]{1,0:T(8,128)}, u32[]{:S(2)}) copy-start(f32[256,128]{1,0:T(8,128)} %copy.106) | copy-start | bytes 393220
  61.7 6.3 %collective-permute-start.2 = (bf16[2,32768]{1,0:T(2,128)(2,1)S(1)}, bf16[2,32768]{1,0:T(2,128)(2,1)S(1)}, u32[]{:S(2)}, u32[]{:S(2)}) collective-permute-start(bf16[2,32768]{1,0:T(2,128)(2,1)S(1)} %get-tuple-element.27), channel_id=1, source_target_pairs={{4,0},{8,4},{12,8},{16,12},{20,16},{24,20},{28,24},{32,28},{36,32}... | collective-permute-start | bytes 393224 | tf_op jit(solution)/shard_map/ppermute | solution.py:29
  63.7 5.6 %collective-permute-start.3 = (bf16[2,32768]{1,0:T(2,128)(2,1)S(1)}, bf16[2,32768]{1,0:T(2,128)(2,1)S(1)}, u32[]{:S(2)}, u32[]{:S(2)}) collective-permute-start(bf16[2,32768]{1,0:T(2,128)(2,1)S(1)} %get-tuple-element.28), channel_id=1, source_target_pairs={{0,4},{4,8},{8,12},{12,16},{16,20},{20,24},{24,28},{28,32},{32,36}... | collective-permute-start | bytes 393224 | tf_op jit(solution)/shard_map/ppermute | solution.py:29
  67.7 2.4 %copy-start.8 = (bf16[256,128]{1,0:T(8,128)(2,1)S(1)}, bf16[256,128]{1,0:T(8,128)(2,1)}, u32[]{:S(2)}) copy-start(bf16[256,128]{1,0:T(8,128)(2,1)} %copy-done.7) | copy-start | bytes 196612
  67.7 2.4 %copy-start.10 = (bf16[256,128]{1,0:T(8,128)(2,1)S(1)}, bf16[256,128]{1,0:T(8,128)(2,1)}, u32[]{:S(2)}) copy-start(bf16[256,128]{1,0:T(8,128)(2,1)} %copy-done.9) | copy-start | bytes 196612
  71.4 3.3 %collective-permute-start.4 = (bf16[256,384]{1,0:T(8,128)(2,1)S(1)}, bf16[256,384]{1,0:T(8,128)(2,1)S(1)}, u32[]{:S(2)}, u32[]{:S(2)}) collective-permute-start(bf16[256,384]{1,0:T(8,128)(2,1)S(1)} %dynamic-slice_convert_fusion), channel_id=1, source_target_pairs={{0,4},{4,0},{8,12},{12,8},{16,20},{20,16},{24,28},{28,24},{32,36},... | collective-permute-start | bytes 589832 | tf_op jit(solution)/shard_map/ppermute | solution.py:57
  74.9 59.1 %copy-start.1 = (f32[2,2,9,128,128]{4,3,2,1,0:T(8,128)S(1)}, f32[2,2,9,128,128]{4,3,2,1,0:T(8,128)}, u32[]{:S(2)}) copy-start(f32[2,2,9,128,128]{4,3,2,1,0:T(8,128)} %copy-done) | copy-start | bytes 7077892
  110.5 18.1 %all-to-all-start.2 = ((bf16[64,12,128]{2,1,0:T(8,128)(2,1)}), bf16[64,12,128]{2,1,0:T(8,128)(2,1)S(1)}, u32[]{:S(2)}, u32[]{:S(2)}) async-start(bf16[64,12,128]{2,1,0:T(8,128)(2,1)} %broadcast_in_dim.34), calls=%async_computation.2 | async-start | bytes 524288 | tf_op jit(solution)/shard_map/all_to_all | solution.py:46
  116.0 30.5 %reduce-scatter.4.cloned.1.call-start = ((), (), s32[]{:S(2)}) async-start(), calls=%async_computation.4 | async-start | bytes 327680
  128.8 19.3 %collective-permute-start.5 = (bf16[256,384]{1,0:T(8,128)(2,1)S(1)}, bf16[256,384]{1,0:T(8,128)(2,1)S(1)}, u32[]{:S(2)}, u32[]{:S(2)}) collective-permute-start(bf16[256,384]{1,0:T(8,128)(2,1)S(1)} %pad_maximum_fusion.5), channel_id=1, source_target_pairs={{0,4},{4,0},{8,12},{12,8},{16,20},{20,16},{24,28},{28,24},{32,36},... | collective-permute-start | bytes 589832 | tf_op jit(solution)/shard_map/ppermute | solution.py:66
Sparse Core Ops, SparseCore 0:
  120.3 26.2 reduce-scatter.3

commit v2 on v0

v2 whole, which is shorter than its diff:
```python
import jax
import jax.numpy as jnp
from jax import lax
from jax.experimental import pallas as pl
from jax.experimental.pallas import tpu as pltpu
from jax.sharding import PartitionSpec as P

EPS = 1e-06
F32 = jnp.float32
BF16 = jnp.bfloat16
LANES = 128
VMEM = pl.BlockSpec(memory_space=pltpu.VMEM)
SMEM = pl.BlockSpec(memory_space=pltpu.SMEM)
NN = (((1,), (0,)), ((), ()))
NT = (((1,), (1,)), ((), ()))
TN = (((0,), (0,)), ((), ()))


def mul(a, b, dims=NN):
    return lax.dot_general(a, b, dims, preferred_element_type=F32)


def call(kernel, out, in_specs, scratch=(), flops=0, moved=0):
    return pl.pallas_call(
        kernel,
        out_shape=out,
        in_specs=in_specs,
        out_specs=jax.tree.map(lambda _: VMEM, out),
        scratch_shapes=list(scratch),
        compiler_params=pltpu.CompilerParams(vmem_limit_bytes=40 * 1024 * 1024),
        cost_estimate=pl.CostEstimate(flops=flops, bytes_accessed=moved, transcendentals=0),
    )


def shape(dims, kind):
    return jax.ShapeDtypeStruct(dims, kind)


def count_kernel(place_ref, words_ref, count_ref, total):
    blocks, tiles, words = words_ref.shape
    block = LANES
    per_row = words // block
    rows = block // per_row * 1
    total[...] = jnp.zeros_like(total)
    lane = lax.broadcasted_iota(jnp.int32, (block, block), 1)
    row = lax.broadcasted_iota(jnp.int32, (block, block), 0)
    same = (row % per_row) == (lane // 16)
    low_pick = jnp.where(same & (lane % 16 < 8), 1.0, 0.0)
    high_pick = jnp.where(same & (lane % 16 >= 8), 1.0, 0.0)
    pick = jnp.concatenate([low_pick, high_pick], axis=0).astype(BF16)
    mine = (row[:rows] == lane[:rows] // per_row).astype(F32)
    shift = lane % 8
    for b in range(blocks):
        for t in range(tiles):
            line = words_ref[b, t : t + 1, :]
            low = (line & 255).astype(F32)
            high = lax.shift_right_logical(line, 8).astype(F32)
            spread_rows = []
            for r in range(per_row):
                at = slice(r * block, (r + 1) * block)
                spread_rows.append(
                    jnp.concatenate([low[:, at] * mine, high[:, at] * mine], axis=1)
                )
            wide = jnp.concatenate(spread_rows, axis=0).astype(BF16)
            byte = mul(wide, pick).astype(jnp.int32)
            bits = (lax.shift_right_logical(byte, shift) & 1).astype(F32)
            place = place_ref[b, t]
            total[b, place] = total[b, place] + bits
    for b in range(blocks):
        for s in range(4):
            count_ref[b * block : (b + 1) * block, s * block : (s + 1) * block] = total[
                b, s
            ].astype(BF16)


def head_mean(value, mixer):
    high = value.astype(BF16)
    low = (value - high.astype(F32)).astype(BF16)
    return mul(high, mixer) + mul(low, mixer)


def attend_kernel(
    info_ref,
    scale_ref,
    x_ref,
    xa_ref,
    xb_ref,
    wq_ref,
    wk_ref,
    wv_ref,
    up_ref,
    count_ref,
    att_ref,
    gq_ref,
    gown_ref,
    back_a_ref,
    back_b_ref,
    keep_ref,
    away_ref,
    x_all,
    dw,
):
    core, before, after = info_ref[0], info_ref[1], info_ref[2]
    n = LANES
    for i in range(4):
        x_all[0 : 2 * n, i * n : (i + 1) * n] = x_ref[i]

    @pl.when(core == 0)
    def _():
        for i in range(4):
            x_all[2 * n : 3 * n, i * n : (i + 1) * n] = xb_ref[i, pl.ds(before * n, n), :]
            x_all[3 * n : 4 * n, i * n : (i + 1) * n] = xa_ref[i, pl.ds(after * n, n), :]

    @pl.when(core != 0)
    def _():
        for i in range(4):
            x_all[2 * n : 3 * n, i * n : (i + 1) * n] = xa_ref[i, pl.ds(before * n, n), :]
            x_all[3 * n : 4 * n, i * n : (i + 1) * n] = xb_ref[i, pl.ds(after * n, n), :]

    x = x_all[...]
    q = mul(x[: 2 * n], wq_ref[...])
    k = mul(x, wk_ref[...])
    v = mul(x, wv_ref[...])
    mixer = jnp.where(
        lax.broadcasted_iota(jnp.int32, (n, n), 0) // 64
        == lax.broadcasted_iota(jnp.int32, (n, n), 1) // 64,
        1.0 / 64,
        0.0,
    ).astype(BF16)
    q_scale = lax.rsqrt(head_mean(q * q, mixer) + EPS)
    k_scale = lax.rsqrt(head_mean(k * k, mixer) + EPS)
    q_unit, k_unit = q * q_scale, k * k_scale
    q_round, k_round, v_round = q_unit.astype(BF16), k_unit.astype(BF16), v.astype(BF16)
    up = up_ref[...]
    first = lax.broadcasted_iota(jnp.int32, (1, n), 1) < 64
    heads = [first.astype(F32).astype(BF16), (1 - first.astype(F32)).astype(BF16)]
    factors = [scale_ref[0] / 64, scale_ref[1] / 64]
    lane_factor = jnp.where(first, factors[0], factors[1])
    att, gq = [], []
    gk = jnp.zeros((4 * n, n), F32)
    gv = jnp.zeros((4 * n, n), F32)
    for b in range(2):
        at = slice(b * n, (b + 1) * n)
        count = count_ref[at, :].astype(F32)
        att_b = jnp.zeros((n, n), F32)
        gq_b = jnp.zeros((n, n), F32)
        for h in range(2):
            q_h = q_round[at] * heads[h]
            up_h = up[at] * heads[h]
            scores = mul(q_h, k_round, NT) * factors[h]
            w = count * jnp.exp(scores)
            w = w * (1.0 / jnp.sum(w, axis=1, keepdims=True))
            gw = mul(up_h, v_round, NT)
            delta = jnp.sum(w * gw, axis=1, keepdims=True)
            gs = (w * (gw - delta)).astype(BF16)
            w_round = w.astype(BF16)
            att_b += mul(w_round, v_round * heads[h])
            gq_b += mul(gs, k_round * heads[h])
            gk += mul(gs, q_h, TN)
            gv += mul(w_round, up_h, TN)
        att.append(att_b)
        gq.append(gq_b)
    att_ref[...] = jnp.concatenate(att, axis=0).astype(BF16)
    gqn = jnp.concatenate(gq, axis=0) * lane_factor
    gkn = gk * lane_factor
    gq = (q_scale * (gqn - q_unit * head_mean(gqn * q_unit, mixer))).astype(BF16)
    gk = k_scale * (gkn - k_unit * head_mean(gkn * k_unit, mixer))
    gq_ref[...] = gq
    gown_ref[:, :n] = gk[: 2 * n]
    gown_ref[:, n:] = gv[: 2 * n]
    gk_round, gv_round = gk.astype(BF16), gv.astype(BF16)
    dw[:, :n] = mul(x[: 2 * n], gq, TN)
    dw[:, n : 2 * n] = mul(x, gk_round, TN)
    dw[:, 2 * n :] = mul(x, gv_round, TN)
    sides = [
        (jnp.concatenate([gk_round[s], gv_round[s]], axis=1), which)
        for s, which in ((slice(2 * n, 3 * n), before), (slice(3 * n, 4 * n), after))
    ]

    def put(ref, side):
        ref[:n] = side[0]
        ref[n:] = jnp.full((16, 2 * n), side[1], jnp.int32).astype(F32).astype(BF16)

    @pl.when(core == 0)
    def _():
        put(back_a_ref, sides[1])
        put(back_b_ref, sides[0])

    @pl.when(core != 0)
    def _():
        put(back_a_ref, sides[0])
        put(back_b_ref, sides[1])

    for j in range(3):
        rows, columns = slice(2 * n * j, 2 * n * (j + 1)), slice(n * j, n * (j + 1))
        keep_ref[rows] = dw[pl.ds(core * 2 * n, 2 * n), columns]
        away_ref[rows] = dw[pl.ds((1 - core) * 2 * n, 2 * n), columns].astype(BF16)


def input_kernel(gq_ref, gown_ref, back_a_ref, back_b_ref, wq_ref, wk_ref, wv_ref, part_ref):
    n = LANES
    g = [gown_ref[:n], gown_ref[n:]]
    for ref in (back_a_ref, back_b_ref):
        body = ref[:n].astype(F32)
        which = ref[n : n + 16].astype(F32)[:1]
        g = [g[0] + body * (1 - which), g[1] + body * which]
    g = jnp.concatenate(g, axis=0).astype(BF16)
    part = mul(gq_ref[...], wq_ref[...], NT)
    part += mul(g[:, :n], wk_ref[...], NT)
    part += mul(g[:, n:], wv_ref[...], NT)
    for i in range(4):
        part_ref[i] = part[:, i * n : (i + 1) * n].astype(BF16)


def final_kernel(grad_scale, core_ref, mine_ref, other_ref, gq_ref, gk_ref, gv_ref):
    n = 2 * LANES
    core = core_ref[0]
    for j, ref in enumerate((gq_ref, gk_ref, gv_ref)):
        rows = slice(n * j, n * (j + 1))
        ref[pl.ds(core * n, n), :] = mine_ref[rows].astype(F32) * grad_scale
        ref[pl.ds((1 - core) * n, n), :] = other_ref[rows].astype(F32) * grad_scale


def spread(value, axis, groups, count):
    copies = jnp.broadcast_to(value[None], (count,) + value.shape)
    return lax.all_to_all(copies, axis, 0, 0, tiled=True, axis_index_groups=groups)


def shards(x, up, wq, wk, wv, scales, table, bitmap):
    parts = lax.axis_size("dom")
    part = lax.axis_index("dom")
    core = part % 2
    pairs = [(i, i ^ 1) for i in range(parts)]
    edges = [(i, i + 1) for i in range(1, parts - 1, 2)]
    edges = edges + [(b, a) for a, b in edges]
    peers = parts // 2
    groups = [[2 * i + c for i in range(peers)] for c in range(2)]

    gathered = spread(x, "mp", None, lax.axis_size("mp"))

    side = table // 2 - part
    place = jnp.where(side == 0, table % 2, jnp.where(side < 0, 2, 3))
    place = jnp.concatenate([jnp.arange(2, dtype=jnp.int32)[:, None], place], axis=1)
    info = jnp.stack([core, table[0, 0] % 2, table[0, 1] % 2]).astype(jnp.int32)
    count = call(
        count_kernel,
        shape((256, 512), BF16),
        [SMEM, VMEM],
        [pltpu.VMEM((2, 4, LANES, LANES), F32)],
        flops=2_000_000_000,
        moved=400_000,
    )(place, bitmap)

    xa = lax.ppermute(gathered, "dom", pairs)
    xb = lax.ppermute(gathered, "dom", edges)
    att, gq, gown, back_a, back_b, keep, away = call(
        attend_kernel,
        (
            shape((256, 128), BF16),
            shape((256, 128), BF16),
            shape((256, 256), F32),
            shape((144, 256), BF16),
            shape((144, 256), BF16),
            shape((768, 128), F32),
            shape((768, 128), BF16),
        ),
        [SMEM, SMEM] + [VMEM] * 8,
        [pltpu.VMEM((512, 512), BF16), pltpu.VMEM((512, 384), F32)],
        flops=5_000_000_000,
        moved=4_000_000,
    )(info, scales, gathered, xa, xb, wq, wk, wv, up, count)

    swapped = lax.ppermute(away, "dom", pairs)
    back_a = lax.ppermute(back_a, "dom", pairs)
    back_b = lax.ppermute(back_b, "dom", edges)
    pieces = (keep + swapped.astype(F32)).astype(BF16).reshape(peers, -1, LANES)
    got = lax.all_to_all(pieces, "dom", 0, 0, tiled=True, axis_index_groups=groups)

    input_part = call(
        input_kernel, shape((4, 256, 128), BF16), [VMEM] * 7, flops=1_000_000_000, moved=1_500_000
    )(gq, gown, back_a, back_b, wq, wk, wv)
    input_parts = lax.all_to_all(input_part, "mp", 0, 0, tiled=True)
    input_grad = jnp.sum(input_parts.astype(F32), axis=0).astype(BF16)

    mine = jnp.sum(got.astype(F32), axis=0).astype(BF16)
    mine = spread(mine, "dom", groups, peers).reshape(-1, LANES)
    other = lax.ppermute(mine, "dom", pairs)
    grad_scale = float(parts * 256) ** -0.5

    def finish(*refs):
        final_kernel(grad_scale, *refs)

    grads = call(
        finish, (shape((512, 128), F32),) * 3, [SMEM, VMEM, VMEM], moved=1_500_000
    )(info[:1], mine, other)
    return (att, input_grad) + tuple(grads)


def solution(mesh):
    in_specs = (
        P("dom", "mp"),
        P("dom", "mp"),
        P(None, "mp"),
        P(None, "mp"),
        P(None, "mp"),
        P("mp"),
        P("dom", None),
        P("dom", None, None),
    )
    out_specs = (P("dom", "mp"), P("dom", "mp"), P(None, "mp"), P(None, "mp"), P(None, "mp"))
    return jax.shard_map(shards, mesh=mesh, in_specs=in_specs, out_specs=out_specs, check_vma=False)
```

time: 293 us -> 92.9 us (0.32)
  the two profiles are of different devices: /device:TPU:1 before, /device:TPU:8 now
where the time goes in v2:
time: 92.9 us; the launch traced here: 92.2 us
  blocking collectives  32.2 us (35%)
  starting transfers between devices  26.9 us (29%)
  waiting for transfers between devices  16.2 us (17%)
  Pallas kernels  7.46 us (8%)
  between operations  4.72 us (5%)
  local copies, waits for them, and re-layouts  3.73 us (4%)
  other arithmetic  0.96 us (1%)
    all_to_all x1, blocking collectives, shards(): lax.all_to_all(pieces, 'dom', 0, 0, tiled=True, axis_index_groups=groups)  32.2 us
    all_to_all x2, starting transfers between devices, spread(): lax.all_to_all(copies, axis, 0, 0, tiled=True, axis_index_groups=groups)  9.53 us
    all_to_all x2, waiting for transfers between devices, spread(): lax.all_to_all(copies, axis, 0, 0, tiled=True, axis_index_groups=groups)  6.06 us
    all_to_all x1, waiting for transfers between devices, shards(): input_parts = lax.all_to_all(input_part, 'mp', 0, 0, tiled=True)  4.7 us
    pallas_call x1, Pallas kernels, shards(): call(attend_kernel, (shape((256, 128), BF16), shape((256, 128), BF16), sh...  4.31 us
    ppermute x1, starting transfers between devices, shards(): xa = lax.ppermute(gathered, 'dom', pairs)  3.59 us
    all_to_all x1, starting transfers between devices, shards(): input_parts = lax.all_to_all(input_part, 'mp', 0, 0, tiled=True)  3.47 us
    ppermute x1, waiting for transfers between devices, shards(): back_b = lax.ppermute(back_b, 'dom', edges)  3.21 us
  transfers between devices with their start and end apart: 9, of which 6 were waited for; matrix products, arithmetic and copies ran while one was open for 2% of the time, Pallas kernels for 2%

profile of v2, /device:TPU:8, one launch (start us, length us, event | category | flops | bytes accessed | tf_op | source)
XLA Modules:
  0.0 92.2 jit_solution(6466121279916212562)
XLA Ops:
  0.6 1.6 %broadcast_in_dim.10 = bf16[4,256,128]{2,1,0:T(8,128)(2,1)} broadcast(bf16[256,128]{1,0:T(8,128)(2,1)} %param.8), dimensions={1,2} | broadcast | bytes 327680 | tf_op jit(solution)/shard_map/broadcast_in_dim | solution.py:225
  2.2 4.4 %all-to-all-start = ((bf16[4,256,128]{2,1,0:T(8,128)(2,1)}), bf16[4,256,128]{2,1,0:T(8,128)(2,1)S(1)}, u32[]{:S(2)}, u32[]{:S(2)}) async-start(bf16[4,256,128]{2,1,0:T(8,128)(2,1)} %broadcast_in_dim.10), calls=%async_computation | async-start | bytes 524288 | tf_op jit(solution)/shard_map/all_to_all | solution.py:226
  6.6 0.7 copy-done.6
  7.3 0.6 fusion
  11.9 0.1 pad_add_fusion.place_ref
  12.0 1.3 %all-to-all-done.x_ref = bf16[4,256,128]{2,1,0:T(8,128)(2,1)S(1)} async-done(((bf16[4,256,128]{2,1,0:T(8,128)(2,1)}), bf16[4,256,128]{2,1,0:T(8,128)(2,1)S(1)}, u32[]{:S(2)}, u32[]{:S(2)}) %all-to-all-start) | async-done | bytes 262176 | tf_op jit(solution)/shard_map/all_to_all | solution.py:226
  13.3 1.9 %collective-permute-start.1 = (bf16[4,256,128]{2,1,0:T(8,128)(2,1)S(1)}, bf16[4,256,128]{2,1,0:T(8,128)(2,1)S(1)}, u32[]{:S(2)}, u32[]{:S(2)}) collective-permute-start(bf16[4,256,128]{2,1,0:T(8,128)(2,1)S(1)} %all-to-all-done.x_ref), channel_id=1, source_target_pairs={{4,8},{12,16},{20,24},{28,32},{36,40},{44,48},{52,56},{60,64},{68,... | collective-permute-start | bytes 786440 | tf_op jit(solution)/shard_map/ppermute | solution.py:255
  15.2 3.6 %collective-permute-start = (bf16[4,256,128]{2,1,0:T(8,128)(2,1)S(1)}, bf16[4,256,128]{2,1,0:T(8,128)(2,1)S(1)}, u32[]{:S(2)}, u32[]{:S(2)}) collective-permute-start(bf16[4,256,128]{2,1,0:T(8,128)(2,1)S(1)} %all-to-all-done.x_ref), channel_id=1, source_target_pairs={{0,4},{4,0},{8,12},{12,8},{16,20},{20,16},{24,28},{28,24},{32,36},... | collective-permute-start | bytes 786440 | tf_op jit(solution)/shard_map/ppermute | solution.py:254
  18.8 0.1 pad_add_fusion.1.info_ref
  18.9 0.0 copy-start.4
  18.9 1.1 %shard_map.119.count_ref = bf16[256,512]{1,0:T(8,128)(2,1)S(1)} custom-call(s32[2,9]{1,0:T(2,128)S(1)} %pad_add_fusion.place_ref, s32[2,9,1024]{2,1,0:T(8,128)S(1)} %copy.14.words_ref), custom_call_target="tpu_custom_call" | custom-call | flops 2000000000 | bytes 400000 | tf_op jit(solution)/shard_map/pallas_call | solution.py:245
  20.1 0.9 collective-permute-done.1.xb_ref
  21.0 0.0 collective-permute-done.xa_ref
  21.0 4.3 %shard_map.120 = (bf16[256,128]{1,0:T(8,128)(2,1)}, bf16[256,128]{1,0:T(8,128)(2,1)S(1)}, f32[256,256]{1,0:T(8,128)S(1)}, bf16[144,256]{1,0:T(8,128)(2,1)S(1)}, ...) custom-call(s32[3]{0:T(128)S(1)} %pad_add_fusion.1.info_ref, f32[2]{0:T(128)S(1)} %copy-done.4, ...), custom_call_target="tpu_custom_call" | custom-call | flops 5000000000 | bytes 4000000 | tf_op jit(solution)/shard_map/pallas_call | solution.py:256
  25.4 2.0 %collective-permute-start.4 = (bf16[768,128]{1,0:T(8,128)(2,1)S(1)}, bf16[768,128]{1,0:T(8,128)(2,1)S(1)}, u32[]{:S(2)}, u32[]{:S(2)}) collective-permute-start(bf16[768,128]{1,0:T(8,128)(2,1)S(1)} %get-tuple-element.21), channel_id=1, source_target_pairs={{0,4},{4,0},{8,12},{12,8},{16,20},{20,16},{24,28},{28,24},{32,36},... | collective-permute-start | bytes 589832 | tf_op jit(solution)/shard_map/ppermute | solution.py:273
  27.4 1.3 %collective-permute-done.4 = bf16[768,128]{1,0:T(8,128)(2,1)S(1)} collective-permute-done((bf16[768,128]{1,0:T(8,128)(2,1)S(1)}, bf16[768,128]{1,0:T(8,128)(2,1)S(1)}, u32[]{:S(2)}, u32[]{:S(2)}) %collective-permute-start.4) | collective-permute-done | bytes 196640 | tf_op jit(solution)/shard_map/ppermute | solution.py:273
  28.8 32.2 %all_to_all.20 = bf16[64,12,128]{2,1,0:T(8,128)(2,1)S(1)} all-to-all(bf16[64,12,128]{2,1,0:T(8,128)(2,1)S(1)} %reshape.18), channel_id=1, replica_groups={{0,8,16,24,32,40,48,56,64,72,80,88,96,104,112,120,128,136,144,152,160,1..., dimensions={0} | all-to-all | bytes 393216 | tf_op jit(solution)/shard_map/all_to_all | solution.py:277
  61.0 0.1 reduce_sum.25
  61.1 0.7 broadcast_in_dim.12
  61.8 5.1 %all-to-all-start.3 = ((bf16[64,12,128]{2,1,0:T(8,128)(2,1)}), bf16[64,12,128]{2,1,0:T(8,128)(2,1)S(1)}, u32[]{:S(2)}, u32[]{:S(2)}) async-start(bf16[64,12,128]{2,1,0:T(8,128)(2,1)} %broadcast_in_dim.12), calls=%async_computation.3 | async-start | bytes 524288 | tf_op jit(solution)/shard_map/all_to_all | solution.py:226
  66.9 1.9 %collective-permute-start.2 = (bf16[144,256]{1,0:T(8,128)(2,1)S(1)}, bf16[144,256]{1,0:T(8,128)(2,1)S(1)}, u32[]{:S(2)}, u32[]{:S(2)}) collective-permute-start(bf16[144,256]{1,0:T(8,128)(2,1)S(1)} %get-tuple-element.18), channel_id=1, source_target_pairs={{0,4},{4,0},{8,12},{12,8},{16,20},{20,16},{24,28},{28,24},{32,36},... | collective-permute-start | bytes 221192 | tf_op jit(solution)/shard_map/ppermute | solution.py:274
  68.9 2.6 %collective-permute-start.3 = (bf16[144,256]{1,0:T(8,128)(2,1)S(1)}, bf16[144,256]{1,0:T(8,128)(2,1)S(1)}, u32[]{:S(2)}, u32[]{:S(2)}) collective-permute-start(bf16[144,256]{1,0:T(8,128)(2,1)S(1)} %get-tuple-element.19), channel_id=1, source_target_pairs={{4,8},{12,16},{20,24},{28,32},{36,40},{44,48},{52,56},{60,64},{68,... | collective-permute-start | bytes 221192 | tf_op jit(solution)/shard_map/ppermute | solution.py:275
  71.4 0.0 collective-permute-done.2.back_a_ref
  71.5 3.2 %collective-permute-done.3.back_b_ref = bf16[144,256]{1,0:T(8,128)(2,1)S(1)} collective-permute-done((bf16[144,256]{1,0:T(8,128)(2,1)S(1)}, bf16[144,256]{1,0:T(8,128)(2,1)S(1)}, u32[]{:S(2)}, u32[]{:S(2)}) %collective-permute-start.3) | collective-permute-done | bytes 73760 | tf_op jit(solution)/shard_map/ppermute | solution.py:275
  74.7 1.1 %shard_map.121 = bf16[4,256,128]{2,1,0:T(8,128)(2,1)} custom-call(bf16[256,128]{1,0:T(8,128)(2,1)S(1)} %get-tuple-element.16.gq_ref, f32[256,256]{1,0:T(8,128)S(1)} %get-tuple-element.17.gown_ref, bf16[144,256]{1,0:T(8,128)(2,1)S(1)} %collective-permute-done.2.back_a_ref, bf16[144,256]{1,0:T(8,128)(2,1)S(1)} %collective-permute-done.3.back_b_ref, ...), custom_call_target="tpu_custom_call" | custom-call | flops 1000000000 | bytes 1500000 | tf_op jit(solution)/shard_map/pallas_call | solution.py:279
  75.7 4.7 %all-to-all-done.3 = bf16[64,12,128]{2,1,0:T(8,128)(2,1)S(1)} async-done(((bf16[64,12,128]{2,1,0:T(8,128)(2,1)}), bf16[64,12,128]{2,1,0:T(8,128)(2,1)S(1)}, u32[]{:S(2)}, u32[]{:S(2)}) %all-to-all-start.3) | async-done | bytes 196640 | tf_op jit(solution)/shard_map/all_to_all | solution.py:226
  80.5 3.5 %all-to-all-start.1 = ((bf16[4,256,128]{2,1,0:T(8,128)(2,1)}), bf16[4,256,128]{2,1,0:T(8,128)(2,1)S(1)}, u32[]{:S(2)}, u32[]{:S(2)}) async-start(bf16[4,256,128]{2,1,0:T(8,128)(2,1)} %shard_map.121), calls=%async_computation.1 | async-start | bytes 524288 | tf_op jit(solution)/shard_map/all_to_all | solution.py:282
  84.0 1.9 %collective-permute-start.5 = (bf16[768,128]{1,0:T(8,128)(2,1)S(1)}, bf16[768,128]{1,0:T(8,128)(2,1)S(1)}, u32[]{:S(2)}, u32[]{:S(2)}) collective-permute-start(bf16[768,128]{1,0:T(8,128)(2,1)S(1)} %reshape.19.refs_1_), channel_id=1, source_target_pairs={{0,4},{4,0},{8,12},{12,8},{16,20},{20,16},{24,28},{28,24},{32,36},... | collective-permute-start | bytes 589832 | tf_op jit(solution)/shard_map/ppermute | solution.py:287
  85.9 4.7 %all-to-all-done.1 = bf16[4,256,128]{2,1,0:T(8,128)(2,1)S(1)} async-done(((bf16[4,256,128]{2,1,0:T(8,128)(2,1)}), bf16[4,256,128]{2,1,0:T(8,128)(2,1)S(1)}, u32[]{:S(2)}, u32[]{:S(2)}) %all-to-all-start.1) | async-done | bytes 262176 | tf_op jit(solution)/shard_map/all_to_all | solution.py:282
  90.6 0.7 reduce_sum.24
  91.3 0.0 collective-permute-done.5.refs_2_
  91.3 0.9 shard_map.122
  (18 shorter events, 0.2 us)
Async XLA Ops:
  2.2 9.6 %copy-start.5 = (s32[2,9,1024]{2,0,1:T(2,128)S(1)}, s32[2,9,1024]{2,0,1:T(2,128)}, u32[]{:S(2)}) copy-start(s32[2,9,1024]{2,0,1:T(2,128)} %param.15) | copy-start | bytes 221188
  2.2 11.1 %all-to-all-start = ((bf16[4,256,128]{2,1,0:T(8,128)(2,1)}), bf16[4,256,128]{2,1,0:T(8,128)(2,1)S(1)}, u32[]{:S(2)}, u32[]{:S(2)}) async-start(bf16[4,256,128]{2,1,0:T(8,128)(2,1)} %broadcast_in_dim.10), calls=%async_computation | async-start | bytes 524288 | tf_op jit(solution)/shard_map/all_to_all | solution.py:226
  6.6 0.7 copy-start.6
  13.3 7.7 %collective-permute-start.1 = (bf16[4,256,128]{2,1,0:T(8,128)(2,1)S(1)}, bf16[4,256,128]{2,1,0:T(8,128)(2,1)S(1)}, u32[]{:S(2)}, u32[]{:S(2)}) collective-permute-start(bf16[4,256,128]{2,1,0:T(8,128)(2,1)S(1)} %all-to-all-done.x_ref), channel_id=1, source_target_pairs={{4,8},{12,16},{20,24},{28,32},{36,40},{44,48},{52,56},{60,64},{68,... | collective-permute-start | bytes 786440 | tf_op jit(solution)/shard_map/ppermute | solution.py:255
  15.2 5.8 %collective-permute-start = (bf16[4,256,128]{2,1,0:T(8,128)(2,1)S(1)}, bf16[4,256,128]{2,1,0:T(8,128)(2,1)S(1)}, u32[]{:S(2)}, u32[]{:S(2)}) collective-permute-start(bf16[4,256,128]{2,1,0:T(8,128)(2,1)S(1)} %all-to-all-done.x_ref), channel_id=1, source_target_pairs={{0,4},{4,0},{8,12},{12,8},{16,20},{20,16},{24,28},{28,24},{32,36},... | collective-permute-start | bytes 786440 | tf_op jit(solution)/shard_map/ppermute | solution.py:254
  18.9 2.1 %copy-start = (bf16[512,128]{1,0:T(8,128)(2,1)S(1)}, bf16[512,128]{1,0:T(8,128)(2,1)}, u32[]{:S(2)}) copy-start(bf16[512,128]{1,0:T(8,128)(2,1)} %wq_ref.3) | copy-start | bytes 393220
  18.9 2.1 %copy-start.1 = (bf16[512,128]{1,0:T(8,128)(2,1)S(1)}, bf16[512,128]{1,0:T(8,128)(2,1)}, u32[]{:S(2)}) copy-start(bf16[512,128]{1,0:T(8,128)(2,1)} %wk_ref.3) | copy-start | bytes 393220
  18.9 2.1 %copy-start.2 = (bf16[512,128]{1,0:T(8,128)(2,1)S(1)}, bf16[512,128]{1,0:T(8,128)(2,1)}, u32[]{:S(2)}) copy-start(bf16[512,128]{1,0:T(8,128)(2,1)} %wv_ref.3) | copy-start | bytes 393220
  18.9 2.1 %copy-start.3 = (bf16[256,128]{1,0:T(8,128)(2,1)S(1)}, bf16[256,128]{1,0:T(8,128)(2,1)}, u32[]{:S(2)}) copy-start(bf16[256,128]{1,0:T(8,128)(2,1)} %up_ref.1) | copy-start | bytes 196612
  18.9 2.1 %copy-start.4 = (f32[2]{0:T(128)S(1)}, f32[2]{0:T(128)}, u32[]{:S(2)}) copy-start(f32[2]{0:T(128)} %scale_ref.1) | copy-start | bytes 28
  25.4 3.3 %collective-permute-start.4 = (bf16[768,128]{1,0:T(8,128)(2,1)S(1)}, bf16[768,128]{1,0:T(8,128)(2,1)S(1)}, u32[]{:S(2)}, u32[]{:S(2)}) collective-permute-start(bf16[768,128]{1,0:T(8,128)(2,1)S(1)} %get-tuple-element.21), channel_id=1, source_target_pairs={{0,4},{4,0},{8,12},{12,8},{16,20},{20,16},{24,28},{28,24},{32,36},... | collective-permute-start | bytes 589832 | tf_op jit(solution)/shard_map/ppermute | solution.py:273
  61.8 18.7 %all-to-all-start.3 = ((bf16[64,12,128]{2,1,0:T(8,128)(2,1)}), bf16[64,12,128]{2,1,0:T(8,128)(2,1)S(1)}, u32[]{:S(2)}, u32[]{:S(2)}) async-start(bf16[64,12,128]{2,1,0:T(8,128)(2,1)} %broadcast_in_dim.12), calls=%async_computation.3 | async-start | bytes 524288 | tf_op jit(solution)/shard_map/all_to_all | solution.py:226
  66.9 4.5 %collective-permute-start.2 = (bf16[144,256]{1,0:T(8,128)(2,1)S(1)}, bf16[144,256]{1,0:T(8,128)(2,1)S(1)}, u32[]{:S(2)}, u32[]{:S(2)}) collective-permute-start(bf16[144,256]{1,0:T(8,128)(2,1)S(1)} %get-tuple-element.18), channel_id=1, source_target_pairs={{0,4},{4,0},{8,12},{12,8},{16,20},{20,16},{24,28},{28,24},{32,36},... | collective-permute-start | bytes 221192 | tf_op jit(solution)/shard_map/ppermute | solution.py:274
  68.9 5.8 %collective-permute-start.3 = (bf16[144,256]{1,0:T(8,128)(2,1)S(1)}, bf16[144,256]{1,0:T(8,128)(2,1)S(1)}, u32[]{:S(2)}, u32[]{:S(2)}) collective-permute-start(bf16[144,256]{1,0:T(8,128)(2,1)S(1)} %get-tuple-element.19), channel_id=1, source_target_pairs={{4,8},{12,16},{20,24},{28,32},{36,40},{44,48},{52,56},{60,64},{68,... | collective-permute-start | bytes 221192 | tf_op jit(solution)/shard_map/ppermute | solution.py:275
  80.5 10.1 %all-to-all-start.1 = ((bf16[4,256,128]{2,1,0:T(8,128)(2,1)}), bf16[4,256,128]{2,1,0:T(8,128)(2,1)S(1)}, u32[]{:S(2)}, u32[]{:S(2)}) async-start(bf16[4,256,128]{2,1,0:T(8,128)(2,1)} %shard_map.121), calls=%async_computation.1 | async-start | bytes 524288 | tf_op jit(solution)/shard_map/all_to_all | solution.py:282
  84.0 7.3 %collective-permute-start.5 = (bf16[768,128]{1,0:T(8,128)(2,1)S(1)}, bf16[768,128]{1,0:T(8,128)(2,1)S(1)}, u32[]{:S(2)}, u32[]{:S(2)}) collective-permute-start(bf16[768,128]{1,0:T(8,128)(2,1)S(1)} %reshape.19.refs_1_), channel_id=1, source_target_pairs={{0,4},{4,0},{8,12},{12,8},{16,20},{20,16},{24,28},{28,24},{32,36},... | collective-permute-start | bytes 589832 | tf_op jit(solution)/shard_map/ppermute | solution.py:287

commit v3 on v2

--- a/solution.py
+++ b/solution.py
@@ -99,6 +99,7 @@
     away_ref,
     x_all,
     dw,
+    away,
 ):
     core, before, after = info_ref[0], info_ref[1], info_ref[2]
     n = LANES
@@ -191,13 +192,29 @@
         put(back_a_ref, sides[0])
         put(back_b_ref, sides[1])
 
-    for j in range(3):
-        rows, columns = slice(2 * n * j, 2 * n * (j + 1)), slice(n * j, n * (j + 1))
-        keep_ref[rows] = dw[pl.ds(core * 2 * n, 2 * n), columns]
-        away_ref[rows] = dw[pl.ds((1 - core) * 2 * n, 2 * n), columns].astype(BF16)
-
-
-def input_kernel(gq_ref, gown_ref, back_a_ref, back_b_ref, wq_ref, wk_ref, wv_ref, part_ref):
+    for ref, half in ((keep_ref, core), (away, 1 - core)):
+        for j in range(3):
+            for i in range(4):
+                rows = pl.ds(pl.multiple_of(half * 2 * n + i * 64, 64), 64)
+                ref[:, 4 * j + i, :] = dw[rows, n * j : n * (j + 1)]
+    away_ref[...] = away[...].astype(BF16)
+
+
+def input_kernel(
+    member_ref,
+    gq_ref,
+    gown_ref,
+    back_a_ref,
+    back_b_ref,
+    wq_ref,
+    wk_ref,
+    wv_ref,
+    own_ref,
+    one_ref,
+    two_ref,
+    three_ref,
+    pieces,
+):
     n = LANES
     g = [gown_ref[:n], gown_ref[n:]]
     for ref in (back_a_ref, back_b_ref):
@@ -209,21 +226,42 @@
     part += mul(g[:, :n], wk_ref[...], NT)
     part += mul(g[:, n:], wv_ref[...], NT)
     for i in range(4):
-        part_ref[i] = part[:, i * n : (i + 1) * n].astype(BF16)
-
-
-def final_kernel(grad_scale, core_ref, mine_ref, other_ref, gq_ref, gk_ref, gv_ref):
+        pieces[i] = part[:, i * n : (i + 1) * n]
+    member = member_ref[0]
+    own_ref[...] = pieces[member]
+    for step, ref in enumerate((one_ref, two_ref, three_ref)):
+        ref[...] = pieces[lax.rem(member + step + 1, 4)].astype(BF16)
+
+
+def copies_kernel(value_ref, out_ref):
+    for i in range(out_ref.shape[0]):
+        out_ref[i] = value_ref[...]
+
+
+def total_kernel(got_ref, out_ref):
+    total = jnp.sum(got_ref[...].astype(F32), axis=0).astype(BF16)
+    out_ref[...] = jnp.broadcast_to(total[None], out_ref.shape)
+
+
+def add_kernel(own_ref, one_ref, two_ref, three_ref, out_ref):
+    total = own_ref[...] + one_ref[...].astype(F32)
+    total = total + two_ref[...].astype(F32) + three_ref[...].astype(F32)
+    out_ref[...] = total.astype(BF16)
+
+
+def final_kernel(grad_scale, core_ref, mine_ref, other_ref, gq_ref, gk_ref, gv_ref, wide):
     n = 2 * LANES
     core = core_ref[0]
-    for j, ref in enumerate((gq_ref, gk_ref, gv_ref)):
-        rows = slice(n * j, n * (j + 1))
-        ref[pl.ds(core * n, n), :] = mine_ref[rows].astype(F32) * grad_scale
-        ref[pl.ds((1 - core) * n, n), :] = other_ref[rows].astype(F32) * grad_scale
-
-
-def spread(value, axis, groups, count):
-    copies = jnp.broadcast_to(value[None], (count,) + value.shape)
-    return lax.all_to_all(copies, axis, 0, 0, tiled=True, axis_index_groups=groups)
+    for ref, half in ((mine_ref, core), (other_ref, 1 - core)):
+        wide[...] = ref[...].astype(F32) * grad_scale
+        for j, out in enumerate((gq_ref, gk_ref, gv_ref)):
+            for i in range(4):
+                rows = pl.ds(pl.multiple_of(half * n + i * 64, 64), 64)
+                out[rows, :] = wide[:, 4 * j + i, :]
+
+
+def merge_kernel(keep_ref, swapped_ref, out_ref):
+    out_ref[...] = (keep_ref[...] + swapped_ref[...].astype(F32)).astype(BF16)
 
 
 def shards(x, up, wq, wk, wv, scales, table, bitmap):
@@ -236,7 +274,9 @@
     peers = parts // 2
     groups = [[2 * i + c for i in range(peers)] for c in range(2)]
 
-    gathered = spread(x, "mp", None, lax.axis_size("mp"))
+    members = lax.axis_size("mp")
+    copies = call(copies_kernel, shape((members,) + x.shape, BF16), [VMEM], moved=400_000)(x)
+    gathered = lax.all_to_all(copies, "mp", 0, 0, tiled=True)
 
     side = table // 2 - part
     place = jnp.where(side == 0, table % 2, jnp.where(side < 0, 2, 3))
@@ -251,6 +291,7 @@
         moved=400_000,
     )(place, bitmap)
 
+    gathered, count = lax.optimization_barrier((gathered, count))
     xa = lax.ppermute(gathered, "dom", pairs)
     xb = lax.ppermute(gathered, "dom", edges)
     att, gq, gown, back_a, back_b, keep, away = call(
@@ -261,11 +302,11 @@
             shape((256, 256), F32),
             shape((144, 256), BF16),
             shape((144, 256), BF16),
-            shape((768, 128), F32),
-            shape((768, 128), BF16),
+            shape((64, 12, 128), F32),
+            shape((64, 12, 128), BF16),
         ),
         [SMEM, SMEM] + [VMEM] * 8,
-        [pltpu.VMEM((512, 512), BF16), pltpu.VMEM((512, 384), F32)],
+        [pltpu.VMEM((512, 512), BF16), pltpu.VMEM((512, 384), F32), pltpu.VMEM((64, 12, 128), F32)],
         flops=5_000_000_000,
         moved=4_000_000,
     )(info, scales, gathered, xa, xb, wq, wk, wv, up, count)
@@ -273,17 +314,32 @@
     swapped = lax.ppermute(away, "dom", pairs)
     back_a = lax.ppermute(back_a, "dom", pairs)
     back_b = lax.ppermute(back_b, "dom", edges)
-    pieces = (keep + swapped.astype(F32)).astype(BF16).reshape(peers, -1, LANES)
+    pieces = call(merge_kernel, shape((64, 12, 128), BF16), [VMEM] * 2, moved=800_000)(
+        keep, swapped
+    )
     got = lax.all_to_all(pieces, "dom", 0, 0, tiled=True, axis_index_groups=groups)
 
-    input_part = call(
-        input_kernel, shape((4, 256, 128), BF16), [VMEM] * 7, flops=1_000_000_000, moved=1_500_000
-    )(gq, gown, back_a, back_b, wq, wk, wv)
-    input_parts = lax.all_to_all(input_part, "mp", 0, 0, tiled=True)
-    input_grad = jnp.sum(input_parts.astype(F32), axis=0).astype(BF16)
-
-    mine = jnp.sum(got.astype(F32), axis=0).astype(BF16)
-    mine = spread(mine, "dom", groups, peers).reshape(-1, LANES)
+    totals = call(total_kernel, shape(got.shape, BF16), [VMEM], moved=500_000)(got)
+    totals, back_a, back_b = lax.optimization_barrier((totals, back_a, back_b))
+    member = lax.axis_index("mp").reshape(1)
+    own, one, two, three = call(
+        input_kernel,
+        (shape((256, 128), F32),) + (shape((256, 128), BF16),) * 3,
+        [SMEM] + [VMEM] * 7,
+        [pltpu.VMEM((4, 256, 128), F32)],
+        flops=20_000_000_000,
+        moved=1_500_000,
+    )(member, gq, gown, back_a, back_b, wq, wk, wv)
+    one, two, three = (
+        lax.ppermute(v, "mp", [(i, (i + s) % members) for i in range(members)])
+        for s, v in ((1, one), (2, two), (3, three))
+    )
+    input_grad = call(add_kernel, shape((256, 128), BF16), [VMEM] * 4, moved=400_000)(
+        own, one, two, three
+    )
+
+    mine = lax.all_to_all(totals, "dom", 0, 0, tiled=True, axis_index_groups=groups)
+    mine, input_grad = lax.optimization_barrier((mine, input_grad))
     other = lax.ppermute(mine, "dom", pairs)
     grad_scale = float(parts * 256) ** -0.5
 
@@ -291,7 +347,8 @@
         final_kernel(grad_scale, *refs)
 
     grads = call(
-        finish, (shape((512, 128), F32),) * 3, [SMEM, VMEM, VMEM], moved=1_500_000
+        finish, (shape((512, 128), F32),) * 3, [SMEM, VMEM, VMEM], [pltpu.VMEM((64, 12, 128), F32)],
+        moved=1_500_000,
     )(info[:1], mine, other)
     return (att, input_grad) + tuple(grads)
 

time: 92.9 us -> 91.4 us (0.984)
  the two profiles are of different devices: /device:TPU:8 before, /device:TPU:1 now
where the time goes in v3:
time: 91.4 us; the launch traced here: 90.7 us
  starting transfers between devices  55.7 us (61%)
  waiting for transfers between devices  16.8 us (18%)
  Pallas kernels  10.6 us (12%)
  between operations  4.76 us (5%)
  local copies, waits for them, and re-layouts  2.69 us (3%)
    all_to_all x1, starting transfers between devices, shards(): lax.all_to_all(pieces, 'dom', 0, 0, tiled=True, axis_index_groups=groups)  13.5 us
    ppermute x3, starting transfers between devices, shards(): lax.ppermute(v, 'mp', [(i, (i + s) % members) for i in range(members)])  8.41 us
    all_to_all x1, waiting for transfers between devices, shards(): lax.all_to_all(pieces, 'dom', 0, 0, tiled=True, axis_index_groups=groups)  7.41 us
    all_to_all x1, starting transfers between devices, shards(): lax.all_to_all(totals, 'dom', 0, 0, tiled=True, axis_index_groups=groups)  7.06 us
    ppermute x1, starting transfers between devices, shards(): xb = lax.ppermute(gathered, 'dom', edges)  5.18 us
    ppermute x1, starting transfers between devices, shards(): other = lax.ppermute(mine, 'dom', pairs)  5.06 us
    all_to_all x1, starting transfers between devices, shards(): gathered = lax.all_to_all(copies, 'mp', 0, 0, tiled=True)  4.97 us
    pallas_call x1, Pallas kernels, shards(): call(attend_kernel, (shape((256, 128), BF16), shape((256, 128), BF16), sh...  4.68 us
  transfers between devices with their start and end apart: 12, of which 6 were waited for; matrix products, arithmetic and copies ran while one was open for 1% of the time, Pallas kernels for 3%

profile of v3, /device:TPU:1, one launch (start us, length us, event | category | flops | bytes accessed | tf_op | source)
XLA Modules:
  0.0 90.7 jit_solution(13406694105659541974)
XLA Ops:
  0.6 0.8 copy-done
  1.5 0.7 shard_map.119
  2.2 5.0 %all-to-all-start = ((bf16[4,256,128]{2,1,0:T(8,128)(2,1)}), bf16[4,256,128]{2,1,0:T(8,128)(2,1)S(1)}, u32[]{:S(2)}, u32[]{:S(2)}) async-start(bf16[4,256,128]{2,1,0:T(8,128)(2,1)} %shard_map.119), calls=%async_computation | async-start | bytes 524288 | tf_op jit(solution)/shard_map/all_to_all | solution.py:279
  7.2 0.7 copy-done.7
  7.9 0.1 pad_add_fusion.place_ref
  8.0 1.1 %shard_map.120.count_ref = bf16[256,512]{1,0:T(8,128)(2,1)S(1)} custom-call(s32[2,9]{1,0:T(2,128)S(1)} %pad_add_fusion.place_ref, s32[2,9,1024]{2,1,0:T(8,128)S(1)} %copy.13.words_ref), custom_call_target="tpu_custom_call" | custom-call | flops 2000000000 | bytes 400000 | tf_op jit(solution)/shard_map/pallas_call | solution.py:285
  9.2 3.5 %all-to-all-done.x_ref = bf16[4,256,128]{2,1,0:T(8,128)(2,1)S(1)} async-done(((bf16[4,256,128]{2,1,0:T(8,128)(2,1)}), bf16[4,256,128]{2,1,0:T(8,128)(2,1)S(1)}, u32[]{:S(2)}, u32[]{:S(2)}) %all-to-all-start) | async-done | bytes 262176 | tf_op jit(solution)/shard_map/all_to_all | solution.py:279
  12.7 5.2 %collective-permute-start.1 = (bf16[4,256,128]{2,1,0:T(8,128)(2,1)S(1)}, bf16[4,256,128]{2,1,0:T(8,128)(2,1)S(1)}, u32[]{:S(2)}, u32[]{:S(2)}) collective-permute-start(bf16[4,256,128]{2,1,0:T(8,128)(2,1)S(1)} %all-to-all-done.x_ref), channel_id=1, source_target_pairs={{4,8},{12,16},{20,24},{28,32},{36,40},{44,48},{52,56},{60,64},{68,... | collective-permute-start | bytes 786440 | tf_op jit(solution)/shard_map/ppermute | solution.py:296
  17.9 4.0 %collective-permute-start = (bf16[4,256,128]{2,1,0:T(8,128)(2,1)S(1)}, bf16[4,256,128]{2,1,0:T(8,128)(2,1)S(1)}, u32[]{:S(2)}, u32[]{:S(2)}) collective-permute-start(bf16[4,256,128]{2,1,0:T(8,128)(2,1)S(1)} %all-to-all-done.x_ref), channel_id=1, source_target_pairs={{0,4},{4,0},{8,12},{12,8},{16,20},{20,16},{24,28},{28,24},{32,36},... | collective-permute-start | bytes 786440 | tf_op jit(solution)/shard_map/ppermute | solution.py:295
  21.9 0.6 fusion
  26.4 0.1 pad_add_fusion.1.info_ref
  26.5 0.5 copy-done.5
  27.0 4.7 %shard_map.121 = (bf16[256,128]{1,0:T(8,128)(2,1)}, bf16[256,128]{1,0:T(8,128)(2,1)S(1)}, f32[256,256]{1,0:T(8,128)S(1)}, bf16[144,256]{1,0:T(8,128)(2,1)S(1)}, ...) custom-call(s32[3]{0:T(128)S(1)} %pad_add_fusion.1.info_ref, ...), custom_call_target="tpu_custom_call" | custom-call | flops 5000000000 | bytes 4000000 | tf_op jit(solution)/shard_map/pallas_call | solution.py:297
  31.7 1.9 %collective-permute-start.2 = (bf16[64,12,128]{2,1,0:T(8,128)(2,1)S(1)}, bf16[64,12,128]{2,1,0:T(8,128)(2,1)S(1)}, u32[]{:S(2)}, u32[]{:S(2)}) collective-permute-start(bf16[64,12,128]{2,1,0:T(8,128)(2,1)S(1)} %get-tuple-element.30), channel_id=1, source_target_pairs={{0,4},{4,0},{8,12},{12,8},{16,20},{20,16},{24,28},{28,24},{32,36},... | collective-permute-start | bytes 589832 | tf_op jit(solution)/shard_map/ppermute | solution.py:314
  33.6 1.5 %collective-permute-done.2.swapped_ref = bf16[64,12,128]{2,1,0:T(8,128)(2,1)S(1)} collective-permute-done((bf16[64,12,128]{2,1,0:T(8,128)(2,1)S(1)}, bf16[64,12,128]{2,1,0:T(8,128)(2,1)S(1)}, u32[]{:S(2)}, u32[]{:S(2)}) %collective-permute-start.2) | collective-permute-done | bytes 196640 | tf_op jit(solution)/shard_map/ppermute | solution.py:314
  35.1 0.8 shard_map.122
  35.9 13.5 %all-to-all-start.1 = ((bf16[64,12,128]{2,1,0:T(8,128)(2,1)}), bf16[64,12,128]{2,1,0:T(8,128)(2,1)S(1)}, u32[]{:S(2)}, u32[]{:S(2)}) async-start(bf16[64,12,128]{2,1,0:T(8,128)(2,1)} %shard_map.122), calls=%async_computation.1 | async-start | bytes 524288 | tf_op jit(solution)/shard_map/all_to_all | solution.py:320
  49.4 2.6 %collective-permute-start.3 = (bf16[144,256]{1,0:T(8,128)(2,1)S(1)}, bf16[144,256]{1,0:T(8,128)(2,1)S(1)}, u32[]{:S(2)}, u32[]{:S(2)}) collective-permute-start(bf16[144,256]{1,0:T(8,128)(2,1)S(1)} %get-tuple-element.31), channel_id=1, source_target_pairs={{0,4},{4,0},{8,12},{12,8},{16,20},{20,16},{24,28},{28,24},{32,36},... | collective-permute-start | bytes 221192 | tf_op jit(solution)/shard_map/ppermute | solution.py:315
  52.0 3.1 %collective-permute-start.4 = (bf16[144,256]{1,0:T(8,128)(2,1)S(1)}, bf16[144,256]{1,0:T(8,128)(2,1)S(1)}, u32[]{:S(2)}, u32[]{:S(2)}) collective-permute-start(bf16[144,256]{1,0:T(8,128)(2,1)S(1)} %get-tuple-element.32), channel_id=1, source_target_pairs={{4,8},{12,16},{20,24},{28,32},{36,40},{44,48},{52,56},{60,64},{68,... | collective-permute-start | bytes 221192 | tf_op jit(solution)/shard_map/ppermute | solution.py:316
  55.1 7.4 %all-to-all-done.1.got_ref = bf16[64,12,128]{2,1,0:T(8,128)(2,1)S(1)} async-done(((bf16[64,12,128]{2,1,0:T(8,128)(2,1)}), bf16[64,12,128]{2,1,0:T(8,128)(2,1)S(1)}, u32[]{:S(2)}, u32[]{:S(2)}) %all-to-all-start.1) | async-done | bytes 196640 | tf_op jit(solution)/shard_map/all_to_all | solution.py:320
  62.5 0.8 shard_map.123
  63.3 7.1 %all-to-all-start.2 = ((bf16[64,12,128]{2,1,0:T(8,128)(2,1)}), bf16[64,12,128]{2,1,0:T(8,128)(2,1)S(1)}, u32[]{:S(2)}, u32[]{:S(2)}) async-start(bf16[64,12,128]{2,1,0:T(8,128)(2,1)} %shard_map.123), calls=%async_computation.2 | async-start | bytes 524288 | tf_op jit(solution)/shard_map/all_to_all | solution.py:341
  70.4 0.4 shard_map.124
  70.8 2.2 %collective-permute-start.5 = (bf16[256,128]{1,0:T(8,128)(2,1)S(1)}, bf16[256,128]{1,0:T(8,128)(2,1)S(1)}, u32[]{:S(2)}, u32[]{:S(2)}) collective-permute-start(bf16[256,128]{1,0:T(8,128)(2,1)S(1)} %get-tuple-element.39), channel_id=1, source_target_pairs={{0,1},{1,2},{2,3},{3,0},{4,5},{5,6},{6,7},{7,4},{8,9},{9,10},{10,1... | collective-permute-start | bytes 196616 | tf_op jit(solution)/shard_map/ppermute | solution.py:334
  73.0 3.7 %collective-permute-start.6 = (bf16[256,128]{1,0:T(8,128)(2,1)S(1)}, bf16[256,128]{1,0:T(8,128)(2,1)S(1)}, u32[]{:S(2)}, u32[]{:S(2)}) collective-permute-start(bf16[256,128]{1,0:T(8,128)(2,1)S(1)} %get-tuple-element.40), channel_id=1, source_target_pairs={{0,2},{1,3},{2,0},{3,1},{4,6},{5,7},{6,4},{7,5},{8,10},{9,11},{10,... | collective-permute-start | bytes 196616 | tf_op jit(solution)/shard_map/ppermute | solution.py:334
  76.7 2.5 %collective-permute-start.7 = (bf16[256,128]{1,0:T(8,128)(2,1)S(1)}, bf16[256,128]{1,0:T(8,128)(2,1)S(1)}, u32[]{:S(2)}, u32[]{:S(2)}) collective-permute-start(bf16[256,128]{1,0:T(8,128)(2,1)S(1)} %get-tuple-element.41), channel_id=1, source_target_pairs={{0,3},{1,0},{2,1},{3,2},{4,7},{5,4},{6,5},{7,6},{8,11},{9,8},{10,9... | collective-permute-start | bytes 196616 | tf_op jit(solution)/shard_map/ppermute | solution.py:334
  79.3 0.6 collective-permute-done.6.two_ref
  79.8 2.7 %collective-permute-done.7.three_ref = bf16[256,128]{1,0:T(8,128)(2,1)S(1)} collective-permute-done((bf16[256,128]{1,0:T(8,128)(2,1)S(1)}, bf16[256,128]{1,0:T(8,128)(2,1)S(1)}, u32[]{:S(2)}, u32[]{:S(2)}) %collective-permute-start.7) | collective-permute-done | bytes 65568 | tf_op jit(solution)/shard_map/ppermute | solution.py:334
  82.5 0.7 shard_map.125
  83.1 5.1 %collective-permute-start.8 = (bf16[64,12,128]{2,1,0:T(8,128)(2,1)S(1)}, bf16[64,12,128]{2,1,0:T(8,128)(2,1)S(1)}, u32[]{:S(2)}, u32[]{:S(2)}) collective-permute-start(bf16[64,12,128]{2,1,0:T(8,128)(2,1)S(1)} %all-to-all-done.2.refs_1_), channel_id=1, source_target_pairs={{0,4},{4,0},{8,12},{12,8},{16,20},{20,16},{24,28},{28,24},{32,36},... | collective-permute-start | bytes 589832 | tf_op jit(solution)/shard_map/ppermute | solution.py:343
  88.2 1.1 %collective-permute-done.8.refs_2_ = bf16[64,12,128]{2,1,0:T(8,128)(2,1)S(1)} collective-permute-done((bf16[64,12,128]{2,1,0:T(8,128)(2,1)S(1)}, bf16[64,12,128]{2,1,0:T(8,128)(2,1)S(1)}, u32[]{:S(2)}, u32[]{:S(2)}) %collective-permute-start.8) | collective-permute-done | bytes 196640 | tf_op jit(solution)/shard_map/ppermute | solution.py:343
  89.3 1.3 %shard_map.126 = (f32[512,128]{1,0:T(8,128)}, f32[512,128]{1,0:T(8,128)}, f32[512,128]{1,0:T(8,128)}) custom-call(s32[1]{0:T(128)} %bitcast.refs_0_, bf16[64,12,128]{2,1,0:T(8,128)(2,1)S(1)} %all-to-all-done.2.refs_1_, bf16[64,12,128]{2,1,0:T(8,128)(2,1)S(1)} %collective-permute-done.8.refs_2_), custom_call_target="tpu_custom_call" | custom-call | bytes 1500000 | tf_op jit(solution)/shard_map/pallas_call | solution.py:349
  (22 shorter events, 0.1 us)
Async XLA Ops:
  0.6 0.8 copy-start
  2.2 5.8 %copy-start.6 = (s32[2,9,1024]{2,0,1:T(2,128)S(1)}, s32[2,9,1024]{2,0,1:T(2,128)}, u32[]{:S(2)}) copy-start(s32[2,9,1024]{2,0,1:T(2,128)} %param.15) | copy-start | bytes 221188
  2.2 10.5 %all-to-all-start = ((bf16[4,256,128]{2,1,0:T(8,128)(2,1)}), bf16[4,256,128]{2,1,0:T(8,128)(2,1)S(1)}, u32[]{:S(2)}, u32[]{:S(2)}) async-start(bf16[4,256,128]{2,1,0:T(8,128)(2,1)} %shard_map.119), calls=%async_computation | async-start | bytes 524288 | tf_op jit(solution)/shard_map/all_to_all | solution.py:279
  7.2 0.7 copy-start.7
  8.0 18.5 %copy-start.1 = (bf16[512,128]{1,0:T(8,128)(2,1)S(1)}, bf16[512,128]{1,0:T(8,128)(2,1)}, u32[]{:S(2)}) copy-start(bf16[512,128]{1,0:T(8,128)(2,1)} %wq_ref.3) | copy-start | bytes 393220
  8.0 18.5 %copy-start.2 = (bf16[512,128]{1,0:T(8,128)(2,1)S(1)}, bf16[512,128]{1,0:T(8,128)(2,1)}, u32[]{:S(2)}) copy-start(bf16[512,128]{1,0:T(8,128)(2,1)} %wk_ref.3) | copy-start | bytes 393220
  8.0 18.5 %copy-start.3 = (bf16[512,128]{1,0:T(8,128)(2,1)S(1)}, bf16[512,128]{1,0:T(8,128)(2,1)}, u32[]{:S(2)}) copy-start(bf16[512,128]{1,0:T(8,128)(2,1)} %wv_ref.3) | copy-start | bytes 393220
  9.2 17.3 %copy-start.4 = (bf16[256,128]{1,0:T(8,128)(2,1)S(1)}, bf16[256,128]{1,0:T(8,128)(2,1)}, u32[]{:S(2)}) copy-start(bf16[256,128]{1,0:T(8,128)(2,1)} %up_ref.1) | copy-start | bytes 196612
  12.7 13.8 %collective-permute-start.1 = (bf16[4,256,128]{2,1,0:T(8,128)(2,1)S(1)}, bf16[4,256,128]{2,1,0:T(8,128)(2,1)S(1)}, u32[]{:S(2)}, u32[]{:S(2)}) collective-permute-start(bf16[4,256,128]{2,1,0:T(8,128)(2,1)S(1)} %all-to-all-done.x_ref), channel_id=1, source_target_pairs={{4,8},{12,16},{20,24},{28,32},{36,40},{44,48},{52,56},{60,64},{68,... | collective-permute-start | bytes 786440 | tf_op jit(solution)/shard_map/ppermute | solution.py:296
  17.9 8.6 %collective-permute-start = (bf16[4,256,128]{2,1,0:T(8,128)(2,1)S(1)}, bf16[4,256,128]{2,1,0:T(8,128)(2,1)S(1)}, u32[]{:S(2)}, u32[]{:S(2)}) collective-permute-start(bf16[4,256,128]{2,1,0:T(8,128)(2,1)S(1)} %all-to-all-done.x_ref), channel_id=1, source_target_pairs={{0,4},{4,0},{8,12},{12,8},{16,20},{20,16},{24,28},{28,24},{32,36},... | collective-permute-start | bytes 786440 | tf_op jit(solution)/shard_map/ppermute | solution.py:295
  26.4 0.7 copy-start.5
  31.7 3.4 %collective-permute-start.2 = (bf16[64,12,128]{2,1,0:T(8,128)(2,1)S(1)}, bf16[64,12,128]{2,1,0:T(8,128)(2,1)S(1)}, u32[]{:S(2)}, u32[]{:S(2)}) collective-permute-start(bf16[64,12,128]{2,1,0:T(8,128)(2,1)S(1)} %get-tuple-element.30), channel_id=1, source_target_pairs={{0,4},{4,0},{8,12},{12,8},{16,20},{20,16},{24,28},{28,24},{32,36},... | collective-permute-start | bytes 589832 | tf_op jit(solution)/shard_map/ppermute | solution.py:314
  35.9 26.6 %all-to-all-start.1 = ((bf16[64,12,128]{2,1,0:T(8,128)(2,1)}), bf16[64,12,128]{2,1,0:T(8,128)(2,1)S(1)}, u32[]{:S(2)}, u32[]{:S(2)}) async-start(bf16[64,12,128]{2,1,0:T(8,128)(2,1)} %shard_map.122), calls=%async_computation.1 | async-start | bytes 524288 | tf_op jit(solution)/shard_map/all_to_all | solution.py:320
  49.4 13.9 %collective-permute-start.3 = (bf16[144,256]{1,0:T(8,128)(2,1)S(1)}, bf16[144,256]{1,0:T(8,128)(2,1)S(1)}, u32[]{:S(2)}, u32[]{:S(2)}) collective-permute-start(bf16[144,256]{1,0:T(8,128)(2,1)S(1)} %get-tuple-element.31), channel_id=1, source_target_pairs={{0,4},{4,0},{8,12},{12,8},{16,20},{20,16},{24,28},{28,24},{32,36},... | collective-permute-start | bytes 221192 | tf_op jit(solution)/shard_map/ppermute | solution.py:315
  52.0 11.3 %collective-permute-start.4 = (bf16[144,256]{1,0:T(8,128)(2,1)S(1)}, bf16[144,256]{1,0:T(8,128)(2,1)S(1)}, u32[]{:S(2)}, u32[]{:S(2)}) collective-permute-start(bf16[144,256]{1,0:T(8,128)(2,1)S(1)} %get-tuple-element.32), channel_id=1, source_target_pairs={{4,8},{12,16},{20,24},{28,32},{36,40},{44,48},{52,56},{60,64},{68,... | collective-permute-start | bytes 221192 | tf_op jit(solution)/shard_map/ppermute | solution.py:316
  63.3 19.8 %all-to-all-start.2 = ((bf16[64,12,128]{2,1,0:T(8,128)(2,1)}), bf16[64,12,128]{2,1,0:T(8,128)(2,1)S(1)}, u32[]{:S(2)}, u32[]{:S(2)}) async-start(bf16[64,12,128]{2,1,0:T(8,128)(2,1)} %shard_map.123), calls=%async_computation.2 | async-start | bytes 524288 | tf_op jit(solution)/shard_map/all_to_all | solution.py:341
  70.8 8.4 %collective-permute-start.5 = (bf16[256,128]{1,0:T(8,128)(2,1)S(1)}, bf16[256,128]{1,0:T(8,128)(2,1)S(1)}, u32[]{:S(2)}, u32[]{:S(2)}) collective-permute-start(bf16[256,128]{1,0:T(8,128)(2,1)S(1)} %get-tuple-element.39), channel_id=1, source_target_pairs={{0,1},{1,2},{2,3},{3,0},{4,5},{5,6},{6,7},{7,4},{8,9},{9,10},{10,1... | collective-permute-start | bytes 196616 | tf_op jit(solution)/shard_map/ppermute | solution.py:334
  73.0 6.8 %collective-permute-start.6 = (bf16[256,128]{1,0:T(8,128)(2,1)S(1)}, bf16[256,128]{1,0:T(8,128)(2,1)S(1)}, u32[]{:S(2)}, u32[]{:S(2)}) collective-permute-start(bf16[256,128]{1,0:T(8,128)(2,1)S(1)} %get-tuple-element.40), channel_id=1, source_target_pairs={{0,2},{1,3},{2,0},{3,1},{4,6},{5,7},{6,4},{7,5},{8,10},{9,11},{10,... | collective-permute-start | bytes 196616 | tf_op jit(solution)/shard_map/ppermute | solution.py:334
  76.7 5.8 %collective-permute-start.7 = (bf16[256,128]{1,0:T(8,128)(2,1)S(1)}, bf16[256,128]{1,0:T(8,128)(2,1)S(1)}, u32[]{:S(2)}, u32[]{:S(2)}) collective-permute-start(bf16[256,128]{1,0:T(8,128)(2,1)S(1)} %get-tuple-element.41), channel_id=1, source_target_pairs={{0,3},{1,0},{2,1},{3,2},{4,7},{5,4},{6,5},{7,6},{8,11},{9,8},{10,9... | collective-permute-start | bytes 196616 | tf_op jit(solution)/shard_map/ppermute | solution.py:334
  83.1 6.2 %collective-permute-start.8 = (bf16[64,12,128]{2,1,0:T(8,128)(2,1)S(1)}, bf16[64,12,128]{2,1,0:T(8,128)(2,1)S(1)}, u32[]{:S(2)}, u32[]{:S(2)}) collective-permute-start(bf16[64,12,128]{2,1,0:T(8,128)(2,1)S(1)} %all-to-all-done.2.refs_1_), channel_id=1, source_target_pairs={{0,4},{4,0},{8,12},{12,8},{16,20},{20,16},{24,28},{28,24},{32,36},... | collective-permute-start | bytes 589832 | tf_op jit(solution)/shard_map/ppermute | solution.py:343

commit v4 on v3

v4 whole, which is shorter than its diff:
```python
import jax
import jax.numpy as jnp
from jax import lax
from jax.experimental import pallas as pl
from jax.experimental.pallas import tpu as pltpu
from jax.sharding import PartitionSpec as P

EPS = 1e-06
F32 = jnp.float32
BF16 = jnp.bfloat16
LANES = 128
VMEM = pl.BlockSpec(memory_space=pltpu.VMEM)
SMEM = pl.BlockSpec(memory_space=pltpu.SMEM)
NN = (((1,), (0,)), ((), ()))
NT = (((1,), (1,)), ((), ()))
TN = (((0,), (0,)), ((), ()))


def mul(a, b, dims=NN):
    return lax.dot_general(a, b, dims, preferred_element_type=F32)


def call(kernel, out, in_specs, scratch=(), flops=0, moved=0):
    return pl.pallas_call(
        kernel,
        out_shape=out,
        in_specs=in_specs,
        out_specs=jax.tree.map(lambda _: VMEM, out),
        scratch_shapes=list(scratch),
        compiler_params=pltpu.CompilerParams(vmem_limit_bytes=40 * 1024 * 1024),
        cost_estimate=pl.CostEstimate(flops=flops, bytes_accessed=moved, transcendentals=0),
    )


def shape(dims, kind):
    return jax.ShapeDtypeStruct(dims, kind)


def count_kernel(part_ref, table_ref, words_ref, count_ref, total):
    blocks, tiles, words = words_ref.shape
    block = LANES
    per_row = words // block
    rows = block // per_row * 1
    total[...] = jnp.zeros_like(total)
    lane = lax.broadcasted_iota(jnp.int32, (block, block), 1)
    row = lax.broadcasted_iota(jnp.int32, (block, block), 0)
    same = (row % per_row) == (lane // 16)
    low_pick = jnp.where(same & (lane % 16 < 8), 1.0, 0.0)
    high_pick = jnp.where(same & (lane % 16 >= 8), 1.0, 0.0)
    pick = jnp.concatenate([low_pick, high_pick], axis=0).astype(BF16)
    mine = (row[:rows] == lane[:rows] // per_row).astype(F32)
    shift = lane % 8
    for b in range(blocks):
        for t in range(tiles):
            line = words_ref[b, t : t + 1, :]
            low = (line & 255).astype(F32)
            high = lax.shift_right_logical(line, 8).astype(F32)
            spread_rows = []
            for r in range(per_row):
                at = slice(r * block, (r + 1) * block)
                spread_rows.append(
                    jnp.concatenate([low[:, at] * mine, high[:, at] * mine], axis=1)
                )
            wide = jnp.concatenate(spread_rows, axis=0).astype(BF16)
            byte = mul(wide, pick).astype(jnp.int32)
            bits = (lax.shift_right_logical(byte, shift) & 1).astype(F32)
            place = b
            if t > 0:
                block_id = table_ref[b, t - 1]
                side = block_id // 2 - part_ref[0]
                place = jnp.where(side == 0, block_id % 2, jnp.where(side < 0, 2, 3))
            total[b, place] = total[b, place] + bits
    for b in range(blocks):
        for s in range(4):
            count_ref[b * block : (b + 1) * block, s * block : (s + 1) * block] = total[
                b, s
            ].astype(BF16)


def head_mixer():
    n = LANES
    row = lax.broadcasted_iota(jnp.int32, (2 * n, n), 0) % n
    lane = lax.broadcasted_iota(jnp.int32, (2 * n, n), 1)
    return jnp.where(row // 64 == lane // 64, 1.0 / 64, 0.0).astype(BF16)


def head_mean(value, mixer):
    high = value.astype(BF16)
    low = (value - high.astype(F32)).astype(BF16)
    return mul(jnp.concatenate([high, low], axis=1), mixer)


def head_lanes():
    first = lax.broadcasted_iota(jnp.int32, (1, LANES), 1) < 64
    ones = first.astype(F32)
    return first, [ones.astype(BF16), (1 - ones).astype(BF16)]


def own_kernel(
    scale_ref,
    x_ref,
    wq_ref,
    wk_ref,
    wv_ref,
    up_ref,
    count_ref,
    q_unit_ref,
    q_scale_ref,
    k_unit_ref,
    k_scale_ref,
    v_ref,
    e_ref,
    gw_ref,
    x_own,
):
    n = LANES
    for i in range(4):
        x_own[:, i * n : (i + 1) * n] = x_ref[i]
    x = x_own[...]
    mixer = head_mixer()
    first, heads = head_lanes()
    w_kv = jnp.concatenate([wk_ref[...], wv_ref[...]], axis=1)
    kv = mul(x, w_kv)
    q, k = mul(x, wq_ref[...]), kv[:, :n]
    q_scale = lax.rsqrt(head_mean(q * q, mixer) + EPS)
    k_scale = lax.rsqrt(head_mean(k * k, mixer) + EPS)
    q_unit, k_unit = q * q_scale, k * k_scale
    q_unit_ref[...], q_scale_ref[...] = q_unit, q_scale
    k_unit_ref[...], k_scale_ref[...] = k_unit, k_scale
    q_round, k_round, v_round = q_unit.astype(BF16), k_unit.astype(BF16), kv[:, n:].astype(BF16)
    v_ref[...] = v_round
    count = count_ref[:, : 2 * n].astype(F32)
    up = up_ref[...]
    for h in range(2):
        scores = mul(q_round * heads[h], k_round, NT) * (scale_ref[h] / 64)
        e_ref[h] = count * jnp.exp(scores)
        gw_ref[h] = mul(up * heads[h], v_round, NT)


def attend_kernel(
    part_ref,
    table_ref,
    scale_ref,
    x_ref,
    xa_ref,
    xb_ref,
    wk_ref,
    wv_ref,
    up_ref,
    count_ref,
    q_unit_ref,
    q_scale_ref,
    k_unit_ref,
    k_scale_ref,
    v_ref,
    e_ref,
    gw_ref,
    att_ref,
    gq_ref,
    gown_ref,
    back_a_ref,
    back_b_ref,
    pieces_ref,
    x_all,
    dw,
    wide,
    kv_near,
    q_stack,
    up_stack,
    gs_stack,
    w_stack,
):
    core, before, after = part_ref[0] % 2, table_ref[0, 0] % 2, table_ref[0, 1] % 2
    n = LANES
    for i in range(4):
        x_all[0 : 2 * n, i * n : (i + 1) * n] = x_ref[i]

    @pl.when(core == 0)
    def _():
        for i in range(4):
            x_all[2 * n : 3 * n, i * n : (i + 1) * n] = xb_ref[i, pl.ds(before * n, n), :]
            x_all[3 * n : 4 * n, i * n : (i + 1) * n] = xa_ref[i, pl.ds(after * n, n), :]

    @pl.when(core != 0)
    def _():
        for i in range(4):
            x_all[2 * n : 3 * n, i * n : (i + 1) * n] = xa_ref[i, pl.ds(before * n, n), :]
            x_all[3 * n : 4 * n, i * n : (i + 1) * n] = xb_ref[i, pl.ds(after * n, n), :]

    mixer = head_mixer()
    first, heads = head_lanes()
    w_kv = jnp.concatenate([wk_ref[...], wv_ref[...]], axis=1)
    kv_near[...] = mul(x_all[2 * n :], w_kv)
    k = kv_near[:, :n]
    near_scale = lax.rsqrt(head_mean(k * k, mixer) + EPS)
    near_unit = k * near_scale
    k_near, v_near = near_unit.astype(BF16), kv_near[:, n:].astype(BF16)
    k_round = jnp.concatenate([k_unit_ref[...].astype(BF16), k_near], axis=0)
    v_round = jnp.concatenate([v_ref[...], v_near], axis=0)
    q_round, up = q_unit_ref[...].astype(BF16), up_ref[...]
    factors = [scale_ref[0] / 64, scale_ref[1] / 64]
    lane_factor = jnp.where(first, factors[0], factors[1])
    for b in range(2):
        at = slice(b * n, (b + 1) * n)
        count = count_ref[at, 2 * n :].astype(F32)
        for h in range(2):
            put = slice((2 * b + h) * n, (2 * b + h + 1) * n)
            q_h, up_h = q_round[at] * heads[h], up[at] * heads[h]
            q_stack[put], up_stack[put] = q_h, up_h
            far = count * jnp.exp(mul(q_h, k_near, NT) * factors[h])
            own = e_ref[h, at, :]
            total = jnp.sum(own[:, :n] + own[:, n:] + far[:, :n] + far[:, n:], axis=1, keepdims=True)
            inverse = 1.0 / total
            own, far = own * inverse, far * inverse
            gw_own, gw_far = gw_ref[h, at, :], mul(up_h, v_near, NT)
            own_d, far_d = own * gw_own, far * gw_far
            delta = jnp.sum(
                own_d[:, :n] + own_d[:, n:] + far_d[:, :n] + far_d[:, n:], axis=1, keepdims=True
            )
            w_stack[put, : 2 * n], w_stack[put, 2 * n :] = own.astype(BF16), far.astype(BF16)
            gs_stack[put, : 2 * n] = (own_d - own * delta).astype(BF16)
            gs_stack[put, 2 * n :] = (far_d - far * delta).astype(BF16)
    gqn = []
    for b in range(2):
        low, high = slice(2 * b * n, (2 * b + 1) * n), slice((2 * b + 1) * n, (2 * b + 2) * n)
        at = slice(b * n, (b + 1) * n)
        att = jnp.where(first, mul(w_stack[low], v_round), mul(w_stack[high], v_round))
        att_ref[at] = att.astype(BF16)
        gqn.append(jnp.where(first, mul(gs_stack[low], k_round), mul(gs_stack[high], k_round)))
    gqn = jnp.concatenate(gqn, axis=0) * lane_factor
    gkn = mul(gs_stack[...], q_stack[...], TN) * lane_factor
    gv = mul(w_stack[...], up_stack[...], TN)
    q_unit, q_scale = q_unit_ref[...], q_scale_ref[...]
    k_unit = jnp.concatenate([k_unit_ref[...], near_unit], axis=0)
    k_scale = jnp.concatenate([k_scale_ref[...], near_scale], axis=0)
    gq = (q_scale * (gqn - q_unit * head_mean(gqn * q_unit, mixer))).astype(BF16)
    gk = k_scale * (gkn - k_unit * head_mean(gkn * k_unit, mixer))
    gq_ref[...] = gq
    gown_ref[:, :n] = gk[: 2 * n]
    gown_ref[:, n:] = gv[: 2 * n]
    gk_round, gv_round = gk.astype(BF16), gv.astype(BF16)
    dw[:, :n] = mul(x_all[: 2 * n], gq, TN)
    dw[:, n:] = mul(x_all[...], jnp.concatenate([gk_round, gv_round], axis=1), TN)
    for i in range(4):
        lanes = slice((i % 2) * 3 * n, (i % 2 + 1) * 3 * n)
        wide[:, i // 2, lanes] = dw[i * n : (i + 1) * n, :]
    pieces_ref[...] = wide[...].astype(BF16)
    sides = [
        (jnp.concatenate([gk_round[s], gv_round[s]], axis=1), which)
        for s, which in ((slice(2 * n, 3 * n), before), (slice(3 * n, 4 * n), after))
    ]

    def put(ref, side):
        ref[:n] = side[0]
        ref[n:] = jnp.full((16, 2 * n), side[1], jnp.int32).astype(F32).astype(BF16)

    @pl.when(core == 0)
    def _():
        put(back_a_ref, sides[1])
        put(back_b_ref, sides[0])

    @pl.when(core != 0)
    def _():
        put(back_a_ref, sides[0])
        put(back_b_ref, sides[1])


def input_kernel(
    member_ref,
    gq_ref,
    gown_ref,
    back_a_ref,
    back_b_ref,
    wq_ref,
    wk_ref,
    wv_ref,
    own_ref,
    one_ref,
    two_ref,
    three_ref,
    pieces,
):
    n = LANES
    g = [gown_ref[:n], gown_ref[n:]]
    for ref in (back_a_ref, back_b_ref):
        body = ref[:n].astype(F32)
        which = ref[n : n + 16].astype(F32)[:1]
        g = [g[0] + body * (1 - which), g[1] + body * which]
    g = jnp.concatenate(g, axis=0).astype(BF16)
    part = mul(gq_ref[...], wq_ref[...], NT)
    part += mul(g[:, :n], wk_ref[...], NT)
    part += mul(g[:, n:], wv_ref[...], NT)
    for i in range(4):
        pieces[i] = part[:, i * n : (i + 1) * n]
    member = member_ref[0]
    own_ref[...] = pieces[member]
    for step, ref in enumerate((one_ref, two_ref, three_ref)):
        ref[...] = pieces[lax.rem(member + step + 1, 4)].astype(BF16)


def copies_kernel(value_ref, out_ref):
    for i in range(out_ref.shape[0]):
        out_ref[i] = value_ref[...]


def total_kernel(got_ref, out_ref):
    total = jnp.sum(got_ref[...].astype(F32), axis=0).astype(BF16)
    out_ref[...] = jnp.broadcast_to(total[None], out_ref.shape)


def add_kernel(own_ref, one_ref, two_ref, three_ref, out_ref):
    total = own_ref[...] + one_ref[...].astype(F32)
    total = total + two_ref[...].astype(F32) + three_ref[...].astype(F32)
    out_ref[...] = total.astype(BF16)


def final_kernel(grad_scale, mine_ref, gq_ref, gk_ref, gv_ref, wide):
    n = LANES
    wide[...] = mine_ref[...].astype(F32) * grad_scale
    for i in range(4):
        for j, out in enumerate((gq_ref, gk_ref, gv_ref)):
            at = ((i % 2) * 3 + j) * n
            out[i * n : (i + 1) * n, :] = wide[:, i // 2, at : at + n]


def shards(x, up, wq, wk, wv, scales, table, bitmap):
    parts = lax.axis_size("dom")
    part = lax.axis_index("dom")
    pairs = [(i, i ^ 1) for i in range(parts)]
    edges = [(i, i + 1) for i in range(1, parts - 1, 2)]
    edges = edges + [(b, a) for a, b in edges]

    members = lax.axis_size("mp")
    copies = call(copies_kernel, shape((members,) + x.shape, BF16), [VMEM], moved=400_000)(x)
    gathered = lax.all_to_all(copies, "mp", 0, 0, tiled=True)

    part_in = part.astype(jnp.int32).reshape(1)
    count = call(
        count_kernel,
        shape((256, 512), BF16),
        [SMEM, SMEM, VMEM],
        [pltpu.VMEM((2, 4, LANES, LANES), F32)],
        flops=2_000_000_000,
        moved=400_000,
    )(part_in, table, bitmap)

    gathered, count = lax.optimization_barrier((gathered, count))
    xa = lax.ppermute(gathered, "dom", pairs)
    xb = lax.ppermute(gathered, "dom", edges)
    tall = shape((256, 128), F32)
    square = shape((2, 256, 256), F32)
    own_parts = call(
        own_kernel,
        (tall, tall, tall, tall, shape((256, 128), BF16), square, square),
        [SMEM] + [VMEM] * 6,
        [pltpu.VMEM((256, 512), BF16)],
        flops=3_000_000_000,
        moved=3_000_000,
    )(scales, gathered, wq, wk, wv, up, count)
    att, gq, gown, back_a, back_b, pieces = call(
        attend_kernel,
        (
            shape((256, 128), BF16),
            shape((256, 128), BF16),
            shape((256, 256), F32),
            shape((144, 256), BF16),
            shape((144, 256), BF16),
            shape((128, 2, 768), BF16),
        ),
        [SMEM, SMEM, SMEM] + [VMEM] * 14,
        [
            pltpu.VMEM((512, 512), BF16),
            pltpu.VMEM((512, 384), F32),
            pltpu.VMEM((128, 2, 768), F32),
            pltpu.VMEM((256, 256), F32),
            pltpu.VMEM((512, 128), BF16),
            pltpu.VMEM((512, 128), BF16),
            pltpu.VMEM((512, 512), BF16),
            pltpu.VMEM((512, 512), BF16),
        ],
        flops=3_000_000_000,
        moved=4_000_000,
    )(part_in, table, scales, gathered, xa, xb, wk, wv, up, count, *own_parts)

    got = lax.all_to_all(pieces, "dom", 0, 0, tiled=True)
    back_a = lax.ppermute(back_a, "dom", pairs)
    back_b = lax.ppermute(back_b, "dom", edges)
    own, one, two, three = call(
        input_kernel,
        (shape((256, 128), F32),) + (shape((256, 128), BF16),) * 3,
        [SMEM] + [VMEM] * 7,
        [pltpu.VMEM((4, 256, 128), F32)],
        flops=1_000_000_000,
        moved=1_500_000,
    )(lax.axis_index("mp").reshape(1), gq, gown, back_a, back_b, wq, wk, wv)
    got, own, one, two, three = lax.optimization_barrier((got, own, one, two, three))
    totals = call(total_kernel, shape(got.shape, BF16), [VMEM], moved=500_000)(got)
    one, two, three = (
        lax.ppermute(v, "mp", [(i, (i + s) % members) for i in range(members)])
        for s, v in ((1, one), (2, two), (3, three))
    )
    input_grad = call(
        add_kernel, shape((256, 128), BF16), [VMEM] * 4, moved=400_000
    )(own, one, two, three)
    mine = lax.all_to_all(totals, "dom", 0, 0, tiled=True)
    grad_scale = float(parts * 256) ** -0.5

    def finish(*refs):
        final_kernel(grad_scale, *refs)

    grads = call(
        finish,
        (shape((512, 128), F32),) * 3,
        [VMEM],
        [pltpu.VMEM((128, 2, 768), F32)],
        moved=1_500_000,
    )(mine)
    return (att, input_grad) + tuple(grads)


def solution(mesh):
    in_specs = (
        P("dom", "mp"),
        P("dom", "mp"),
        P(None, "mp"),
        P(None, "mp"),
        P(None, "mp"),
        P("mp"),
        P("dom", None),
        P("dom", None, None),
    )
    out_specs = (P("dom", "mp"), P("dom", "mp"), P(None, "mp"), P(None, "mp"), P(None, "mp"))
    return jax.shard_map(shards, mesh=mesh, in_specs=in_specs, out_specs=out_specs, check_vma=False)
```

time: 91.4 us -> 89.9 us (0.984)
  waiting for transfers between devices: 16.8 us -> 24.1 us
  between operations: 4.76 us -> 0.84 us
  starting transfers between devices: 55.7 us -> 51.8 us
  local copies, waits for them, and re-layouts: 2.69 us -> 1.56 us
    ppermute x2 -> x0, starting transfers between devices: 6.96 us -> none  [the longest x1 5.06 us: shards(): other = lax.ppermute(mine, 'dom', pairs)]
    ppermute x1, waiting for transfers between devices: 0.01 us -> 5.56 us  [shards(): back_b = lax.ppermute(back_b, 'dom', edges)]
    all_to_all x2, waiting for transfers between devices: 7.42 us -> 12.3 us  [the longest x1 6.42 us: shards(): got = lax.all_to_all(pieces, 'dom', 0, 0, tiled=True)]
    all_to_all x2, starting transfers between devices: 20.5 us -> 23.6 us  [the longest x1 17.4 us: shards(): got = lax.all_to_all(pieces, 'dom', 0, 0, tiled=True)]
    ppermute x2 -> x0, waiting for transfers between devices: 2.64 us -> none  [the longest x1 1.5 us: shards(): swapped = lax.ppermute(away, 'dom', pairs)]
  transfers between devices with their start and end apart: 12 -> 10, of which waited for: 6 -> 6; matrix products, arithmetic and copies ran while one was open for 1% -> 0% of each run, Pallas kernels for 3% -> 4%
where the time goes in v4:
time: 89.9 us; the launch traced here: 89.3 us
  starting transfers between devices  51.8 us (58%)
  waiting for transfers between devices  24.1 us (27%)
  Pallas kernels  11 us (12%)
  local copies, waits for them, and re-layouts  1.56 us (2%)
    all_to_all x1, starting transfers between devices, shards(): got = lax.all_to_all(pieces, 'dom', 0, 0, tiled=True)  17.4 us
    ppermute x3, starting transfers between devices, shards(): lax.ppermute(v, 'mp', [(i, (i + s) % members) for i in range(members)])  8.41 us
    all_to_all x1, waiting for transfers between devices, shards(): got = lax.all_to_all(pieces, 'dom', 0, 0, tiled=True)  6.42 us
    all_to_all x1, starting transfers between devices, shards(): mine = lax.all_to_all(totals, 'dom', 0, 0, tiled=True)  6.23 us
    all_to_all x1, waiting for transfers between devices, shards(): mine = lax.all_to_all(totals, 'dom', 0, 0, tiled=True)  5.89 us
    ppermute x1, waiting for transfers between devices, shards(): back_b = lax.ppermute(back_b, 'dom', edges)  5.56 us
    ppermute x1, starting transfers between devices, shards(): xb = lax.ppermute(gathered, 'dom', edges)  5.18 us
    all_to_all x1, starting transfers between devices, shards(): gathered = lax.all_to_all(copies, 'mp', 0, 0, tiled=True)  4.97 us
  transfers between devices with their start and end apart: 10, of which 6 were waited for; matrix products, arithmetic and copies ran while one was open for 0% of the time, Pallas kernels for 4%

profile of v4, /device:TPU:1, one launch (start us, length us, event | category | flops | bytes accessed | tf_op | source)
XLA Modules:
  0.0 89.3 jit_solution(5463970893352019700)
XLA Ops:
  0.6 0.8 copy-done
  1.5 0.7 shard_map.119
  2.2 5.0 %all-to-all-start = ((bf16[4,256,128]{2,1,0:T(8,128)(2,1)}), bf16[4,256,128]{2,1,0:T(8,128)(2,1)S(1)}, u32[]{:S(2)}, u32[]{:S(2)}) async-start(bf16[4,256,128]{2,1,0:T(8,128)(2,1)} %shard_map.119), calls=%async_computation | async-start | bytes 524288 | tf_op jit(solution)/shard_map/all_to_all | solution.py:335
  7.2 0.0 copy-start.5
  7.2 0.7 copy-done.5
  7.9 0.0 copy-start.6
  7.9 1.4 %shard_map.120.count_ref = bf16[256,512]{1,0:T(8,128)(2,1)S(1)} custom-call(s32[1]{0:T(128)} %bitcast.part_ref, s32[2,8]{1,0:T(2,128)S(1)} %copy-done.5, s32[2,9,1024]{2,1,0:T(8,128)S(1)} %copy.13.words_ref), custom_call_target="tpu_custom_call" | custom-call | flops 2000000000 | bytes 400000 | tf_op jit(solution)/shard_map/pallas_call | solution.py:338
  9.4 3.4 %all-to-all-done.x_ref = bf16[4,256,128]{2,1,0:T(8,128)(2,1)S(1)} async-done(((bf16[4,256,128]{2,1,0:T(8,128)(2,1)}), bf16[4,256,128]{2,1,0:T(8,128)(2,1)S(1)}, u32[]{:S(2)}, u32[]{:S(2)}) %all-to-all-start) | async-done | bytes 262176 | tf_op jit(solution)/shard_map/all_to_all | solution.py:335
  12.7 5.2 %collective-permute-start.1 = (bf16[4,256,128]{2,1,0:T(8,128)(2,1)S(1)}, bf16[4,256,128]{2,1,0:T(8,128)(2,1)S(1)}, u32[]{:S(2)}, u32[]{:S(2)}) collective-permute-start(bf16[4,256,128]{2,1,0:T(8,128)(2,1)S(1)} %all-to-all-done.x_ref), channel_id=1, source_target_pairs={{4,8},{12,16},{20,24},{28,32},{36,40},{44,48},{52,56},{60,64},{68,... | collective-permute-start | bytes 786440 | tf_op jit(solution)/shard_map/ppermute | solution.py:349
  17.9 4.0 %collective-permute-start = (bf16[4,256,128]{2,1,0:T(8,128)(2,1)S(1)}, bf16[4,256,128]{2,1,0:T(8,128)(2,1)S(1)}, u32[]{:S(2)}, u32[]{:S(2)}) collective-permute-start(bf16[4,256,128]{2,1,0:T(8,128)(2,1)S(1)} %all-to-all-done.x_ref), channel_id=1, source_target_pairs={{0,4},{4,0},{8,12},{12,8},{16,20},{20,16},{24,28},{28,24},{32,36},... | collective-permute-start | bytes 786440 | tf_op jit(solution)/shard_map/ppermute | solution.py:348
  21.9 1.2 %shard_map.121 = (f32[256,128]{1,0:T(8,128)S(1)}, f32[256,128]{1,0:T(8,128)S(1)}, f32[256,128]{1,0:T(8,128)S(1)}, f32[256,128]{1,0:T(8,128)S(1)}, bf16[256,128]{...) custom-call(f32[2]{0:T(128)S(1)} %copy-done.6, ...), custom_call_target="tpu_custom_call" | custom-call | flops 3000000000 | bytes 3000000 | tf_op jit(solution)/shard_map/pallas_call | solution.py:352
  23.2 0.0 collective-permute-done.1.xb_ref
  23.2 0.0 collective-permute-done.xa_ref
  23.2 3.8 %shard_map.122 = (bf16[256,128]{1,0:T(8,128)(2,1)}, bf16[256,128]{1,0:T(8,128)(2,1)S(1)}, f32[256,256]{1,0:T(8,128)S(1)}, bf16[144,256]{1,0:T(8,128)(2,1)S(1)}, ...) custom-call(s32[1]{0:T(128)} %bitcast.part_ref, s32[2,8]{1,0:T(2,128)S(1)} %copy-done.5, f32[2]{0:T(128)S(1)} %copy-done.6, ...), custom_call_target="tpu_custom_call" | custom-call | flops 3000000000 | bytes 4000000 | tf_op jit(solution)/shard_map/pallas_call | solution.py:360
  27.0 17.4 %all-to-all-start.1 = ((bf16[128,2,768]{2,1,0:T(2,128)(2,1)}), bf16[128,2,768]{2,1,0:T(2,128)(2,1)S(1)}, u32[]{:S(2)}, u32[]{:S(2)}) async-start(bf16[128,2,768]{2,1,0:T(2,128)(2,1)} %get-tuple-element.42), calls=%async_computation.1 | async-start | bytes 786432 | tf_op jit(solution)/shard_map/all_to_all | solution.py:385
  44.4 2.8 %collective-permute-start.2 = (bf16[144,256]{1,0:T(8,128)(2,1)S(1)}, bf16[144,256]{1,0:T(8,128)(2,1)S(1)}, u32[]{:S(2)}, u32[]{:S(2)}) collective-permute-start(bf16[144,256]{1,0:T(8,128)(2,1)S(1)} %get-tuple-element.45), channel_id=1, source_target_pairs={{0,4},{4,0},{8,12},{12,8},{16,20},{20,16},{24,28},{28,24},{32,36},... | collective-permute-start | bytes 221192 | tf_op jit(solution)/shard_map/ppermute | solution.py:386
  47.3 2.8 %collective-permute-start.3 = (bf16[144,256]{1,0:T(8,128)(2,1)S(1)}, bf16[144,256]{1,0:T(8,128)(2,1)S(1)}, u32[]{:S(2)}, u32[]{:S(2)}) collective-permute-start(bf16[144,256]{1,0:T(8,128)(2,1)S(1)} %get-tuple-element.46), channel_id=1, source_target_pairs={{4,8},{12,16},{20,24},{28,32},{36,40},{44,48},{52,56},{60,64},{68,... | collective-permute-start | bytes 221192 | tf_op jit(solution)/shard_map/ppermute | solution.py:387
  50.1 0.0 collective-permute-done.2.back_a_ref
  50.1 5.6 %collective-permute-done.3.back_b_ref = bf16[144,256]{1,0:T(8,128)(2,1)S(1)} collective-permute-done((bf16[144,256]{1,0:T(8,128)(2,1)S(1)}, bf16[144,256]{1,0:T(8,128)(2,1)S(1)}, u32[]{:S(2)}, u32[]{:S(2)}) %collective-permute-start.3) | collective-permute-done | bytes 73760 | tf_op jit(solution)/shard_map/ppermute | solution.py:387
  55.6 0.4 shard_map.123
  56.1 6.4 %all-to-all-done.1.got_ref = bf16[128,2,768]{2,1,0:T(2,128)(2,1)S(1)} async-done(((bf16[128,2,768]{2,1,0:T(2,128)(2,1)}), bf16[128,2,768]{2,1,0:T(2,128)(2,1)S(1)}, u32[]{:S(2)}, u32[]{:S(2)}) %all-to-all-start.1) | async-done | bytes 393248 | tf_op jit(solution)/shard_map/all_to_all | solution.py:385
  62.5 1.2 %shard_map.125 = bf16[128,2,768]{2,1,0:T(2,128)(2,1)} custom-call(bf16[128,2,768]{2,1,0:T(2,128)(2,1)S(1)} %all-to-all-done.1.got_ref), custom_call_target="tpu_custom_call" | custom-call | bytes 500000 | tf_op jit(solution)/shard_map/pallas_call | solution.py:397
  63.7 6.2 %all-to-all-start.2 = ((bf16[128,2,768]{2,1,0:T(2,128)(2,1)}), bf16[128,2,768]{2,1,0:T(2,128)(2,1)S(1)}, u32[]{:S(2)}, u32[]{:S(2)}) async-start(bf16[128,2,768]{2,1,0:T(2,128)(2,1)} %shard_map.125), calls=%async_computation.2 | async-start | bytes 786432 | tf_op jit(solution)/shard_map/all_to_all | solution.py:405
  69.9 2.2 %collective-permute-start.4 = (bf16[256,128]{1,0:T(8,128)(2,1)S(1)}, bf16[256,128]{1,0:T(8,128)(2,1)S(1)}, u32[]{:S(2)}, u32[]{:S(2)}) collective-permute-start(bf16[256,128]{1,0:T(8,128)(2,1)S(1)} %get-tuple-element.52), channel_id=1, source_target_pairs={{0,1},{1,2},{2,3},{3,0},{4,5},{5,6},{6,7},{7,4},{8,9},{9,10},{10,1... | collective-permute-start | bytes 196616 | tf_op jit(solution)/shard_map/ppermute | solution.py:399
  72.1 3.7 %collective-permute-start.5 = (bf16[256,128]{1,0:T(8,128)(2,1)S(1)}, bf16[256,128]{1,0:T(8,128)(2,1)S(1)}, u32[]{:S(2)}, u32[]{:S(2)}) collective-permute-start(bf16[256,128]{1,0:T(8,128)(2,1)S(1)} %get-tuple-element.53), channel_id=1, source_target_pairs={{0,2},{1,3},{2,0},{3,1},{4,6},{5,7},{6,4},{7,5},{8,10},{9,11},{10,... | collective-permute-start | bytes 196616 | tf_op jit(solution)/shard_map/ppermute | solution.py:399
  75.8 2.5 %collective-permute-start.6 = (bf16[256,128]{1,0:T(8,128)(2,1)S(1)}, bf16[256,128]{1,0:T(8,128)(2,1)S(1)}, u32[]{:S(2)}, u32[]{:S(2)}) collective-permute-start(bf16[256,128]{1,0:T(8,128)(2,1)S(1)} %get-tuple-element.54), channel_id=1, source_target_pairs={{0,3},{1,0},{2,1},{3,2},{4,7},{5,4},{6,5},{7,6},{8,11},{9,8},{10,9... | collective-permute-start | bytes 196616 | tf_op jit(solution)/shard_map/ppermute | solution.py:399
  78.4 0.0 collective-permute-done.4.one_ref
  78.4 0.6 collective-permute-done.5.two_ref
  78.9 2.3 %collective-permute-done.6.three_ref = bf16[256,128]{1,0:T(8,128)(2,1)S(1)} collective-permute-done((bf16[256,128]{1,0:T(8,128)(2,1)S(1)}, bf16[256,128]{1,0:T(8,128)(2,1)S(1)}, u32[]{:S(2)}, u32[]{:S(2)}) %collective-permute-start.6) | collective-permute-done | bytes 65568 | tf_op jit(solution)/shard_map/ppermute | solution.py:399
  81.3 0.7 shard_map.124
  81.9 5.9 %all-to-all-done.2.refs_0_ = bf16[128,2,768]{2,1,0:T(2,128)(2,1)S(1)} async-done(((bf16[128,2,768]{2,1,0:T(2,128)(2,1)}), bf16[128,2,768]{2,1,0:T(2,128)(2,1)S(1)}, u32[]{:S(2)}, u32[]{:S(2)}) %all-to-all-start.2) | async-done | bytes 393248 | tf_op jit(solution)/shard_map/all_to_all | solution.py:405
  87.8 1.5 %shard_map.126 = (f32[512,128]{1,0:T(8,128)}, f32[512,128]{1,0:T(8,128)}, f32[512,128]{1,0:T(8,128)}) custom-call(bf16[128,2,768]{2,1,0:T(2,128)(2,1)S(1)} %all-to-all-done.2.refs_0_), custom_call_target="tpu_custom_call" | custom-call | bytes 1500000 | tf_op jit(solution)/shard_map/pallas_call | solution.py:411
  (13 shorter events, 0.1 us)
Async XLA Ops:
  0.6 0.8 copy-start
  2.2 5.0 %copy-start.7 = (s32[2,9,1024]{2,0,1:T(2,128)S(1)}, s32[2,9,1024]{2,0,1:T(2,128)}, u32[]{:S(2)}) copy-start(s32[2,9,1024]{2,0,1:T(2,128)} %param.15) | copy-start | bytes 221188
  2.2 10.5 %all-to-all-start = ((bf16[4,256,128]{2,1,0:T(8,128)(2,1)}), bf16[4,256,128]{2,1,0:T(8,128)(2,1)S(1)}, u32[]{:S(2)}, u32[]{:S(2)}) async-start(bf16[4,256,128]{2,1,0:T(8,128)(2,1)} %shard_map.119), calls=%async_computation | async-start | bytes 524288 | tf_op jit(solution)/shard_map/all_to_all | solution.py:335
  7.2 0.7 copy-start.5
  7.9 14.0 %copy-start.1 = (bf16[512,128]{1,0:T(8,128)(2,1)S(1)}, bf16[512,128]{1,0:T(8,128)(2,1)}, u32[]{:S(2)}) copy-start(bf16[512,128]{1,0:T(8,128)(2,1)} %wk_ref.5) | copy-start | bytes 393220
  7.9 14.0 %copy-start.2 = (bf16[512,128]{1,0:T(8,128)(2,1)S(1)}, bf16[512,128]{1,0:T(8,128)(2,1)}, u32[]{:S(2)}) copy-start(bf16[512,128]{1,0:T(8,128)(2,1)} %wv_ref.5) | copy-start | bytes 393220
  7.9 14.0 %copy-start.3 = (bf16[512,128]{1,0:T(8,128)(2,1)S(1)}, bf16[512,128]{1,0:T(8,128)(2,1)}, u32[]{:S(2)}) copy-start(bf16[512,128]{1,0:T(8,128)(2,1)} %wq_ref.3) | copy-start | bytes 393220
  7.9 14.0 %copy-start.4 = (bf16[256,128]{1,0:T(8,128)(2,1)S(1)}, bf16[256,128]{1,0:T(8,128)(2,1)}, u32[]{:S(2)}) copy-start(bf16[256,128]{1,0:T(8,128)(2,1)} %up_ref.3) | copy-start | bytes 196612
  7.9 14.0 %copy-start.6 = (f32[2]{0:T(128)S(1)}, f32[2]{0:T(128)}, u32[]{:S(2)}) copy-start(f32[2]{0:T(128)} %scale_ref.3) | copy-start | bytes 28
  12.7 10.5 %collective-permute-start.1 = (bf16[4,256,128]{2,1,0:T(8,128)(2,1)S(1)}, bf16[4,256,128]{2,1,0:T(8,128)(2,1)S(1)}, u32[]{:S(2)}, u32[]{:S(2)}) collective-permute-start(bf16[4,256,128]{2,1,0:T(8,128)(2,1)S(1)} %all-to-all-done.x_ref), channel_id=1, source_target_pairs={{4,8},{12,16},{20,24},{28,32},{36,40},{44,48},{52,56},{60,64},{68,... | collective-permute-start | bytes 786440 | tf_op jit(solution)/shard_map/ppermute | solution.py:349
  17.9 5.3 %collective-permute-start = (bf16[4,256,128]{2,1,0:T(8,128)(2,1)S(1)}, bf16[4,256,128]{2,1,0:T(8,128)(2,1)S(1)}, u32[]{:S(2)}, u32[]{:S(2)}) collective-permute-start(bf16[4,256,128]{2,1,0:T(8,128)(2,1)S(1)} %all-to-all-done.x_ref), channel_id=1, source_target_pairs={{0,4},{4,0},{8,12},{12,8},{16,20},{20,16},{24,28},{28,24},{32,36},... | collective-permute-start | bytes 786440 | tf_op jit(solution)/shard_map/ppermute | solution.py:348
  27.0 35.5 %all-to-all-start.1 = ((bf16[128,2,768]{2,1,0:T(2,128)(2,1)}), bf16[128,2,768]{2,1,0:T(2,128)(2,1)S(1)}, u32[]{:S(2)}, u32[]{:S(2)}) async-start(bf16[128,2,768]{2,1,0:T(2,128)(2,1)} %get-tuple-element.42), calls=%async_computation.1 | async-start | bytes 786432 | tf_op jit(solution)/shard_map/all_to_all | solution.py:385
  44.4 5.6 %collective-permute-start.2 = (bf16[144,256]{1,0:T(8,128)(2,1)S(1)}, bf16[144,256]{1,0:T(8,128)(2,1)S(1)}, u32[]{:S(2)}, u32[]{:S(2)}) collective-permute-start(bf16[144,256]{1,0:T(8,128)(2,1)S(1)} %get-tuple-element.45), channel_id=1, source_target_pairs={{0,4},{4,0},{8,12},{12,8},{16,20},{20,16},{24,28},{28,24},{32,36},... | collective-permute-start | bytes 221192 | tf_op jit(solution)/shard_map/ppermute | solution.py:386
  47.3 8.4 %collective-permute-start.3 = (bf16[144,256]{1,0:T(8,128)(2,1)S(1)}, bf16[144,256]{1,0:T(8,128)(2,1)S(1)}, u32[]{:S(2)}, u32[]{:S(2)}) collective-permute-start(bf16[144,256]{1,0:T(8,128)(2,1)S(1)} %get-tuple-element.46), channel_id=1, source_target_pairs={{4,8},{12,16},{20,24},{28,32},{36,40},{44,48},{52,56},{60,64},{68,... | collective-permute-start | bytes 221192 | tf_op jit(solution)/shard_map/ppermute | solution.py:387
  63.7 24.1 %all-to-all-start.2 = ((bf16[128,2,768]{2,1,0:T(2,128)(2,1)}), bf16[128,2,768]{2,1,0:T(2,128)(2,1)S(1)}, u32[]{:S(2)}, u32[]{:S(2)}) async-start(bf16[128,2,768]{2,1,0:T(2,128)(2,1)} %shard_map.125), calls=%async_computation.2 | async-start | bytes 786432 | tf_op jit(solution)/shard_map/all_to_all | solution.py:405
  69.9 8.4 %collective-permute-start.4 = (bf16[256,128]{1,0:T(8,128)(2,1)S(1)}, bf16[256,128]{1,0:T(8,128)(2,1)S(1)}, u32[]{:S(2)}, u32[]{:S(2)}) collective-permute-start(bf16[256,128]{1,0:T(8,128)(2,1)S(1)} %get-tuple-element.52), channel_id=1, source_target_pairs={{0,1},{1,2},{2,3},{3,0},{4,5},{5,6},{6,7},{7,4},{8,9},{9,10},{10,1... | collective-permute-start | bytes 196616 | tf_op jit(solution)/shard_map/ppermute | solution.py:399
  72.1 6.8 %collective-permute-start.5 = (bf16[256,128]{1,0:T(8,128)(2,1)S(1)}, bf16[256,128]{1,0:T(8,128)(2,1)S(1)}, u32[]{:S(2)}, u32[]{:S(2)}) collective-permute-start(bf16[256,128]{1,0:T(8,128)(2,1)S(1)} %get-tuple-element.53), channel_id=1, source_target_pairs={{0,2},{1,3},{2,0},{3,1},{4,6},{5,7},{6,4},{7,5},{8,10},{9,11},{10,... | collective-permute-start | bytes 196616 | tf_op jit(solution)/shard_map/ppermute | solution.py:399
  75.8 5.4 %collective-permute-start.6 = (bf16[256,128]{1,0:T(8,128)(2,1)S(1)}, bf16[256,128]{1,0:T(8,128)(2,1)S(1)}, u32[]{:S(2)}, u32[]{:S(2)}) collective-permute-start(bf16[256,128]{1,0:T(8,128)(2,1)S(1)} %get-tuple-element.54), channel_id=1, source_target_pairs={{0,3},{1,0},{2,1},{3,2},{4,7},{5,4},{6,5},{7,6},{8,11},{9,8},{10,9... | collective-permute-start | bytes 196616 | tf_op jit(solution)/shard_map/ppermute | solution.py:399

commit v5 on v4

--- a/solution.py
+++ b/solution.py
@@ -111,12 +111,14 @@
     v_ref,
     e_ref,
     gw_ref,
+    xt_ref,
     x_own,
 ):
     n = LANES
     for i in range(4):
         x_own[:, i * n : (i + 1) * n] = x_ref[i]
     x = x_own[...]
+    xt_ref[...] = x.T
     mixer = head_mixer()
     first, heads = head_lanes()
     w_kv = jnp.concatenate([wk_ref[...], wv_ref[...]], axis=1)
@@ -141,7 +143,6 @@
     part_ref,
     table_ref,
     scale_ref,
-    x_ref,
     xa_ref,
     xb_ref,
     wk_ref,
@@ -155,13 +156,14 @@
     v_ref,
     e_ref,
     gw_ref,
+    xt_ref,
     att_ref,
     gq_ref,
     gown_ref,
-    back_a_ref,
     back_b_ref,
-    pieces_ref,
-    x_all,
+    keep_ref,
+    away_ref,
+    x_near,
     dw,
     wide,
     kv_near,
@@ -172,25 +174,23 @@
 ):
     core, before, after = part_ref[0] % 2, table_ref[0, 0] % 2, table_ref[0, 1] % 2
     n = LANES
-    for i in range(4):
-        x_all[0 : 2 * n, i * n : (i + 1) * n] = x_ref[i]
 
     @pl.when(core == 0)
     def _():
         for i in range(4):
-            x_all[2 * n : 3 * n, i * n : (i + 1) * n] = xb_ref[i, pl.ds(before * n, n), :]
-            x_all[3 * n : 4 * n, i * n : (i + 1) * n] = xa_ref[i, pl.ds(after * n, n), :]
+            x_near[:n, i * n : (i + 1) * n] = xb_ref[i, pl.ds(before * n, n), :]
+            x_near[n:, i * n : (i + 1) * n] = xa_ref[i, pl.ds(after * n, n), :]
 
     @pl.when(core != 0)
     def _():
         for i in range(4):
-            x_all[2 * n : 3 * n, i * n : (i + 1) * n] = xa_ref[i, pl.ds(before * n, n), :]
-            x_all[3 * n : 4 * n, i * n : (i + 1) * n] = xb_ref[i, pl.ds(after * n, n), :]
+            x_near[:n, i * n : (i + 1) * n] = xa_ref[i, pl.ds(before * n, n), :]
+            x_near[n:, i * n : (i + 1) * n] = xb_ref[i, pl.ds(after * n, n), :]
 
     mixer = head_mixer()
     first, heads = head_lanes()
     w_kv = jnp.concatenate([wk_ref[...], wv_ref[...]], axis=1)
-    kv_near[...] = mul(x_all[2 * n :], w_kv)
+    kv_near[...] = mul(x_near[...], w_kv)
     k = kv_near[:, :n]
     near_scale = lax.rsqrt(head_mean(k * k, mixer) + EPS)
     near_unit = k * near_scale
@@ -228,8 +228,8 @@
         att_ref[at] = att.astype(BF16)
         gqn.append(jnp.where(first, mul(gs_stack[low], k_round), mul(gs_stack[high], k_round)))
     gqn = jnp.concatenate(gqn, axis=0) * lane_factor
-    gkn = mul(gs_stack[...], q_stack[...], TN) * lane_factor
-    gv = mul(w_stack[...], up_stack[...], TN)
+    gkn = mul(q_stack[...], gs_stack[...], TN).T * lane_factor
+    gv = mul(up_stack[...], w_stack[...], TN).T
     q_unit, q_scale = q_unit_ref[...], q_scale_ref[...]
     k_unit = jnp.concatenate([k_unit_ref[...], near_unit], axis=0)
     k_scale = jnp.concatenate([k_scale_ref[...], near_scale], axis=0)
@@ -239,37 +239,44 @@
     gown_ref[:, :n] = gk[: 2 * n]
     gown_ref[:, n:] = gv[: 2 * n]
     gk_round, gv_round = gk.astype(BF16), gv.astype(BF16)
-    dw[:, :n] = mul(x_all[: 2 * n], gq, TN)
-    dw[:, n:] = mul(x_all[...], jnp.concatenate([gk_round, gv_round], axis=1), TN)
+    g_own = jnp.concatenate([gq, gk_round[: 2 * n], gv_round[: 2 * n]], axis=1)
+    g_near = jnp.concatenate([gk_round[2 * n :], gv_round[2 * n :]], axis=1)
+    dw[...] = mul(xt_ref[...], g_own)
+    dw[:, n:] += mul(x_near[...], g_near, TN)
     for i in range(4):
-        lanes = slice((i % 2) * 3 * n, (i % 2 + 1) * 3 * n)
-        wide[:, i // 2, lanes] = dw[i * n : (i + 1) * n, :]
-    pieces_ref[...] = wide[...].astype(BF16)
-    sides = [
-        (jnp.concatenate([gk_round[s], gv_round[s]], axis=1), which)
-        for s, which in ((slice(2 * n, 3 * n), before), (slice(3 * n, 4 * n), after))
-    ]
-
-    def put(ref, side):
-        ref[:n] = side[0]
-        ref[n:] = jnp.full((16, 2 * n), side[1], jnp.int32).astype(F32).astype(BF16)
+        for ref, half in ((keep_ref, core), (wide, 1 - core)):
+            rows = pl.ds(pl.multiple_of(half * 2 * n + i * 64, 64), 64)
+            ref[0:64, i, : 3 * n] = dw[rows, :]
+    wide[64] = jnp.full((4, 4 * n), jnp.where(core == 0, after, before), jnp.int32).astype(F32)
+    back_b_ref[n:] = (
+        jnp.full((16, 2 * n), jnp.where(core == 0, before, after), jnp.int32)
+        .astype(F32)
+        .astype(BF16)
+    )
+
+    def put_sides(near, other):
+        for i in range(2):
+            wide[0:64, i, 3 * n :] = gk[near + 64 * i : near + 64 * (i + 1)]
+            wide[0:64, 2 + i, 3 * n :] = gv[near + 64 * i : near + 64 * (i + 1)]
+        back_b_ref[:n, :n] = gk_round[other : other + n]
+        back_b_ref[:n, n:] = gv_round[other : other + n]
 
     @pl.when(core == 0)
     def _():
-        put(back_a_ref, sides[1])
-        put(back_b_ref, sides[0])
+        put_sides(3 * n, 2 * n)
 
     @pl.when(core != 0)
     def _():
-        put(back_a_ref, sides[0])
-        put(back_b_ref, sides[1])
+        put_sides(2 * n, 3 * n)
+
+    away_ref[...] = wide[...].astype(BF16)
 
 
 def input_kernel(
     member_ref,
     gq_ref,
     gown_ref,
-    back_a_ref,
+    swapped_ref,
     back_b_ref,
     wq_ref,
     wk_ref,
@@ -278,14 +285,23 @@
     one_ref,
     two_ref,
     three_ref,
+    wide,
     pieces,
 ):
     n = LANES
-    g = [gown_ref[:n], gown_ref[n:]]
-    for ref in (back_a_ref, back_b_ref):
-        body = ref[:n].astype(F32)
-        which = ref[n : n + 16].astype(F32)[:1]
-        g = [g[0] + body * (1 - which), g[1] + body * which]
+    wide[...] = swapped_ref[:, :, 3 * n :].astype(F32)
+    near = jnp.concatenate(
+        [
+            jnp.concatenate([wide[0:64, i, :], wide[0:64, i + 1, :]], axis=0) for i in (0, 2)
+        ],
+        axis=1,
+    )
+    which = wide[64][:1]
+    which = jnp.concatenate([which, which], axis=1)
+    g = [gown_ref[:n] + near * (1 - which), gown_ref[n:] + near * which]
+    body = back_b_ref[:n].astype(F32)
+    which = back_b_ref[n : n + 16].astype(F32)[:1]
+    g = [g[0] + body * (1 - which), g[1] + body * which]
     g = jnp.concatenate(g, axis=0).astype(BF16)
     part = mul(gq_ref[...], wq_ref[...], NT)
     part += mul(g[:, :n], wk_ref[...], NT)
@@ -303,6 +319,11 @@
         out_ref[i] = value_ref[...]
 
 
+def merge_kernel(keep_ref, swapped_ref, out_ref):
+    width = keep_ref.shape[2]
+    out_ref[...] = (keep_ref[...] + swapped_ref[0:64, :, :width].astype(F32)).astype(BF16)
+
+
 def total_kernel(got_ref, out_ref):
     total = jnp.sum(got_ref[...].astype(F32), axis=0).astype(BF16)
     out_ref[...] = jnp.broadcast_to(total[None], out_ref.shape)
@@ -317,10 +338,11 @@
 def final_kernel(grad_scale, mine_ref, gq_ref, gk_ref, gv_ref, wide):
     n = LANES
     wide[...] = mine_ref[...].astype(F32) * grad_scale
-    for i in range(4):
-        for j, out in enumerate((gq_ref, gk_ref, gv_ref)):
-            at = ((i % 2) * 3 + j) * n
-            out[i * n : (i + 1) * n, :] = wide[:, i // 2, at : at + n]
+    for half in range(2):
+        for i in range(4):
+            rows = slice(half * 256 + i * 64, half * 256 + (i + 1) * 64)
+            for j, out in enumerate((gq_ref, gk_ref, gv_ref)):
+                out[rows, :] = wide[:, half, i, j * n : (j + 1) * n]
 
 
 def shards(x, up, wq, wk, wv, scales, table, bitmap):
@@ -351,27 +373,27 @@
     square = shape((2, 256, 256), F32)
     own_parts = call(
         own_kernel,
-        (tall, tall, tall, tall, shape((256, 128), BF16), square, square),
+        (tall, tall, tall, tall, shape((256, 128), BF16), square, square, shape((512, 256), BF16)),
         [SMEM] + [VMEM] * 6,
         [pltpu.VMEM((256, 512), BF16)],
         flops=3_000_000_000,
         moved=3_000_000,
     )(scales, gathered, wq, wk, wv, up, count)
-    att, gq, gown, back_a, back_b, pieces = call(
+    att, gq, gown, back_b, keep, away = call(
         attend_kernel,
         (
             shape((256, 128), BF16),
             shape((256, 128), BF16),
             shape((256, 256), F32),
             shape((144, 256), BF16),
-            shape((144, 256), BF16),
-            shape((128, 2, 768), BF16),
+            shape((64, 4, 384), F32),
+            shape((65, 4, 512), BF16),
         ),
         [SMEM, SMEM, SMEM] + [VMEM] * 14,
         [
-            pltpu.VMEM((512, 512), BF16),
+            pltpu.VMEM((256, 512), BF16),
             pltpu.VMEM((512, 384), F32),
-            pltpu.VMEM((128, 2, 768), F32),
+            pltpu.VMEM((65, 4, 512), F32),
             pltpu.VMEM((256, 256), F32),
             pltpu.VMEM((512, 128), BF16),
             pltpu.VMEM((512, 128), BF16),
@@ -380,21 +402,25 @@
         ],
         flops=3_000_000_000,
         moved=4_000_000,
-    )(part_in, table, scales, gathered, xa, xb, wk, wv, up, count, *own_parts)
-
-    got = lax.all_to_all(pieces, "dom", 0, 0, tiled=True)
-    back_a = lax.ppermute(back_a, "dom", pairs)
+    )(part_in, table, scales, xa, xb, wk, wv, up, count, *own_parts)
+
+    swapped = lax.ppermute(away, "dom", pairs)
     back_b = lax.ppermute(back_b, "dom", edges)
+    pieces = call(merge_kernel, shape((64, 4, 384), BF16), [VMEM] * 2, moved=800_000)(
+        keep, swapped
+    )
+    groups = [[2 * i + c for i in range(parts // 2)] for c in range(2)]
+    got = lax.all_to_all(pieces, "dom", 0, 0, tiled=True, axis_index_groups=groups)
+    totals = call(total_kernel, shape((128, 4, 384), BF16), [VMEM], moved=500_000)(got)
+    totals, gown = lax.optimization_barrier((totals, gown))
     own, one, two, three = call(
         input_kernel,
         (shape((256, 128), F32),) + (shape((256, 128), BF16),) * 3,
         [SMEM] + [VMEM] * 7,
-        [pltpu.VMEM((4, 256, 128), F32)],
-        flops=1_000_000_000,
+        [pltpu.VMEM((65, 4, 128), F32), pltpu.VMEM((4, 256, 128), F32)],
+        flops=20_000_000_000,
         moved=1_500_000,
-    )(lax.axis_index("mp").reshape(1), gq, gown, back_a, back_b, wq, wk, wv)
-    got, own, one, two, three = lax.optimization_barrier((got, own, one, two, three))
-    totals = call(total_kernel, shape(got.shape, BF16), [VMEM], moved=500_000)(got)
+    )(lax.axis_index("mp").reshape(1), gq, gown, swapped, back_b, wq, wk, wv)
     one, two, three = (
         lax.ppermute(v, "mp", [(i, (i + s) % members) for i in range(members)])
         for s, v in ((1, one), (2, two), (3, three))
@@ -412,9 +438,9 @@
         finish,
         (shape((512, 128), F32),) * 3,
         [VMEM],
-        [pltpu.VMEM((128, 2, 768), F32)],
+        [pltpu.VMEM((64, 2, 4, 384), F32)],
         moved=1_500_000,
-    )(mine)
+    )(mine.reshape(64, 2, 4, 384))
     return (att, input_grad) + tuple(grads)
 
 

time: 89.9 us -> 88.1 us (0.980)
  waiting for transfers between devices: 24.1 us -> 21.7 us
    ppermute x1, waiting for transfers between devices: 5.56 us -> 0.01 us  [shards(): back_b = lax.ppermute(back_b, 'dom', edges)]
    all_to_all x1, waiting for transfers between devices: 6.42 us -> 8.54 us  [shards(): lax.all_to_all(pieces, 'dom', 0, 0, tiled=True, axis_index_groups=groups)]
    all_to_all x1, starting transfers between devices: 6.23 us -> 7.62 us  [shards(): mine = lax.all_to_all(totals, 'dom', 0, 0, tiled=True)]
    ppermute x1, waiting for transfers between devices: 0.01 us -> 1.36 us  [shards(): swapped = lax.ppermute(away, 'dom', pairs)]
    all_to_all x1, starting transfers between devices: 17.4 us -> 16.4 us  [shards(): lax.all_to_all(pieces, 'dom', 0, 0, tiled=True, axis_index_groups=groups)]
    ppermute x1, starting transfers between devices: 2.8 us -> 3.74 us  [shards(): back_b = lax.ppermute(back_b, 'dom', edges)]
    pallas_call x2 -> x3, Pallas kernels: 2.67 us -> 3.04 us  [the longest x1 1.39 us: shards(): call(finish, (shape((512, 128), F32),) * 3, [VMEM], [pltpu.VMEM((64, 2, 4...]
  transfers between devices with their start and end apart: 10 -> 10, of which waited for: 6 -> 6; matrix products, arithmetic and copies ran while one was open for 0% -> 0% of each run, Pallas kernels for 4% -> 5%
where the time goes in v5:
time: 88.1 us; the launch traced here: 87.5 us
  starting transfers between devices  52.4 us (59%)
  waiting for transfers between devices  21.7 us (25%)
  Pallas kernels  11.1 us (13%)
  local copies, waits for them, and re-layouts  1.56 us (2%)
    all_to_all x1, starting transfers between devices, shards(): lax.all_to_all(pieces, 'dom', 0, 0, tiled=True, axis_index_groups=groups)  16.4 us
    all_to_all x1, waiting for transfers between devices, shards(): lax.all_to_all(pieces, 'dom', 0, 0, tiled=True, axis_index_groups=groups)  8.54 us
    ppermute x3, starting transfers between devices, shards(): lax.ppermute(v, 'mp', [(i, (i + s) % members) for i in range(members)])  8.42 us
    all_to_all x1, starting transfers between devices, shards(): mine = lax.all_to_all(totals, 'dom', 0, 0, tiled=True)  7.62 us
    all_to_all x1, waiting for transfers between devices, shards(): mine = lax.all_to_all(totals, 'dom', 0, 0, tiled=True)  5.39 us
    ppermute x1, starting transfers between devices, shards(): xb = lax.ppermute(gathered, 'dom', edges)  5.18 us
    all_to_all x1, starting transfers between devices, shards(): gathered = lax.all_to_all(copies, 'mp', 0, 0, tiled=True)  4.97 us
    ppermute x1, starting transfers between devices, shards(): xa = lax.ppermute(gathered, 'dom', pairs)  3.96 us
  transfers between devices with their start and end apart: 10, of which 6 were waited for; matrix products, arithmetic and copies ran while one was open for 0% of the time, Pallas kernels for 5%

profile of v5, /device:TPU:1, one launch (start us, length us, event | category | flops | bytes accessed | tf_op | source)
XLA Modules:
  0.0 87.5 jit_solution(17224045302409291977)
XLA Ops:
  0.6 0.8 copy-done
  1.5 0.7 shard_map.119
  2.2 5.0 %all-to-all-start = ((bf16[4,256,128]{2,1,0:T(8,128)(2,1)}), bf16[4,256,128]{2,1,0:T(8,128)(2,1)S(1)}, u32[]{:S(2)}, u32[]{:S(2)}) async-start(bf16[4,256,128]{2,1,0:T(8,128)(2,1)} %shard_map.119), calls=%async_computation | async-start | bytes 524288 | tf_op jit(solution)/shard_map/all_to_all | solution.py:357
  7.2 0.0 copy-start.5
  7.2 0.7 copy-done.5
  7.9 0.0 copy-start.6
  7.9 1.4 %shard_map.120.count_ref = bf16[256,512]{1,0:T(8,128)(2,1)S(1)} custom-call(s32[1]{0:T(128)} %bitcast.part_ref, s32[2,8]{1,0:T(2,128)S(1)} %copy-done.5, s32[2,9,1024]{2,1,0:T(8,128)S(1)} %copy.13.words_ref), custom_call_target="tpu_custom_call" | custom-call | flops 2000000000 | bytes 400000 | tf_op jit(solution)/shard_map/pallas_call | solution.py:360
  9.4 3.4 %all-to-all-done.x_ref = bf16[4,256,128]{2,1,0:T(8,128)(2,1)S(1)} async-done(((bf16[4,256,128]{2,1,0:T(8,128)(2,1)}), bf16[4,256,128]{2,1,0:T(8,128)(2,1)S(1)}, u32[]{:S(2)}, u32[]{:S(2)}) %all-to-all-start) | async-done | bytes 262176 | tf_op jit(solution)/shard_map/all_to_all | solution.py:357
  12.7 5.2 %collective-permute-start.1 = (bf16[4,256,128]{2,1,0:T(8,128)(2,1)S(1)}, bf16[4,256,128]{2,1,0:T(8,128)(2,1)S(1)}, u32[]{:S(2)}, u32[]{:S(2)}) collective-permute-start(bf16[4,256,128]{2,1,0:T(8,128)(2,1)S(1)} %all-to-all-done.x_ref), channel_id=1, source_target_pairs={{4,8},{12,16},{20,24},{28,32},{36,40},{44,48},{52,56},{60,64},{68,... | collective-permute-start | bytes 786440 | tf_op jit(solution)/shard_map/ppermute | solution.py:371
  17.9 4.0 %collective-permute-start = (bf16[4,256,128]{2,1,0:T(8,128)(2,1)S(1)}, bf16[4,256,128]{2,1,0:T(8,128)(2,1)S(1)}, u32[]{:S(2)}, u32[]{:S(2)}) collective-permute-start(bf16[4,256,128]{2,1,0:T(8,128)(2,1)S(1)} %all-to-all-done.x_ref), channel_id=1, source_target_pairs={{0,4},{4,0},{8,12},{12,8},{16,20},{20,16},{24,28},{28,24},{32,36},... | collective-permute-start | bytes 786440 | tf_op jit(solution)/shard_map/ppermute | solution.py:370
  21.9 1.3 %shard_map.121 = (f32[256,128]{1,0:T(8,128)S(1)}, f32[256,128]{1,0:T(8,128)S(1)}, f32[256,128]{1,0:T(8,128)S(1)}, f32[256,128]{1,0:T(8,128)S(1)}, bf16[256,128]{...) custom-call(f32[2]{0:T(128)S(1)} %copy-done.6, ...), custom_call_target="tpu_custom_call" | custom-call | flops 3000000000 | bytes 3000000 | tf_op jit(solution)/shard_map/pallas_call | solution.py:374
  23.2 0.0 collective-permute-done.1.xb_ref
  23.2 0.0 collective-permute-done.xa_ref
  23.2 3.5 %shard_map.122 = (bf16[256,128]{1,0:T(8,128)(2,1)}, bf16[256,128]{1,0:T(8,128)(2,1)S(1)}, f32[256,256]{1,0:T(8,128)S(1)}, bf16[144,256]{1,0:T(8,128)(2,1)S(1)}, ...) custom-call(s32[1]{0:T(128)} %bitcast.part_ref, s32[2,8]{1,0:T(2,128)S(1)} %copy-done.5, f32[2]{0:T(128)S(1)} %copy-done.6, ...), custom_call_target="tpu_custom_call" | custom-call | flops 3000000000 | bytes 4000000 | tf_op jit(solution)/shard_map/pallas_call | solution.py:382
  26.7 2.1 %collective-permute-start.2 = (bf16[65,4,512]{2,1,0:T(4,128)(2,1)S(1)}, bf16[65,4,512]{2,1,0:T(4,128)(2,1)S(1)}, u32[]{:S(2)}, u32[]{:S(2)}) collective-permute-start(bf16[65,4,512]{2,1,0:T(4,128)(2,1)S(1)} %get-tuple-element.43), channel_id=1, source_target_pairs={{0,4},{4,0},{8,12},{12,8},{16,20},{20,16},{24,28},{28,24},{32,36},... | collective-permute-start | bytes 798728 | tf_op jit(solution)/shard_map/ppermute | solution.py:407
  28.7 1.4 %collective-permute-done.2.swapped_ref = bf16[65,4,512]{2,1,0:T(4,128)(2,1)S(1)} collective-permute-done((bf16[65,4,512]{2,1,0:T(4,128)(2,1)S(1)}, bf16[65,4,512]{2,1,0:T(4,128)(2,1)S(1)}, u32[]{:S(2)}, u32[]{:S(2)}) %collective-permute-start.2) | collective-permute-done | bytes 266272 | tf_op jit(solution)/shard_map/ppermute | solution.py:407
  30.1 0.8 shard_map.123
  30.9 16.4 %all-to-all-start.1 = ((bf16[64,4,384]{2,1,0:T(4,128)(2,1)}), bf16[64,4,384]{2,1,0:T(4,128)(2,1)S(1)}, u32[]{:S(2)}, u32[]{:S(2)}) async-start(bf16[64,4,384]{2,1,0:T(4,128)(2,1)} %shard_map.123), calls=%async_computation.1 | async-start | bytes 393216 | tf_op jit(solution)/shard_map/all_to_all | solution.py:413
  47.3 3.7 %collective-permute-start.3 = (bf16[144,256]{1,0:T(8,128)(2,1)S(1)}, bf16[144,256]{1,0:T(8,128)(2,1)S(1)}, u32[]{:S(2)}, u32[]{:S(2)}) collective-permute-start(bf16[144,256]{1,0:T(8,128)(2,1)S(1)} %get-tuple-element.46), channel_id=1, source_target_pairs={{4,8},{12,16},{20,24},{28,32},{36,40},{44,48},{52,56},{60,64},{68,... | collective-permute-start | bytes 221192 | tf_op jit(solution)/shard_map/ppermute | solution.py:408
  51.1 8.5 %all-to-all-done.1.got_ref = bf16[64,4,384]{2,1,0:T(4,128)(2,1)S(1)} async-done(((bf16[64,4,384]{2,1,0:T(4,128)(2,1)}), bf16[64,4,384]{2,1,0:T(4,128)(2,1)S(1)}, u32[]{:S(2)}, u32[]{:S(2)}) %all-to-all-start.1) | async-done | bytes 196640 | tf_op jit(solution)/shard_map/all_to_all | solution.py:413
  59.6 0.9 %shard_map.124 = bf16[128,4,384]{2,1,0:T(4,128)(2,1)} custom-call(bf16[64,4,384]{2,1,0:T(4,128)(2,1)S(1)} %all-to-all-done.1.got_ref), custom_call_target="tpu_custom_call" | custom-call | bytes 500000 | tf_op jit(solution)/shard_map/pallas_call | solution.py:414
  60.5 7.6 %all-to-all-start.2 = ((bf16[128,4,384]{2,1,0:T(4,128)(2,1)}), bf16[128,4,384]{2,1,0:T(4,128)(2,1)S(1)}, u32[]{:S(2)}, u32[]{:S(2)}) async-start(bf16[128,4,384]{2,1,0:T(4,128)(2,1)} %shard_map.124), calls=%async_computation.2 | async-start | bytes 786432 | tf_op jit(solution)/shard_map/all_to_all | solution.py:431
  68.1 0.0 collective-permute-done.3.back_b_ref
  68.1 0.5 shard_map.125
  68.6 2.2 %collective-permute-start.4 = (bf16[256,128]{1,0:T(8,128)(2,1)S(1)}, bf16[256,128]{1,0:T(8,128)(2,1)S(1)}, u32[]{:S(2)}, u32[]{:S(2)}) collective-permute-start(bf16[256,128]{1,0:T(8,128)(2,1)S(1)} %get-tuple-element.48), channel_id=1, source_target_pairs={{0,1},{1,2},{2,3},{3,0},{4,5},{5,6},{6,7},{7,4},{8,9},{9,10},{10,1... | collective-permute-start | bytes 196616 | tf_op jit(solution)/shard_map/ppermute | solution.py:425
  70.8 3.7 %collective-permute-start.5 = (bf16[256,128]{1,0:T(8,128)(2,1)S(1)}, bf16[256,128]{1,0:T(8,128)(2,1)S(1)}, u32[]{:S(2)}, u32[]{:S(2)}) collective-permute-start(bf16[256,128]{1,0:T(8,128)(2,1)S(1)} %get-tuple-element.49), channel_id=1, source_target_pairs={{0,2},{1,3},{2,0},{3,1},{4,6},{5,7},{6,4},{7,5},{8,10},{9,11},{10,... | collective-permute-start | bytes 196616 | tf_op jit(solution)/shard_map/ppermute | solution.py:425
  74.5 2.5 %collective-permute-start.6 = (bf16[256,128]{1,0:T(8,128)(2,1)S(1)}, bf16[256,128]{1,0:T(8,128)(2,1)S(1)}, u32[]{:S(2)}, u32[]{:S(2)}) collective-permute-start(bf16[256,128]{1,0:T(8,128)(2,1)S(1)} %get-tuple-element.50), channel_id=1, source_target_pairs={{0,3},{1,0},{2,1},{3,2},{4,7},{5,4},{6,5},{7,6},{8,11},{9,8},{10,9... | collective-permute-start | bytes 196616 | tf_op jit(solution)/shard_map/ppermute | solution.py:425
  77.1 0.6 collective-permute-done.5.two_ref
  77.6 2.4 %collective-permute-done.6.three_ref = bf16[256,128]{1,0:T(8,128)(2,1)S(1)} collective-permute-done((bf16[256,128]{1,0:T(8,128)(2,1)S(1)}, bf16[256,128]{1,0:T(8,128)(2,1)S(1)}, u32[]{:S(2)}, u32[]{:S(2)}) %collective-permute-start.6) | collective-permute-done | bytes 65568 | tf_op jit(solution)/shard_map/ppermute | solution.py:425
  80.1 0.7 shard_map.126
  80.7 5.4 %all-to-all-done.2 = bf16[128,4,384]{2,1,0:T(4,128)(2,1)S(1)} async-done(((bf16[128,4,384]{2,1,0:T(4,128)(2,1)}), bf16[128,4,384]{2,1,0:T(4,128)(2,1)S(1)}, u32[]{:S(2)}, u32[]{:S(2)}) %all-to-all-start.2) | async-done | bytes 393248 | tf_op jit(solution)/shard_map/all_to_all | solution.py:431
  86.1 1.4 %shard_map.127 = (f32[512,128]{1,0:T(8,128)}, f32[512,128]{1,0:T(8,128)}, f32[512,128]{1,0:T(8,128)}) custom-call(bf16[64,2,4,384]{3,2,1,0:T(4,128)(2,1)S(1)} %bitcast.3), custom_call_target="tpu_custom_call" | custom-call | bytes 1500000 | tf_op jit(solution)/shard_map/pallas_call | solution.py:437
  (14 shorter events, 0.1 us)
Async XLA Ops:
  0.6 0.8 copy-start
  2.2 5.0 %copy-start.7 = (s32[2,9,1024]{2,0,1:T(2,128)S(1)}, s32[2,9,1024]{2,0,1:T(2,128)}, u32[]{:S(2)}) copy-start(s32[2,9,1024]{2,0,1:T(2,128)} %param.15) | copy-start | bytes 221188
  2.2 10.5 %all-to-all-start = ((bf16[4,256,128]{2,1,0:T(8,128)(2,1)}), bf16[4,256,128]{2,1,0:T(8,128)(2,1)S(1)}, u32[]{:S(2)}, u32[]{:S(2)}) async-start(bf16[4,256,128]{2,1,0:T(8,128)(2,1)} %shard_map.119), calls=%async_computation | async-start | bytes 524288 | tf_op jit(solution)/shard_map/all_to_all | solution.py:357
  7.2 0.7 copy-start.5
  7.9 14.0 %copy-start.1 = (bf16[512,128]{1,0:T(8,128)(2,1)S(1)}, bf16[512,128]{1,0:T(8,128)(2,1)}, u32[]{:S(2)}) copy-start(bf16[512,128]{1,0:T(8,128)(2,1)} %wk_ref.5) | copy-start | bytes 393220
  7.9 14.0 %copy-start.2 = (bf16[512,128]{1,0:T(8,128)(2,1)S(1)}, bf16[512,128]{1,0:T(8,128)(2,1)}, u32[]{:S(2)}) copy-start(bf16[512,128]{1,0:T(8,128)(2,1)} %wv_ref.5) | copy-start | bytes 393220
  7.9 14.0 %copy-start.3 = (bf16[512,128]{1,0:T(8,128)(2,1)S(1)}, bf16[512,128]{1,0:T(8,128)(2,1)}, u32[]{:S(2)}) copy-start(bf16[512,128]{1,0:T(8,128)(2,1)} %wq_ref.3) | copy-start | bytes 393220
  7.9 14.0 %copy-start.4 = (bf16[256,128]{1,0:T(8,128)(2,1)S(1)}, bf16[256,128]{1,0:T(8,128)(2,1)}, u32[]{:S(2)}) copy-start(bf16[256,128]{1,0:T(8,128)(2,1)} %up_ref.3) | copy-start | bytes 196612
  7.9 14.0 %copy-start.6 = (f32[2]{0:T(128)S(1)}, f32[2]{0:T(128)}, u32[]{:S(2)}) copy-start(f32[2]{0:T(128)} %scale_ref.3) | copy-start | bytes 28
  12.7 10.5 %collective-permute-start.1 = (bf16[4,256,128]{2,1,0:T(8,128)(2,1)S(1)}, bf16[4,256,128]{2,1,0:T(8,128)(2,1)S(1)}, u32[]{:S(2)}, u32[]{:S(2)}) collective-permute-start(bf16[4,256,128]{2,1,0:T(8,128)(2,1)S(1)} %all-to-all-done.x_ref), channel_id=1, source_target_pairs={{4,8},{12,16},{20,24},{28,32},{36,40},{44,48},{52,56},{60,64},{68,... | collective-permute-start | bytes 786440 | tf_op jit(solution)/shard_map/ppermute | solution.py:371
  17.9 5.3 %collective-permute-start = (bf16[4,256,128]{2,1,0:T(8,128)(2,1)S(1)}, bf16[4,256,128]{2,1,0:T(8,128)(2,1)S(1)}, u32[]{:S(2)}, u32[]{:S(2)}) collective-permute-start(bf16[4,256,128]{2,1,0:T(8,128)(2,1)S(1)} %all-to-all-done.x_ref), channel_id=1, source_target_pairs={{0,4},{4,0},{8,12},{12,8},{16,20},{20,16},{24,28},{28,24},{32,36},... | collective-permute-start | bytes 786440 | tf_op jit(solution)/shard_map/ppermute | solution.py:370
  26.7 3.4 %collective-permute-start.2 = (bf16[65,4,512]{2,1,0:T(4,128)(2,1)S(1)}, bf16[65,4,512]{2,1,0:T(4,128)(2,1)S(1)}, u32[]{:S(2)}, u32[]{:S(2)}) collective-permute-start(bf16[65,4,512]{2,1,0:T(4,128)(2,1)S(1)} %get-tuple-element.43), channel_id=1, source_target_pairs={{0,4},{4,0},{8,12},{12,8},{16,20},{20,16},{24,28},{28,24},{32,36},... | collective-permute-start | bytes 798728 | tf_op jit(solution)/shard_map/ppermute | solution.py:407
  30.9 28.7 %all-to-all-start.1 = ((bf16[64,4,384]{2,1,0:T(4,128)(2,1)}), bf16[64,4,384]{2,1,0:T(4,128)(2,1)S(1)}, u32[]{:S(2)}, u32[]{:S(2)}) async-start(bf16[64,4,384]{2,1,0:T(4,128)(2,1)} %shard_map.123), calls=%async_computation.1 | async-start | bytes 393216 | tf_op jit(solution)/shard_map/all_to_all | solution.py:413
  47.3 20.8 %collective-permute-start.3 = (bf16[144,256]{1,0:T(8,128)(2,1)S(1)}, bf16[144,256]{1,0:T(8,128)(2,1)S(1)}, u32[]{:S(2)}, u32[]{:S(2)}) collective-permute-start(bf16[144,256]{1,0:T(8,128)(2,1)S(1)} %get-tuple-element.46), channel_id=1, source_target_pairs={{4,8},{12,16},{20,24},{28,32},{36,40},{44,48},{52,56},{60,64},{68,... | collective-permute-start | bytes 221192 | tf_op jit(solution)/shard_map/ppermute | solution.py:408
  60.5 25.6 %all-to-all-start.2 = ((bf16[128,4,384]{2,1,0:T(4,128)(2,1)}), bf16[128,4,384]{2,1,0:T(4,128)(2,1)S(1)}, u32[]{:S(2)}, u32[]{:S(2)}) async-start(bf16[128,4,384]{2,1,0:T(4,128)(2,1)} %shard_map.124), calls=%async_computation.2 | async-start | bytes 786432 | tf_op jit(solution)/shard_map/all_to_all | solution.py:431
  68.6 8.4 %collective-permute-start.4 = (bf16[256,128]{1,0:T(8,128)(2,1)S(1)}, bf16[256,128]{1,0:T(8,128)(2,1)S(1)}, u32[]{:S(2)}, u32[]{:S(2)}) collective-permute-start(bf16[256,128]{1,0:T(8,128)(2,1)S(1)} %get-tuple-element.48), channel_id=1, source_target_pairs={{0,1},{1,2},{2,3},{3,0},{4,5},{5,6},{6,7},{7,4},{8,9},{9,10},{10,1... | collective-permute-start | bytes 196616 | tf_op jit(solution)/shard_map/ppermute | solution.py:425
  70.8 6.8 %collective-permute-start.5 = (bf16[256,128]{1,0:T(8,128)(2,1)S(1)}, bf16[256,128]{1,0:T(8,128)(2,1)S(1)}, u32[]{:S(2)}, u32[]{:S(2)}) collective-permute-start(bf16[256,128]{1,0:T(8,128)(2,1)S(1)} %get-tuple-element.49), channel_id=1, source_target_pairs={{0,2},{1,3},{2,0},{3,1},{4,6},{5,7},{6,4},{7,5},{8,10},{9,11},{10,... | collective-permute-start | bytes 196616 | tf_op jit(solution)/shard_map/ppermute | solution.py:425
  74.5 5.6 %collective-permute-start.6 = (bf16[256,128]{1,0:T(8,128)(2,1)S(1)}, bf16[256,128]{1,0:T(8,128)(2,1)S(1)}, u32[]{:S(2)}, u32[]{:S(2)}) collective-permute-start(bf16[256,128]{1,0:T(8,128)(2,1)S(1)} %get-tuple-element.50), channel_id=1, source_target_pairs={{0,3},{1,0},{2,1},{3,2},{4,7},{5,4},{6,5},{7,6},{8,11},{9,8},{10,9... | collective-permute-start | bytes 196616 | tf_op jit(solution)/shard_map/ppermute | solution.py:425

commit v6 on v5

--- a/solution.py
+++ b/solution.py
@@ -243,10 +243,9 @@
     g_near = jnp.concatenate([gk_round[2 * n :], gv_round[2 * n :]], axis=1)
     dw[...] = mul(xt_ref[...], g_own)
     dw[:, n:] += mul(x_near[...], g_near, TN)
-    for i in range(4):
-        for ref, half in ((keep_ref, core), (wide, 1 - core)):
-            rows = pl.ds(pl.multiple_of(half * 2 * n + i * 64, 64), 64)
-            ref[0:64, i, : 3 * n] = dw[rows, :]
+    for ref, half in ((keep_ref, core), (wide, 1 - core)):
+        rows = pl.ds(pl.multiple_of(half * 2 * n, 2 * n), 2 * n)
+        ref[0:64, :, : 3 * n] = dw[rows, :].reshape(64, 4, 3 * n)
     wide[64] = jnp.full((4, 4 * n), jnp.where(core == 0, after, before), jnp.int32).astype(F32)
     back_b_ref[n:] = (
         jnp.full((16, 2 * n), jnp.where(core == 0, before, after), jnp.int32)
@@ -255,9 +254,8 @@
     )
 
     def put_sides(near, other):
-        for i in range(2):
-            wide[0:64, i, 3 * n :] = gk[near + 64 * i : near + 64 * (i + 1)]
-            wide[0:64, 2 + i, 3 * n :] = gv[near + 64 * i : near + 64 * (i + 1)]
+        wide[0:32, :, 3 * n :] = gk[near : near + n].reshape(32, 4, n)
+        wide[32:64, :, 3 * n :] = gv[near : near + n].reshape(32, 4, n)
         back_b_ref[:n, :n] = gk_round[other : other + n]
         back_b_ref[:n, n:] = gv_round[other : other + n]
 
@@ -291,10 +289,7 @@
     n = LANES
     wide[...] = swapped_ref[:, :, 3 * n :].astype(F32)
     near = jnp.concatenate(
-        [
-            jnp.concatenate([wide[0:64, i, :], wide[0:64, i + 1, :]], axis=0) for i in (0, 2)
-        ],
-        axis=1,
+        [wide[0:32].reshape(n, n), wide[32:64].reshape(n, n)], axis=1
     )
     which = wide[64][:1]
     which = jnp.concatenate([which, which], axis=1)
@@ -329,20 +324,28 @@
     out_ref[...] = jnp.broadcast_to(total[None], out_ref.shape)
 
 
-def add_kernel(own_ref, one_ref, two_ref, three_ref, out_ref):
+def final_kernel(
+    grad_scale,
+    mine_ref,
+    own_ref,
+    one_ref,
+    two_ref,
+    three_ref,
+    gq_ref,
+    gk_ref,
+    gv_ref,
+    input_ref,
+    wide,
+):
+    n = LANES
     total = own_ref[...] + one_ref[...].astype(F32)
     total = total + two_ref[...].astype(F32) + three_ref[...].astype(F32)
-    out_ref[...] = total.astype(BF16)
-
-
-def final_kernel(grad_scale, mine_ref, gq_ref, gk_ref, gv_ref, wide):
-    n = LANES
+    input_ref[...] = total.astype(BF16)
     wide[...] = mine_ref[...].astype(F32) * grad_scale
     for half in range(2):
-        for i in range(4):
-            rows = slice(half * 256 + i * 64, half * 256 + (i + 1) * 64)
-            for j, out in enumerate((gq_ref, gk_ref, gv_ref)):
-                out[rows, :] = wide[:, half, i, j * n : (j + 1) * n]
+        for j, out in enumerate((gq_ref, gk_ref, gv_ref)):
+            rows = slice(half * 2 * n, (half + 1) * 2 * n)
+            out[rows, :] = wide[:, half, :, j * n : (j + 1) * n].reshape(2 * n, n)
 
 
 def shards(x, up, wq, wk, wv, scales, table, bitmap):
@@ -425,22 +428,20 @@
         lax.ppermute(v, "mp", [(i, (i + s) % members) for i in range(members)])
         for s, v in ((1, one), (2, two), (3, three))
     )
-    input_grad = call(
-        add_kernel, shape((256, 128), BF16), [VMEM] * 4, moved=400_000
-    )(own, one, two, three)
     mine = lax.all_to_all(totals, "dom", 0, 0, tiled=True)
+    mine, one, two, three = lax.optimization_barrier((mine, one, two, three))
     grad_scale = float(parts * 256) ** -0.5
 
     def finish(*refs):
         final_kernel(grad_scale, *refs)
 
-    grads = call(
+    *grads, input_grad = call(
         finish,
-        (shape((512, 128), F32),) * 3,
-        [VMEM],
+        (shape((512, 128), F32),) * 3 + (shape((256, 128), BF16),),
+        [VMEM] * 5,
         [pltpu.VMEM((64, 2, 4, 384), F32)],
         moved=1_500_000,
-    )(mine.reshape(64, 2, 4, 384))
+    )(mine.reshape(64, 2, 4, 384), own, one, two, three)
     return (att, input_grad) + tuple(grads)
 
 

time: 88.1 us -> 87.5 us (level)
  Pallas kernels: 11.1 us -> 9.87 us
    pallas_call x2 -> x1, Pallas kernels: 2.05 us -> 1.03 us  [shards(): call(finish, (shape((512, 128), F32),) * 3 + (shape((256, 128), BF16),),...]
where the time goes in v6:
time: 87.5 us; the launch traced here: 87 us
  starting transfers between devices  52.3 us (60%)
  waiting for transfers between devices  22.4 us (26%)
  Pallas kernels  9.87 us (11%)
  local copies, waits for them, and re-layouts  1.56 us (2%)
    all_to_all x1, starting transfers between devices, shards(): lax.all_to_all(pieces, 'dom', 0, 0, tiled=True, axis_index_groups=groups)  16.4 us
    all_to_all x1, waiting for transfers between devices, shards(): lax.all_to_all(pieces, 'dom', 0, 0, tiled=True, axis_index_groups=groups)  8.54 us
    ppermute x3, starting transfers between devices, shards(): lax.ppermute(v, 'mp', [(i, (i + s) % members) for i in range(members)])  8.41 us
    all_to_all x1, starting transfers between devices, shards(): mine = lax.all_to_all(totals, 'dom', 0, 0, tiled=True)  7.62 us
    all_to_all x1, waiting for transfers between devices, shards(): mine = lax.all_to_all(totals, 'dom', 0, 0, tiled=True)  6.08 us
    ppermute x1, starting transfers between devices, shards(): xb = lax.ppermute(gathered, 'dom', edges)  5.18 us
    all_to_all x1, starting transfers between devices, shards(): gathered = lax.all_to_all(copies, 'mp', 0, 0, tiled=True)  4.97 us
    ppermute x1, starting transfers between devices, shards(): xa = lax.ppermute(gathered, 'dom', pairs)  3.96 us
  transfers between devices with their start and end apart: 10, of which 6 were waited for; matrix products, arithmetic and copies ran while one was open for 0% of the time, Pallas kernels for 5%

profile of v6, /device:TPU:1, one launch (start us, length us, event | category | flops | bytes accessed | tf_op | source)
XLA Modules:
  0.0 87.0 jit_solution(18182075960771579907)
XLA Ops:
  0.6 0.8 copy-done
  1.5 0.7 shard_map.119
  2.2 5.0 %all-to-all-start = ((bf16[4,256,128]{2,1,0:T(8,128)(2,1)}), bf16[4,256,128]{2,1,0:T(8,128)(2,1)S(1)}, u32[]{:S(2)}, u32[]{:S(2)}) async-start(bf16[4,256,128]{2,1,0:T(8,128)(2,1)} %shard_map.119), calls=%async_computation | async-start | bytes 524288 | tf_op jit(solution)/shard_map/all_to_all | solution.py:360
  7.2 0.0 copy-start.5
  7.2 0.7 copy-done.5
  7.9 0.0 copy-start.6
  7.9 1.4 %shard_map.120.count_ref = bf16[256,512]{1,0:T(8,128)(2,1)S(1)} custom-call(s32[1]{0:T(128)} %bitcast.part_ref, s32[2,8]{1,0:T(2,128)S(1)} %copy-done.5, s32[2,9,1024]{2,1,0:T(8,128)S(1)} %copy.13.words_ref), custom_call_target="tpu_custom_call" | custom-call | flops 2000000000 | bytes 400000 | tf_op jit(solution)/shard_map/pallas_call | solution.py:363
  9.4 3.4 %all-to-all-done.x_ref = bf16[4,256,128]{2,1,0:T(8,128)(2,1)S(1)} async-done(((bf16[4,256,128]{2,1,0:T(8,128)(2,1)}), bf16[4,256,128]{2,1,0:T(8,128)(2,1)S(1)}, u32[]{:S(2)}, u32[]{:S(2)}) %all-to-all-start) | async-done | bytes 262176 | tf_op jit(solution)/shard_map/all_to_all | solution.py:360
  12.7 5.2 %collective-permute-start.1 = (bf16[4,256,128]{2,1,0:T(8,128)(2,1)S(1)}, bf16[4,256,128]{2,1,0:T(8,128)(2,1)S(1)}, u32[]{:S(2)}, u32[]{:S(2)}) collective-permute-start(bf16[4,256,128]{2,1,0:T(8,128)(2,1)S(1)} %all-to-all-done.x_ref), channel_id=1, source_target_pairs={{4,8},{12,16},{20,24},{28,32},{36,40},{44,48},{52,56},{60,64},{68,... | collective-permute-start | bytes 786440 | tf_op jit(solution)/shard_map/ppermute | solution.py:374
  17.9 4.0 %collective-permute-start = (bf16[4,256,128]{2,1,0:T(8,128)(2,1)S(1)}, bf16[4,256,128]{2,1,0:T(8,128)(2,1)S(1)}, u32[]{:S(2)}, u32[]{:S(2)}) collective-permute-start(bf16[4,256,128]{2,1,0:T(8,128)(2,1)S(1)} %all-to-all-done.x_ref), channel_id=1, source_target_pairs={{0,4},{4,0},{8,12},{12,8},{16,20},{20,16},{24,28},{28,24},{32,36},... | collective-permute-start | bytes 786440 | tf_op jit(solution)/shard_map/ppermute | solution.py:373
  21.9 1.3 %shard_map.121 = (f32[256,128]{1,0:T(8,128)S(1)}, f32[256,128]{1,0:T(8,128)S(1)}, f32[256,128]{1,0:T(8,128)S(1)}, f32[256,128]{1,0:T(8,128)S(1)}, bf16[256,128]{...) custom-call(f32[2]{0:T(128)S(1)} %copy-done.6, ...), custom_call_target="tpu_custom_call" | custom-call | flops 3000000000 | bytes 3000000 | tf_op jit(solution)/shard_map/pallas_call | solution.py:377
  23.2 0.0 collective-permute-done.1.xb_ref
  23.2 0.0 collective-permute-done.xa_ref
  23.2 3.3 %shard_map.122 = (bf16[256,128]{1,0:T(8,128)(2,1)}, bf16[256,128]{1,0:T(8,128)(2,1)S(1)}, f32[256,256]{1,0:T(8,128)S(1)}, bf16[144,256]{1,0:T(8,128)(2,1)S(1)}, ...) custom-call(s32[1]{0:T(128)} %bitcast.part_ref, s32[2,8]{1,0:T(2,128)S(1)} %copy-done.5, f32[2]{0:T(128)S(1)} %copy-done.6, ...), custom_call_target="tpu_custom_call" | custom-call | flops 3000000000 | bytes 4000000 | tf_op jit(solution)/shard_map/pallas_call | solution.py:385
  26.5 2.0 %collective-permute-start.2 = (bf16[65,4,512]{2,1,0:T(4,128)(2,1)S(1)}, bf16[65,4,512]{2,1,0:T(4,128)(2,1)S(1)}, u32[]{:S(2)}, u32[]{:S(2)}) collective-permute-start(bf16[65,4,512]{2,1,0:T(4,128)(2,1)S(1)} %get-tuple-element.47), channel_id=1, source_target_pairs={{0,4},{4,0},{8,12},{12,8},{16,20},{20,16},{24,28},{28,24},{32,36},... | collective-permute-start | bytes 798728 | tf_op jit(solution)/shard_map/ppermute | solution.py:410
  28.6 1.4 %collective-permute-done.2.swapped_ref = bf16[65,4,512]{2,1,0:T(4,128)(2,1)S(1)} collective-permute-done((bf16[65,4,512]{2,1,0:T(4,128)(2,1)S(1)}, bf16[65,4,512]{2,1,0:T(4,128)(2,1)S(1)}, u32[]{:S(2)}, u32[]{:S(2)}) %collective-permute-start.2) | collective-permute-done | bytes 266272 | tf_op jit(solution)/shard_map/ppermute | solution.py:410
  30.0 0.8 shard_map.123
  30.7 16.4 %all-to-all-start.1 = ((bf16[64,4,384]{2,1,0:T(4,128)(2,1)}), bf16[64,4,384]{2,1,0:T(4,128)(2,1)S(1)}, u32[]{:S(2)}, u32[]{:S(2)}) async-start(bf16[64,4,384]{2,1,0:T(4,128)(2,1)} %shard_map.123), calls=%async_computation.1 | async-start | bytes 393216 | tf_op jit(solution)/shard_map/all_to_all | solution.py:416
  47.1 3.7 %collective-permute-start.3 = (bf16[144,256]{1,0:T(8,128)(2,1)S(1)}, bf16[144,256]{1,0:T(8,128)(2,1)S(1)}, u32[]{:S(2)}, u32[]{:S(2)}) collective-permute-start(bf16[144,256]{1,0:T(8,128)(2,1)S(1)} %get-tuple-element.52), channel_id=1, source_target_pairs={{4,8},{12,16},{20,24},{28,32},{36,40},{44,48},{52,56},{60,64},{68,... | collective-permute-start | bytes 221192 | tf_op jit(solution)/shard_map/ppermute | solution.py:411
  50.9 8.5 %all-to-all-done.1.got_ref = bf16[64,4,384]{2,1,0:T(4,128)(2,1)S(1)} async-done(((bf16[64,4,384]{2,1,0:T(4,128)(2,1)}), bf16[64,4,384]{2,1,0:T(4,128)(2,1)S(1)}, u32[]{:S(2)}, u32[]{:S(2)}) %all-to-all-start.1) | async-done | bytes 196640 | tf_op jit(solution)/shard_map/all_to_all | solution.py:416
  59.4 0.9 %shard_map.124 = bf16[128,4,384]{2,1,0:T(4,128)(2,1)} custom-call(bf16[64,4,384]{2,1,0:T(4,128)(2,1)S(1)} %all-to-all-done.1.got_ref), custom_call_target="tpu_custom_call" | custom-call | bytes 500000 | tf_op jit(solution)/shard_map/pallas_call | solution.py:417
  60.3 7.6 %all-to-all-start.2 = ((bf16[128,4,384]{2,1,0:T(4,128)(2,1)}), bf16[128,4,384]{2,1,0:T(4,128)(2,1)S(1)}, u32[]{:S(2)}, u32[]{:S(2)}) async-start(bf16[128,4,384]{2,1,0:T(4,128)(2,1)} %shard_map.124), calls=%async_computation.2 | async-start | bytes 786432 | tf_op jit(solution)/shard_map/all_to_all | solution.py:431
  67.9 0.0 collective-permute-done.3.back_b_ref
  67.9 0.5 shard_map.125
  68.4 2.2 %collective-permute-start.4 = (bf16[256,128]{1,0:T(8,128)(2,1)S(1)}, bf16[256,128]{1,0:T(8,128)(2,1)S(1)}, u32[]{:S(2)}, u32[]{:S(2)}) collective-permute-start(bf16[256,128]{1,0:T(8,128)(2,1)S(1)} %get-tuple-element.53), channel_id=1, source_target_pairs={{0,1},{1,2},{2,3},{3,0},{4,5},{5,6},{6,7},{7,4},{8,9},{9,10},{10,1... | collective-permute-start | bytes 196616 | tf_op jit(solution)/shard_map/ppermute | solution.py:428
  70.6 3.7 %collective-permute-start.5 = (bf16[256,128]{1,0:T(8,128)(2,1)S(1)}, bf16[256,128]{1,0:T(8,128)(2,1)S(1)}, u32[]{:S(2)}, u32[]{:S(2)}) collective-permute-start(bf16[256,128]{1,0:T(8,128)(2,1)S(1)} %get-tuple-element.54), channel_id=1, source_target_pairs={{0,2},{1,3},{2,0},{3,1},{4,6},{5,7},{6,4},{7,5},{8,10},{9,11},{10,... | collective-permute-start | bytes 196616 | tf_op jit(solution)/shard_map/ppermute | solution.py:428
  74.3 2.5 %collective-permute-start.6 = (bf16[256,128]{1,0:T(8,128)(2,1)S(1)}, bf16[256,128]{1,0:T(8,128)(2,1)S(1)}, u32[]{:S(2)}, u32[]{:S(2)}) collective-permute-start(bf16[256,128]{1,0:T(8,128)(2,1)S(1)} %get-tuple-element.55), channel_id=1, source_target_pairs={{0,3},{1,0},{2,1},{3,2},{4,7},{5,4},{6,5},{7,6},{8,11},{9,8},{10,9... | collective-permute-start | bytes 196616 | tf_op jit(solution)/shard_map/ppermute | solution.py:428
  76.8 0.0 collective-permute-done.4.refs_2_
  76.9 0.6 collective-permute-done.5.refs_3_
  77.4 2.5 %collective-permute-done.6.refs_4_ = bf16[256,128]{1,0:T(8,128)(2,1)S(1)} collective-permute-done((bf16[256,128]{1,0:T(8,128)(2,1)S(1)}, bf16[256,128]{1,0:T(8,128)(2,1)S(1)}, u32[]{:S(2)}, u32[]{:S(2)}) %collective-permute-start.6) | collective-permute-done | bytes 65568 | tf_op jit(solution)/shard_map/ppermute | solution.py:428
  79.9 6.1 %all-to-all-done.2 = bf16[128,4,384]{2,1,0:T(4,128)(2,1)S(1)} async-done(((bf16[128,4,384]{2,1,0:T(4,128)(2,1)}), bf16[128,4,384]{2,1,0:T(4,128)(2,1)S(1)}, u32[]{:S(2)}, u32[]{:S(2)}) %all-to-all-start.2) | async-done | bytes 393248 | tf_op jit(solution)/shard_map/all_to_all | solution.py:431
  85.9 1.0 %shard_map.126 = (f32[512,128]{1,0:T(8,128)}, f32[512,128]{1,0:T(8,128)}, f32[512,128]{1,0:T(8,128)}, bf16[256,128]{1,0:T(8,128)(2,1)}) custom-call(bf16[64,2,4,384]{3,2,1,0:T(4,128)(2,1)S(1)} %bitcast.3, f32[256,128]{1,0:T(8,128)S(1)} %get-tuple-element.57.refs_1_, bf16[256,128]{1,0:T(8,128)(2,1)S(1)} %collective-permute-done.4.refs_2_, ...), custom_call_target="tpu_custom_call" | custom-call | bytes 1500000 | tf_op jit(solution)/shard_map/pallas_call | solution.py:438
  (13 shorter events, 0.1 us)
Async XLA Ops:
  0.6 0.8 copy-start
  2.2 5.0 %copy-start.7 = (s32[2,9,1024]{2,0,1:T(2,128)S(1)}, s32[2,9,1024]{2,0,1:T(2,128)}, u32[]{:S(2)}) copy-start(s32[2,9,1024]{2,0,1:T(2,128)} %param.15) | copy-start | bytes 221188
  2.2 10.5 %all-to-all-start = ((bf16[4,256,128]{2,1,0:T(8,128)(2,1)}), bf16[4,256,128]{2,1,0:T(8,128)(2,1)S(1)}, u32[]{:S(2)}, u32[]{:S(2)}) async-start(bf16[4,256,128]{2,1,0:T(8,128)(2,1)} %shard_map.119), calls=%async_computation | async-start | bytes 524288 | tf_op jit(solution)/shard_map/all_to_all | solution.py:360
  7.2 0.7 copy-start.5
  7.9 14.0 %copy-start.1 = (bf16[512,128]{1,0:T(8,128)(2,1)S(1)}, bf16[512,128]{1,0:T(8,128)(2,1)}, u32[]{:S(2)}) copy-start(bf16[512,128]{1,0:T(8,128)(2,1)} %wk_ref.5) | copy-start | bytes 393220
  7.9 14.0 %copy-start.2 = (bf16[512,128]{1,0:T(8,128)(2,1)S(1)}, bf16[512,128]{1,0:T(8,128)(2,1)}, u32[]{:S(2)}) copy-start(bf16[512,128]{1,0:T(8,128)(2,1)} %wv_ref.5) | copy-start | bytes 393220
  7.9 14.0 %copy-start.3 = (bf16[512,128]{1,0:T(8,128)(2,1)S(1)}, bf16[512,128]{1,0:T(8,128)(2,1)}, u32[]{:S(2)}) copy-start(bf16[512,128]{1,0:T(8,128)(2,1)} %wq_ref.3) | copy-start | bytes 393220
  7.9 14.0 %copy-start.4 = (bf16[256,128]{1,0:T(8,128)(2,1)S(1)}, bf16[256,128]{1,0:T(8,128)(2,1)}, u32[]{:S(2)}) copy-start(bf16[256,128]{1,0:T(8,128)(2,1)} %up_ref.3) | copy-start | bytes 196612
  7.9 14.0 %copy-start.6 = (f32[2]{0:T(128)S(1)}, f32[2]{0:T(128)}, u32[]{:S(2)}) copy-start(f32[2]{0:T(128)} %scale_ref.3) | copy-start | bytes 28
  12.7 10.5 %collective-permute-start.1 = (bf16[4,256,128]{2,1,0:T(8,128)(2,1)S(1)}, bf16[4,256,128]{2,1,0:T(8,128)(2,1)S(1)}, u32[]{:S(2)}, u32[]{:S(2)}) collective-permute-start(bf16[4,256,128]{2,1,0:T(8,128)(2,1)S(1)} %all-to-all-done.x_ref), channel_id=1, source_target_pairs={{4,8},{12,16},{20,24},{28,32},{36,40},{44,48},{52,56},{60,64},{68,... | collective-permute-start | bytes 786440 | tf_op jit(solution)/shard_map/ppermute | solution.py:374
  17.9 5.3 %collective-permute-start = (bf16[4,256,128]{2,1,0:T(8,128)(2,1)S(1)}, bf16[4,256,128]{2,1,0:T(8,128)(2,1)S(1)}, u32[]{:S(2)}, u32[]{:S(2)}) collective-permute-start(bf16[4,256,128]{2,1,0:T(8,128)(2,1)S(1)} %all-to-all-done.x_ref), channel_id=1, source_target_pairs={{0,4},{4,0},{8,12},{12,8},{16,20},{20,16},{24,28},{28,24},{32,36},... | collective-permute-start | bytes 786440 | tf_op jit(solution)/shard_map/ppermute | solution.py:373
  26.5 3.4 %collective-permute-start.2 = (bf16[65,4,512]{2,1,0:T(4,128)(2,1)S(1)}, bf16[65,4,512]{2,1,0:T(4,128)(2,1)S(1)}, u32[]{:S(2)}, u32[]{:S(2)}) collective-permute-start(bf16[65,4,512]{2,1,0:T(4,128)(2,1)S(1)} %get-tuple-element.47), channel_id=1, source_target_pairs={{0,4},{4,0},{8,12},{12,8},{16,20},{20,16},{24,28},{28,24},{32,36},... | collective-permute-start | bytes 798728 | tf_op jit(solution)/shard_map/ppermute | solution.py:410
  30.7 28.7 %all-to-all-start.1 = ((bf16[64,4,384]{2,1,0:T(4,128)(2,1)}), bf16[64,4,384]{2,1,0:T(4,128)(2,1)S(1)}, u32[]{:S(2)}, u32[]{:S(2)}) async-start(bf16[64,4,384]{2,1,0:T(4,128)(2,1)} %shard_map.123), calls=%async_computation.1 | async-start | bytes 393216 | tf_op jit(solution)/shard_map/all_to_all | solution.py:416
  47.1 20.8 %collective-permute-start.3 = (bf16[144,256]{1,0:T(8,128)(2,1)S(1)}, bf16[144,256]{1,0:T(8,128)(2,1)S(1)}, u32[]{:S(2)}, u32[]{:S(2)}) collective-permute-start(bf16[144,256]{1,0:T(8,128)(2,1)S(1)} %get-tuple-element.52), channel_id=1, source_target_pairs={{4,8},{12,16},{20,24},{28,32},{36,40},{44,48},{52,56},{60,64},{68,... | collective-permute-start | bytes 221192 | tf_op jit(solution)/shard_map/ppermute | solution.py:411
  60.3 25.6 %all-to-all-start.2 = ((bf16[128,4,384]{2,1,0:T(4,128)(2,1)}), bf16[128,4,384]{2,1,0:T(4,128)(2,1)S(1)}, u32[]{:S(2)}, u32[]{:S(2)}) async-start(bf16[128,4,384]{2,1,0:T(4,128)(2,1)} %shard_map.124), calls=%async_computation.2 | async-start | bytes 786432 | tf_op jit(solution)/shard_map/all_to_all | solution.py:431
  68.4 8.4 %collective-permute-start.4 = (bf16[256,128]{1,0:T(8,128)(2,1)S(1)}, bf16[256,128]{1,0:T(8,128)(2,1)S(1)}, u32[]{:S(2)}, u32[]{:S(2)}) collective-permute-start(bf16[256,128]{1,0:T(8,128)(2,1)S(1)} %get-tuple-element.53), channel_id=1, source_target_pairs={{0,1},{1,2},{2,3},{3,0},{4,5},{5,6},{6,7},{7,4},{8,9},{9,10},{10,1... | collective-permute-start | bytes 196616 | tf_op jit(solution)/shard_map/ppermute | solution.py:428
  70.6 6.8 %collective-permute-start.5 = (bf16[256,128]{1,0:T(8,128)(2,1)S(1)}, bf16[256,128]{1,0:T(8,128)(2,1)S(1)}, u32[]{:S(2)}, u32[]{:S(2)}) collective-permute-start(bf16[256,128]{1,0:T(8,128)(2,1)S(1)} %get-tuple-element.54), channel_id=1, source_target_pairs={{0,2},{1,3},{2,0},{3,1},{4,6},{5,7},{6,4},{7,5},{8,10},{9,11},{10,... | collective-permute-start | bytes 196616 | tf_op jit(solution)/shard_map/ppermute | solution.py:428
  74.3 5.6 %collective-permute-start.6 = (bf16[256,128]{1,0:T(8,128)(2,1)S(1)}, bf16[256,128]{1,0:T(8,128)(2,1)S(1)}, u32[]{:S(2)}, u32[]{:S(2)}) collective-permute-start(bf16[256,128]{1,0:T(8,128)(2,1)S(1)} %get-tuple-element.55), channel_id=1, source_target_pairs={{0,3},{1,0},{2,1},{3,2},{4,7},{5,4},{6,5},{7,6},{8,11},{9,8},{10,9... | collective-permute-start | bytes 196616 | tf_op jit(solution)/shard_map/ppermute | solution.py:428

commit v7 on v6

--- a/solution.py
+++ b/solution.py
@@ -157,20 +157,18 @@
     e_ref,
     gw_ref,
     xt_ref,
-    att_ref,
+    w_stack,
+    v_all_ref,
     gq_ref,
     gown_ref,
     back_b_ref,
     keep_ref,
     away_ref,
     x_near,
-    dw,
-    wide,
     kv_near,
     q_stack,
     up_stack,
     gs_stack,
-    w_stack,
 ):
     core, before, after = part_ref[0] % 2, table_ref[0, 0] % 2, table_ref[0, 1] % 2
     n = LANES
@@ -197,6 +195,7 @@
     k_near, v_near = near_unit.astype(BF16), kv_near[:, n:].astype(BF16)
     k_round = jnp.concatenate([k_unit_ref[...].astype(BF16), k_near], axis=0)
     v_round = jnp.concatenate([v_ref[...], v_near], axis=0)
+    v_all_ref[...] = v_round
     q_round, up = q_unit_ref[...].astype(BF16), up_ref[...]
     factors = [scale_ref[0] / 64, scale_ref[1] / 64]
     lane_factor = jnp.where(first, factors[0], factors[1])
@@ -223,9 +222,6 @@
     gqn = []
     for b in range(2):
         low, high = slice(2 * b * n, (2 * b + 1) * n), slice((2 * b + 1) * n, (2 * b + 2) * n)
-        at = slice(b * n, (b + 1) * n)
-        att = jnp.where(first, mul(w_stack[low], v_round), mul(w_stack[high], v_round))
-        att_ref[at] = att.astype(BF16)
         gqn.append(jnp.where(first, mul(gs_stack[low], k_round), mul(gs_stack[high], k_round)))
     gqn = jnp.concatenate(gqn, axis=0) * lane_factor
     gkn = mul(q_stack[...], gs_stack[...], TN).T * lane_factor
@@ -241,12 +237,14 @@
     gk_round, gv_round = gk.astype(BF16), gv.astype(BF16)
     g_own = jnp.concatenate([gq, gk_round[: 2 * n], gv_round[: 2 * n]], axis=1)
     g_near = jnp.concatenate([gk_round[2 * n :], gv_round[2 * n :]], axis=1)
-    dw[...] = mul(xt_ref[...], g_own)
-    dw[:, n:] += mul(x_near[...], g_near, TN)
-    for ref, half in ((keep_ref, core), (wide, 1 - core)):
-        rows = pl.ds(pl.multiple_of(half * 2 * n, 2 * n), 2 * n)
-        ref[0:64, :, : 3 * n] = dw[rows, :].reshape(64, 4, 3 * n)
-    wide[64] = jnp.full((4, 4 * n), jnp.where(core == 0, after, before), jnp.int32).astype(F32)
+    for half, ref in ((core, keep_ref), (1 - core, away_ref)):
+        at = pl.ds(pl.multiple_of(half * 2 * n, 2 * n), 2 * n)
+        dw = mul(xt_ref[at, :], g_own)
+        far = mul(x_near[:, at], g_near, TN)
+        dw = jnp.concatenate([dw[:, :n], dw[:, n:] + far], axis=1)
+        ref[0:64, :, : 3 * n] = dw.reshape(64, 4, 3 * n).astype(ref.dtype)
+    which = jnp.full((4, 4 * n), jnp.where(core == 0, after, before), jnp.int32)
+    away_ref[64] = which.astype(F32).astype(BF16)
     back_b_ref[n:] = (
         jnp.full((16, 2 * n), jnp.where(core == 0, before, after), jnp.int32)
         .astype(F32)
@@ -254,8 +252,8 @@
     )
 
     def put_sides(near, other):
-        wide[0:32, :, 3 * n :] = gk[near : near + n].reshape(32, 4, n)
-        wide[32:64, :, 3 * n :] = gv[near : near + n].reshape(32, 4, n)
+        away_ref[0:32, :, 3 * n :] = gk[near : near + n].reshape(32, 4, n).astype(BF16)
+        away_ref[32:64, :, 3 * n :] = gv[near : near + n].reshape(32, 4, n).astype(BF16)
         back_b_ref[:n, :n] = gk_round[other : other + n]
         back_b_ref[:n, n:] = gv_round[other : other + n]
 
@@ -267,11 +265,11 @@
     def _():
         put_sides(2 * n, 3 * n)
 
-    away_ref[...] = wide[...].astype(BF16)
-
 
 def input_kernel(
     member_ref,
+    w_ref,
+    v_ref,
     gq_ref,
     gown_ref,
     swapped_ref,
@@ -279,6 +277,7 @@
     wq_ref,
     wk_ref,
     wv_ref,
+    att_ref,
     own_ref,
     one_ref,
     two_ref,
@@ -303,6 +302,12 @@
     part += mul(g[:, n:], wv_ref[...], NT)
     for i in range(4):
         pieces[i] = part[:, i * n : (i + 1) * n]
+    first, _ = head_lanes()
+    v_all = v_ref[...]
+    for b in range(2):
+        low, high = slice(2 * b * n, (2 * b + 1) * n), slice((2 * b + 1) * n, (2 * b + 2) * n)
+        att = jnp.where(first, mul(w_ref[low], v_all), mul(w_ref[high], v_all))
+        att_ref[b * n : (b + 1) * n] = att.astype(BF16)
     member = member_ref[0]
     own_ref[...] = pieces[member]
     for step, ref in enumerate((one_ref, two_ref, three_ref)):
@@ -382,10 +387,11 @@
         flops=3_000_000_000,
         moved=3_000_000,
     )(scales, gathered, wq, wk, wv, up, count)
-    att, gq, gown, back_b, keep, away = call(
+    w_all, v_all, gq, gown, back_b, keep, away = call(
         attend_kernel,
         (
-            shape((256, 128), BF16),
+            shape((512, 512), BF16),
+            shape((512, 128), BF16),
             shape((256, 128), BF16),
             shape((256, 256), F32),
             shape((144, 256), BF16),
@@ -395,12 +401,9 @@
         [SMEM, SMEM, SMEM] + [VMEM] * 14,
         [
             pltpu.VMEM((256, 512), BF16),
-            pltpu.VMEM((512, 384), F32),
-            pltpu.VMEM((65, 4, 512), F32),
             pltpu.VMEM((256, 256), F32),
             pltpu.VMEM((512, 128), BF16),
             pltpu.VMEM((512, 128), BF16),
-            pltpu.VMEM((512, 512), BF16),
             pltpu.VMEM((512, 512), BF16),
         ],
         flops=3_000_000_000,
@@ -416,14 +419,14 @@
     got = lax.all_to_all(pieces, "dom", 0, 0, tiled=True, axis_index_groups=groups)
     totals = call(total_kernel, shape((128, 4, 384), BF16), [VMEM], moved=500_000)(got)
     totals, gown = lax.optimization_barrier((totals, gown))
-    own, one, two, three = call(
+    att, own, one, two, three = call(
         input_kernel,
-        (shape((256, 128), F32),) + (shape((256, 128), BF16),) * 3,
-        [SMEM] + [VMEM] * 7,
+        (shape((256, 128), BF16), shape((256, 128), F32)) + (shape((256, 128), BF16),) * 3,
+        [SMEM] + [VMEM] * 9,
         [pltpu.VMEM((65, 4, 128), F32), pltpu.VMEM((4, 256, 128), F32)],
         flops=20_000_000_000,
         moved=1_500_000,
-    )(lax.axis_index("mp").reshape(1), gq, gown, swapped, back_b, wq, wk, wv)
+    )(lax.axis_index("mp").reshape(1), w_all, v_all, gq, gown, swapped, back_b, wq, wk, wv)
     one, two, three = (
         lax.ppermute(v, "mp", [(i, (i + s) % members) for i in range(members)])
         for s, v in ((1, one), (2, two), (3, three))

time: 87.5 us -> 86.8 us (level)
  transfers between devices with their start and end apart: 10 -> 10, of which waited for: 6 -> 6; matrix products, arithmetic and copies ran while one was open for 0% -> 0% of each run, Pallas kernels for 5% -> 6%
where the time goes in v7:
time: 86.8 us; the launch traced here: 86.2 us
  starting transfers between devices  52.4 us (60%)
  waiting for transfers between devices  21.6 us (25%)
  Pallas kernels  9.89 us (11%)
  local copies, waits for them, and re-layouts  1.56 us (2%)
    all_to_all x1, starting transfers between devices, shards(): lax.all_to_all(pieces, 'dom', 0, 0, tiled=True, axis_index_groups=groups)  16.4 us
    all_to_all x1, waiting for transfers between devices, shards(): lax.all_to_all(pieces, 'dom', 0, 0, tiled=True, axis_index_groups=groups)  8.54 us
    ppermute x3, starting transfers between devices, shards(): lax.ppermute(v, 'mp', [(i, (i + s) % members) for i in range(members)])  8.41 us
    all_to_all x1, starting transfers between devices, shards(): mine = lax.all_to_all(totals, 'dom', 0, 0, tiled=True)  7.62 us
    all_to_all x1, waiting for transfers between devices, shards(): mine = lax.all_to_all(totals, 'dom', 0, 0, tiled=True)  5.32 us
    ppermute x1, starting transfers between devices, shards(): xb = lax.ppermute(gathered, 'dom', edges)  5.18 us
    all_to_all x1, starting transfers between devices, shards(): gathered = lax.all_to_all(copies, 'mp', 0, 0, tiled=True)  4.97 us
    ppermute x1, starting transfers between devices, shards(): xa = lax.ppermute(gathered, 'dom', pairs)  3.96 us
  transfers between devices with their start and end apart: 10, of which 6 were waited for; matrix products, arithmetic and copies ran while one was open for 0% of the time, Pallas kernels for 6%

profile of v7, /device:TPU:1, one launch (start us, length us, event | category | flops | bytes accessed | tf_op | source)
XLA Modules:
  0.0 86.2 jit_solution(14540420899559549295)
XLA Ops:
  0.6 0.8 copy-done
  1.5 0.7 shard_map.119
  2.2 5.0 %all-to-all-start = ((bf16[4,256,128]{2,1,0:T(8,128)(2,1)}), bf16[4,256,128]{2,1,0:T(8,128)(2,1)S(1)}, u32[]{:S(2)}, u32[]{:S(2)}) async-start(bf16[4,256,128]{2,1,0:T(8,128)(2,1)} %shard_map.119), calls=%async_computation | async-start | bytes 524288 | tf_op jit(solution)/shard_map/all_to_all | solution.py:365
  7.2 0.0 copy-start.5
  7.2 0.7 copy-done.5
  7.9 0.0 copy-start.6
  7.9 1.4 %shard_map.120.count_ref = bf16[256,512]{1,0:T(8,128)(2,1)S(1)} custom-call(s32[1]{0:T(128)} %bitcast.1.part_ref, s32[2,8]{1,0:T(2,128)S(1)} %copy-done.5, s32[2,9,1024]{2,1,0:T(8,128)S(1)} %copy.13.words_ref), custom_call_target="tpu_custom_call" | custom-call | flops 2000000000 | bytes 400000 | tf_op jit(solution)/shard_map/pallas_call | solution.py:368
  9.4 3.4 %all-to-all-done.x_ref = bf16[4,256,128]{2,1,0:T(8,128)(2,1)S(1)} async-done(((bf16[4,256,128]{2,1,0:T(8,128)(2,1)}), bf16[4,256,128]{2,1,0:T(8,128)(2,1)S(1)}, u32[]{:S(2)}, u32[]{:S(2)}) %all-to-all-start) | async-done | bytes 262176 | tf_op jit(solution)/shard_map/all_to_all | solution.py:365
  12.7 5.2 %collective-permute-start.1 = (bf16[4,256,128]{2,1,0:T(8,128)(2,1)S(1)}, bf16[4,256,128]{2,1,0:T(8,128)(2,1)S(1)}, u32[]{:S(2)}, u32[]{:S(2)}) collective-permute-start(bf16[4,256,128]{2,1,0:T(8,128)(2,1)S(1)} %all-to-all-done.x_ref), channel_id=1, source_target_pairs={{4,8},{12,16},{20,24},{28,32},{36,40},{44,48},{52,56},{60,64},{68,... | collective-permute-start | bytes 786440 | tf_op jit(solution)/shard_map/ppermute | solution.py:379
  17.9 4.0 %collective-permute-start = (bf16[4,256,128]{2,1,0:T(8,128)(2,1)S(1)}, bf16[4,256,128]{2,1,0:T(8,128)(2,1)S(1)}, u32[]{:S(2)}, u32[]{:S(2)}) collective-permute-start(bf16[4,256,128]{2,1,0:T(8,128)(2,1)S(1)} %all-to-all-done.x_ref), channel_id=1, source_target_pairs={{0,4},{4,0},{8,12},{12,8},{16,20},{20,16},{24,28},{28,24},{32,36},... | collective-permute-start | bytes 786440 | tf_op jit(solution)/shard_map/ppermute | solution.py:378
  21.9 1.3 %shard_map.121 = (f32[256,128]{1,0:T(8,128)S(1)}, f32[256,128]{1,0:T(8,128)S(1)}, f32[256,128]{1,0:T(8,128)S(1)}, f32[256,128]{1,0:T(8,128)S(1)}, bf16[256,128]{...) custom-call(f32[2]{0:T(128)S(1)} %copy-done.6, ...), custom_call_target="tpu_custom_call" | custom-call | flops 3000000000 | bytes 3000000 | tf_op jit(solution)/shard_map/pallas_call | solution.py:382
  23.2 0.0 collective-permute-done.1.xb_ref
  23.2 0.0 collective-permute-done.xa_ref
  23.2 2.6 %shard_map.122 = (bf16[512,512]{1,0:T(8,128)(2,1)S(1)}, bf16[512,128]{1,0:T(8,128)(2,1)S(1)}, bf16[256,128]{1,0:T(8,128)(2,1)S(1)}, f32[256,256]{1,0:T(8,128)S(1...) custom-call(s32[1]{0:T(128)} %bitcast.1.part_ref, ...), custom_call_target="tpu_custom_call" | custom-call | flops 3000000000 | bytes 4000000 | tf_op jit(solution)/shard_map/pallas_call | solution.py:390
  25.8 2.1 %collective-permute-start.2 = (bf16[65,4,512]{2,1,0:T(4,128)(2,1)S(1)}, bf16[65,4,512]{2,1,0:T(4,128)(2,1)S(1)}, u32[]{:S(2)}, u32[]{:S(2)}) collective-permute-start(bf16[65,4,512]{2,1,0:T(4,128)(2,1)S(1)} %get-tuple-element.51), channel_id=1, source_target_pairs={{0,4},{4,0},{8,12},{12,8},{16,20},{20,16},{24,28},{28,24},{32,36},... | collective-permute-start | bytes 798728 | tf_op jit(solution)/shard_map/ppermute | solution.py:413
  27.9 1.3 %collective-permute-done.2.swapped_ref = bf16[65,4,512]{2,1,0:T(4,128)(2,1)S(1)} collective-permute-done((bf16[65,4,512]{2,1,0:T(4,128)(2,1)S(1)}, bf16[65,4,512]{2,1,0:T(4,128)(2,1)S(1)}, u32[]{:S(2)}, u32[]{:S(2)}) %collective-permute-start.2) | collective-permute-done | bytes 266272 | tf_op jit(solution)/shard_map/ppermute | solution.py:413
  29.2 0.8 shard_map.123
  30.0 16.4 %all-to-all-start.1 = ((bf16[64,4,384]{2,1,0:T(4,128)(2,1)}), bf16[64,4,384]{2,1,0:T(4,128)(2,1)S(1)}, u32[]{:S(2)}, u32[]{:S(2)}) async-start(bf16[64,4,384]{2,1,0:T(4,128)(2,1)} %shard_map.123), calls=%async_computation.1 | async-start | bytes 393216 | tf_op jit(solution)/shard_map/all_to_all | solution.py:419
  46.4 3.7 %collective-permute-start.3 = (bf16[144,256]{1,0:T(8,128)(2,1)S(1)}, bf16[144,256]{1,0:T(8,128)(2,1)S(1)}, u32[]{:S(2)}, u32[]{:S(2)}) collective-permute-start(bf16[144,256]{1,0:T(8,128)(2,1)S(1)} %get-tuple-element.54), channel_id=1, source_target_pairs={{4,8},{12,16},{20,24},{28,32},{36,40},{44,48},{52,56},{60,64},{68,... | collective-permute-start | bytes 221192 | tf_op jit(solution)/shard_map/ppermute | solution.py:414
  50.2 8.5 %all-to-all-done.1.got_ref = bf16[64,4,384]{2,1,0:T(4,128)(2,1)S(1)} async-done(((bf16[64,4,384]{2,1,0:T(4,128)(2,1)}), bf16[64,4,384]{2,1,0:T(4,128)(2,1)S(1)}, u32[]{:S(2)}, u32[]{:S(2)}) %all-to-all-start.1) | async-done | bytes 196640 | tf_op jit(solution)/shard_map/all_to_all | solution.py:419
  58.7 0.9 %shard_map.124 = bf16[128,4,384]{2,1,0:T(4,128)(2,1)} custom-call(bf16[64,4,384]{2,1,0:T(4,128)(2,1)S(1)} %all-to-all-done.1.got_ref), custom_call_target="tpu_custom_call" | custom-call | bytes 500000 | tf_op jit(solution)/shard_map/pallas_call | solution.py:420
  59.6 7.6 %all-to-all-start.2 = ((bf16[128,4,384]{2,1,0:T(4,128)(2,1)}), bf16[128,4,384]{2,1,0:T(4,128)(2,1)S(1)}, u32[]{:S(2)}, u32[]{:S(2)}) async-start(bf16[128,4,384]{2,1,0:T(4,128)(2,1)} %shard_map.124), calls=%async_computation.2 | async-start | bytes 786432 | tf_op jit(solution)/shard_map/all_to_all | solution.py:434
  67.2 0.0 collective-permute-done.3.back_b_ref
  67.2 1.2 %shard_map.125 = (bf16[256,128]{1,0:T(8,128)(2,1)}, f32[256,128]{1,0:T(8,128)S(1)}, bf16[256,128]{1,0:T(8,128)(2,1)S(1)}, bf16[256,128]{1,0:T(8,128)(2,1)S(1)}, bf16[256,128]{1,0:T(8,128)(2,1)S(1)}) custom-call(s32[1]{0:T(128)} %bitcast.member_ref, bf16[512,512]{1,0:T(8,128)(2,1)S(1)} %get-tuple-element.47.w_ref, ...), custom_call_target="tpu_custom_call" | custom-call | flops 20000000000 | bytes 1500000 | tf_op jit(solution)/shard_map/pallas_call | solution.py:422
  68.5 2.2 %collective-permute-start.4 = (bf16[256,128]{1,0:T(8,128)(2,1)S(1)}, bf16[256,128]{1,0:T(8,128)(2,1)S(1)}, u32[]{:S(2)}, u32[]{:S(2)}) collective-permute-start(bf16[256,128]{1,0:T(8,128)(2,1)S(1)} %get-tuple-element.57), channel_id=1, source_target_pairs={{0,1},{1,2},{2,3},{3,0},{4,5},{5,6},{6,7},{7,4},{8,9},{9,10},{10,1... | collective-permute-start | bytes 196616 | tf_op jit(solution)/shard_map/ppermute | solution.py:431
  70.7 3.7 %collective-permute-start.5 = (bf16[256,128]{1,0:T(8,128)(2,1)S(1)}, bf16[256,128]{1,0:T(8,128)(2,1)S(1)}, u32[]{:S(2)}, u32[]{:S(2)}) collective-permute-start(bf16[256,128]{1,0:T(8,128)(2,1)S(1)} %get-tuple-element.58), channel_id=1, source_target_pairs={{0,2},{1,3},{2,0},{3,1},{4,6},{5,7},{6,4},{7,5},{8,10},{9,11},{10,... | collective-permute-start | bytes 196616 | tf_op jit(solution)/shard_map/ppermute | solution.py:431
  74.3 2.5 %collective-permute-start.6 = (bf16[256,128]{1,0:T(8,128)(2,1)S(1)}, bf16[256,128]{1,0:T(8,128)(2,1)S(1)}, u32[]{:S(2)}, u32[]{:S(2)}) collective-permute-start(bf16[256,128]{1,0:T(8,128)(2,1)S(1)} %get-tuple-element.59), channel_id=1, source_target_pairs={{0,3},{1,0},{2,1},{3,2},{4,7},{5,4},{6,5},{7,6},{8,11},{9,8},{10,9... | collective-permute-start | bytes 196616 | tf_op jit(solution)/shard_map/ppermute | solution.py:431
  76.9 0.0 collective-permute-done.4.refs_2_
  76.9 0.6 collective-permute-done.5.refs_3_
  77.5 2.4 %collective-permute-done.6.refs_4_ = bf16[256,128]{1,0:T(8,128)(2,1)S(1)} collective-permute-done((bf16[256,128]{1,0:T(8,128)(2,1)S(1)}, bf16[256,128]{1,0:T(8,128)(2,1)S(1)}, u32[]{:S(2)}, u32[]{:S(2)}) %collective-permute-start.6) | collective-permute-done | bytes 65568 | tf_op jit(solution)/shard_map/ppermute | solution.py:431
  79.9 5.3 %all-to-all-done.2 = bf16[128,4,384]{2,1,0:T(4,128)(2,1)S(1)} async-done(((bf16[128,4,384]{2,1,0:T(4,128)(2,1)}), bf16[128,4,384]{2,1,0:T(4,128)(2,1)S(1)}, u32[]{:S(2)}, u32[]{:S(2)}) %all-to-all-start.2) | async-done | bytes 393248 | tf_op jit(solution)/shard_map/all_to_all | solution.py:434
  85.2 1.0 %shard_map.126 = (f32[512,128]{1,0:T(8,128)}, f32[512,128]{1,0:T(8,128)}, f32[512,128]{1,0:T(8,128)}, bf16[256,128]{1,0:T(8,128)(2,1)}) custom-call(bf16[64,2,4,384]{3,2,1,0:T(4,128)(2,1)S(1)} %bitcast.3, f32[256,128]{1,0:T(8,128)S(1)} %get-tuple-element.61.refs_1_, bf16[256,128]{1,0:T(8,128)(2,1)S(1)} %collective-permute-done.4.refs_2_, ...), custom_call_target="tpu_custom_call" | custom-call | bytes 1500000 | tf_op jit(solution)/shard_map/pallas_call | solution.py:441
  (13 shorter events, 0.1 us)
Async XLA Ops:
  0.6 0.8 copy-start
  2.2 5.0 %copy-start.7 = (s32[2,9,1024]{2,0,1:T(2,128)S(1)}, s32[2,9,1024]{2,0,1:T(2,128)}, u32[]{:S(2)}) copy-start(s32[2,9,1024]{2,0,1:T(2,128)} %param.15) | copy-start | bytes 221188
  2.2 10.5 %all-to-all-start = ((bf16[4,256,128]{2,1,0:T(8,128)(2,1)}), bf16[4,256,128]{2,1,0:T(8,128)(2,1)S(1)}, u32[]{:S(2)}, u32[]{:S(2)}) async-start(bf16[4,256,128]{2,1,0:T(8,128)(2,1)} %shard_map.119), calls=%async_computation | async-start | bytes 524288 | tf_op jit(solution)/shard_map/all_to_all | solution.py:365
  7.2 0.7 copy-start.5
  7.9 14.0 %copy-start.1 = (bf16[512,128]{1,0:T(8,128)(2,1)S(1)}, bf16[512,128]{1,0:T(8,128)(2,1)}, u32[]{:S(2)}) copy-start(bf16[512,128]{1,0:T(8,128)(2,1)} %wk_ref.5) | copy-start | bytes 393220
  7.9 14.0 %copy-start.2 = (bf16[512,128]{1,0:T(8,128)(2,1)S(1)}, bf16[512,128]{1,0:T(8,128)(2,1)}, u32[]{:S(2)}) copy-start(bf16[512,128]{1,0:T(8,128)(2,1)} %wv_ref.5) | copy-start | bytes 393220
  7.9 14.0 %copy-start.3 = (bf16[512,128]{1,0:T(8,128)(2,1)S(1)}, bf16[512,128]{1,0:T(8,128)(2,1)}, u32[]{:S(2)}) copy-start(bf16[512,128]{1,0:T(8,128)(2,1)} %wq_ref.3) | copy-start | bytes 393220
  7.9 14.0 %copy-start.4 = (bf16[256,128]{1,0:T(8,128)(2,1)S(1)}, bf16[256,128]{1,0:T(8,128)(2,1)}, u32[]{:S(2)}) copy-start(bf16[256,128]{1,0:T(8,128)(2,1)} %up_ref.3) | copy-start | bytes 196612
  7.9 14.0 %copy-start.6 = (f32[2]{0:T(128)S(1)}, f32[2]{0:T(128)}, u32[]{:S(2)}) copy-start(f32[2]{0:T(128)} %scale_ref.3) | copy-start | bytes 28
  12.7 10.5 %collective-permute-start.1 = (bf16[4,256,128]{2,1,0:T(8,128)(2,1)S(1)}, bf16[4,256,128]{2,1,0:T(8,128)(2,1)S(1)}, u32[]{:S(2)}, u32[]{:S(2)}) collective-permute-start(bf16[4,256,128]{2,1,0:T(8,128)(2,1)S(1)} %all-to-all-done.x_ref), channel_id=1, source_target_pairs={{4,8},{12,16},{20,24},{28,32},{36,40},{44,48},{52,56},{60,64},{68,... | collective-permute-start | bytes 786440 | tf_op jit(solution)/shard_map/ppermute | solution.py:379
  17.9 5.3 %collective-permute-start = (bf16[4,256,128]{2,1,0:T(8,128)(2,1)S(1)}, bf16[4,256,128]{2,1,0:T(8,128)(2,1)S(1)}, u32[]{:S(2)}, u32[]{:S(2)}) collective-permute-start(bf16[4,256,128]{2,1,0:T(8,128)(2,1)S(1)} %all-to-all-done.x_ref), channel_id=1, source_target_pairs={{0,4},{4,0},{8,12},{12,8},{16,20},{20,16},{24,28},{28,24},{32,36},... | collective-permute-start | bytes 786440 | tf_op jit(solution)/shard_map/ppermute | solution.py:378
  25.8 3.4 %collective-permute-start.2 = (bf16[65,4,512]{2,1,0:T(4,128)(2,1)S(1)}, bf16[65,4,512]{2,1,0:T(4,128)(2,1)S(1)}, u32[]{:S(2)}, u32[]{:S(2)}) collective-permute-start(bf16[65,4,512]{2,1,0:T(4,128)(2,1)S(1)} %get-tuple-element.51), channel_id=1, source_target_pairs={{0,4},{4,0},{8,12},{12,8},{16,20},{20,16},{24,28},{28,24},{32,36},... | collective-permute-start | bytes 798728 | tf_op jit(solution)/shard_map/ppermute | solution.py:413
  30.0 28.7 %all-to-all-start.1 = ((bf16[64,4,384]{2,1,0:T(4,128)(2,1)}), bf16[64,4,384]{2,1,0:T(4,128)(2,1)S(1)}, u32[]{:S(2)}, u32[]{:S(2)}) async-start(bf16[64,4,384]{2,1,0:T(4,128)(2,1)} %shard_map.123), calls=%async_computation.1 | async-start | bytes 393216 | tf_op jit(solution)/shard_map/all_to_all | solution.py:419
  46.4 20.8 %collective-permute-start.3 = (bf16[144,256]{1,0:T(8,128)(2,1)S(1)}, bf16[144,256]{1,0:T(8,128)(2,1)S(1)}, u32[]{:S(2)}, u32[]{:S(2)}) collective-permute-start(bf16[144,256]{1,0:T(8,128)(2,1)S(1)} %get-tuple-element.54), channel_id=1, source_target_pairs={{4,8},{12,16},{20,24},{28,32},{36,40},{44,48},{52,56},{60,64},{68,... | collective-permute-start | bytes 221192 | tf_op jit(solution)/shard_map/ppermute | solution.py:414
  59.6 25.6 %all-to-all-start.2 = ((bf16[128,4,384]{2,1,0:T(4,128)(2,1)}), bf16[128,4,384]{2,1,0:T(4,128)(2,1)S(1)}, u32[]{:S(2)}, u32[]{:S(2)}) async-start(bf16[128,4,384]{2,1,0:T(4,128)(2,1)} %shard_map.124), calls=%async_computation.2 | async-start | bytes 786432 | tf_op jit(solution)/shard_map/all_to_all | solution.py:434
  68.5 8.4 %collective-permute-start.4 = (bf16[256,128]{1,0:T(8,128)(2,1)S(1)}, bf16[256,128]{1,0:T(8,128)(2,1)S(1)}, u32[]{:S(2)}, u32[]{:S(2)}) collective-permute-start(bf16[256,128]{1,0:T(8,128)(2,1)S(1)} %get-tuple-element.57), channel_id=1, source_target_pairs={{0,1},{1,2},{2,3},{3,0},{4,5},{5,6},{6,7},{7,4},{8,9},{9,10},{10,1... | collective-permute-start | bytes 196616 | tf_op jit(solution)/shard_map/ppermute | solution.py:431
  70.7 6.8 %collective-permute-start.5 = (bf16[256,128]{1,0:T(8,128)(2,1)S(1)}, bf16[256,128]{1,0:T(8,128)(2,1)S(1)}, u32[]{:S(2)}, u32[]{:S(2)}) collective-permute-start(bf16[256,128]{1,0:T(8,128)(2,1)S(1)} %get-tuple-element.58), channel_id=1, source_target_pairs={{0,2},{1,3},{2,0},{3,1},{4,6},{5,7},{6,4},{7,5},{8,10},{9,11},{10,... | collective-permute-start | bytes 196616 | tf_op jit(solution)/shard_map/ppermute | solution.py:431
  74.3 5.6 %collective-permute-start.6 = (bf16[256,128]{1,0:T(8,128)(2,1)S(1)}, bf16[256,128]{1,0:T(8,128)(2,1)S(1)}, u32[]{:S(2)}, u32[]{:S(2)}) collective-permute-start(bf16[256,128]{1,0:T(8,128)(2,1)S(1)} %get-tuple-element.59), channel_id=1, source_target_pairs={{0,3},{1,0},{2,1},{3,2},{4,7},{5,4},{6,5},{7,6},{8,11},{9,8},{10,9... | collective-permute-start | bytes 196616 | tf_op jit(solution)/shard_map/ppermute | solution.py:431

commit v8 on v7

--- a/solution.py
+++ b/solution.py
@@ -266,10 +266,18 @@
         put_sides(2 * n, 3 * n)
 
 
+def attended_kernel(w_ref, v_ref, att_ref):
+    n = LANES
+    first, _ = head_lanes()
+    v_all = v_ref[...]
+    for b in range(2):
+        low, high = slice(2 * b * n, (2 * b + 1) * n), slice((2 * b + 1) * n, (2 * b + 2) * n)
+        att = jnp.where(first, mul(w_ref[low], v_all), mul(w_ref[high], v_all))
+        att_ref[b * n : (b + 1) * n] = att.astype(BF16)
+
+
 def input_kernel(
     member_ref,
-    w_ref,
-    v_ref,
     gq_ref,
     gown_ref,
     swapped_ref,
@@ -277,7 +285,6 @@
     wq_ref,
     wk_ref,
     wv_ref,
-    att_ref,
     own_ref,
     one_ref,
     two_ref,
@@ -302,12 +309,6 @@
     part += mul(g[:, n:], wv_ref[...], NT)
     for i in range(4):
         pieces[i] = part[:, i * n : (i + 1) * n]
-    first, _ = head_lanes()
-    v_all = v_ref[...]
-    for b in range(2):
-        low, high = slice(2 * b * n, (2 * b + 1) * n), slice((2 * b + 1) * n, (2 * b + 2) * n)
-        att = jnp.where(first, mul(w_ref[low], v_all), mul(w_ref[high], v_all))
-        att_ref[b * n : (b + 1) * n] = att.astype(BF16)
     member = member_ref[0]
     own_ref[...] = pieces[member]
     for step, ref in enumerate((one_ref, two_ref, three_ref)):
@@ -416,17 +417,26 @@
         keep, swapped
     )
     groups = [[2 * i + c for i in range(parts // 2)] for c in range(2)]
+    pieces, w_all = lax.optimization_barrier((pieces, w_all))
+    att = call(
+        attended_kernel,
+        shape((256, 128), BF16),
+        [VMEM] * 2,
+        flops=500_000_000,
+        moved=800_000,
+    )(w_all, v_all)
     got = lax.all_to_all(pieces, "dom", 0, 0, tiled=True, axis_index_groups=groups)
+    got, att = lax.optimization_barrier((got, att))
     totals = call(total_kernel, shape((128, 4, 384), BF16), [VMEM], moved=500_000)(got)
     totals, gown = lax.optimization_barrier((totals, gown))
-    att, own, one, two, three = call(
+    own, one, two, three = call(
         input_kernel,
-        (shape((256, 128), BF16), shape((256, 128), F32)) + (shape((256, 128), BF16),) * 3,
-        [SMEM] + [VMEM] * 9,
+        (shape((256, 128), F32),) + (shape((256, 128), BF16),) * 3,
+        [SMEM] + [VMEM] * 7,
         [pltpu.VMEM((65, 4, 128), F32), pltpu.VMEM((4, 256, 128), F32)],
         flops=20_000_000_000,
         moved=1_500_000,
-    )(lax.axis_index("mp").reshape(1), w_all, v_all, gq, gown, swapped, back_b, wq, wk, wv)
+    )(lax.axis_index("mp").reshape(1), gq, gown, swapped, back_b, wq, wk, wv)
     one, two, three = (
         lax.ppermute(v, "mp", [(i, (i + s) % members) for i in range(members)])
         for s, v in ((1, one), (2, two), (3, three))

time: 86.8 us -> 86.8 us (level)
    all_to_all x1, waiting for transfers between devices: 8.54 us -> 7.62 us  [shards(): lax.all_to_all(pieces, 'dom', 0, 0, tiled=True, axis_index_groups=groups)]
where the time goes in v8:
time: 86.8 us; the launch traced here: 86.2 us
  starting transfers between devices  52.4 us (60%)
  waiting for transfers between devices  21.4 us (25%)
  Pallas kernels  10 us (12%)
  local copies, waits for them, and re-layouts  1.56 us (2%)
    all_to_all x1, starting transfers between devices, shards(): lax.all_to_all(pieces, 'dom', 0, 0, tiled=True, axis_index_groups=groups)  16.4 us
    ppermute x3, starting transfers between devices, shards(): lax.ppermute(v, 'mp', [(i, (i + s) % members) for i in range(members)])  8.42 us
    all_to_all x1, starting transfers between devices, shards(): mine = lax.all_to_all(totals, 'dom', 0, 0, tiled=True)  7.62 us
    all_to_all x1, waiting for transfers between devices, shards(): lax.all_to_all(pieces, 'dom', 0, 0, tiled=True, axis_index_groups=groups)  7.62 us
    all_to_all x1, waiting for transfers between devices, shards(): mine = lax.all_to_all(totals, 'dom', 0, 0, tiled=True)  6.08 us
    ppermute x1, starting transfers between devices, shards(): xb = lax.ppermute(gathered, 'dom', edges)  5.18 us
    all_to_all x1, starting transfers between devices, shards(): gathered = lax.all_to_all(copies, 'mp', 0, 0, tiled=True)  4.97 us
    ppermute x1, starting transfers between devices, shards(): xa = lax.ppermute(gathered, 'dom', pairs)  3.96 us
  transfers between devices with their start and end apart: 10, of which 6 were waited for; matrix products, arithmetic and copies ran while one was open for 0% of the time, Pallas kernels for 6%

profile of v8, /device:TPU:1, one launch (start us, length us, event | category | flops | bytes accessed | tf_op | source)
XLA Modules:
  0.0 86.2 jit_solution(7475196250802965327)
XLA Ops:
  0.6 0.8 copy-done
  1.5 0.7 shard_map.119
  2.2 5.0 %all-to-all-start = ((bf16[4,256,128]{2,1,0:T(8,128)(2,1)}), bf16[4,256,128]{2,1,0:T(8,128)(2,1)S(1)}, u32[]{:S(2)}, u32[]{:S(2)}) async-start(bf16[4,256,128]{2,1,0:T(8,128)(2,1)} %shard_map.119), calls=%async_computation | async-start | bytes 524288 | tf_op jit(solution)/shard_map/all_to_all | solution.py:366
  7.2 0.0 copy-start.5
  7.2 0.7 copy-done.5
  7.9 0.0 copy-start.6
  7.9 1.4 %shard_map.120.count_ref = bf16[256,512]{1,0:T(8,128)(2,1)S(1)} custom-call(s32[1]{0:T(128)} %bitcast.part_ref, s32[2,8]{1,0:T(2,128)S(1)} %copy-done.5, s32[2,9,1024]{2,1,0:T(8,128)S(1)} %copy.13.words_ref), custom_call_target="tpu_custom_call" | custom-call | flops 2000000000 | bytes 400000 | tf_op jit(solution)/shard_map/pallas_call | solution.py:369
  9.4 3.4 %all-to-all-done.x_ref = bf16[4,256,128]{2,1,0:T(8,128)(2,1)S(1)} async-done(((bf16[4,256,128]{2,1,0:T(8,128)(2,1)}), bf16[4,256,128]{2,1,0:T(8,128)(2,1)S(1)}, u32[]{:S(2)}, u32[]{:S(2)}) %all-to-all-start) | async-done | bytes 262176 | tf_op jit(solution)/shard_map/all_to_all | solution.py:366
  12.7 5.2 %collective-permute-start.1 = (bf16[4,256,128]{2,1,0:T(8,128)(2,1)S(1)}, bf16[4,256,128]{2,1,0:T(8,128)(2,1)S(1)}, u32[]{:S(2)}, u32[]{:S(2)}) collective-permute-start(bf16[4,256,128]{2,1,0:T(8,128)(2,1)S(1)} %all-to-all-done.x_ref), channel_id=1, source_target_pairs={{4,8},{12,16},{20,24},{28,32},{36,40},{44,48},{52,56},{60,64},{68,... | collective-permute-start | bytes 786440 | tf_op jit(solution)/shard_map/ppermute | solution.py:380
  17.9 4.0 %collective-permute-start = (bf16[4,256,128]{2,1,0:T(8,128)(2,1)S(1)}, bf16[4,256,128]{2,1,0:T(8,128)(2,1)S(1)}, u32[]{:S(2)}, u32[]{:S(2)}) collective-permute-start(bf16[4,256,128]{2,1,0:T(8,128)(2,1)S(1)} %all-to-all-done.x_ref), channel_id=1, source_target_pairs={{0,4},{4,0},{8,12},{12,8},{16,20},{20,16},{24,28},{28,24},{32,36},... | collective-permute-start | bytes 786440 | tf_op jit(solution)/shard_map/ppermute | solution.py:379
  21.9 1.3 %shard_map.121 = (f32[256,128]{1,0:T(8,128)S(1)}, f32[256,128]{1,0:T(8,128)S(1)}, f32[256,128]{1,0:T(8,128)S(1)}, f32[256,128]{1,0:T(8,128)S(1)}, bf16[256,128]{...) custom-call(f32[2]{0:T(128)S(1)} %copy-done.6, ...), custom_call_target="tpu_custom_call" | custom-call | flops 3000000000 | bytes 3000000 | tf_op jit(solution)/shard_map/pallas_call | solution.py:383
  23.2 0.0 collective-permute-done.1.xb_ref
  23.2 0.0 collective-permute-done.xa_ref
  23.2 2.5 %shard_map.122 = (bf16[512,512]{1,0:T(8,128)(2,1)S(1)}, bf16[512,128]{1,0:T(8,128)(2,1)S(1)}, bf16[256,128]{1,0:T(8,128)(2,1)S(1)}, f32[256,256]{1,0:T(8,128)S(1...) custom-call(s32[1]{0:T(128)} %bitcast.part_ref, ...), custom_call_target="tpu_custom_call" | custom-call | flops 3000000000 | bytes 4000000 | tf_op jit(solution)/shard_map/pallas_call | solution.py:391
  25.8 2.1 %collective-permute-start.2 = (bf16[65,4,512]{2,1,0:T(4,128)(2,1)S(1)}, bf16[65,4,512]{2,1,0:T(4,128)(2,1)S(1)}, u32[]{:S(2)}, u32[]{:S(2)}) collective-permute-start(bf16[65,4,512]{2,1,0:T(4,128)(2,1)S(1)} %get-tuple-element.51), channel_id=1, source_target_pairs={{0,4},{4,0},{8,12},{12,8},{16,20},{20,16},{24,28},{28,24},{32,36},... | collective-permute-start | bytes 798728 | tf_op jit(solution)/shard_map/ppermute | solution.py:414
  27.9 1.3 %collective-permute-done.2.swapped_ref = bf16[65,4,512]{2,1,0:T(4,128)(2,1)S(1)} collective-permute-done((bf16[65,4,512]{2,1,0:T(4,128)(2,1)S(1)}, bf16[65,4,512]{2,1,0:T(4,128)(2,1)S(1)}, u32[]{:S(2)}, u32[]{:S(2)}) %collective-permute-start.2) | collective-permute-done | bytes 266272 | tf_op jit(solution)/shard_map/ppermute | solution.py:414
  29.2 0.8 shard_map.123
  30.0 16.4 %all-to-all-start.1 = ((bf16[64,4,384]{2,1,0:T(4,128)(2,1)}), bf16[64,4,384]{2,1,0:T(4,128)(2,1)S(1)}, u32[]{:S(2)}, u32[]{:S(2)}) async-start(bf16[64,4,384]{2,1,0:T(4,128)(2,1)} %shard_map.123), calls=%async_computation.1 | async-start | bytes 393216 | tf_op jit(solution)/shard_map/all_to_all | solution.py:428
  46.4 3.7 %collective-permute-start.3 = (bf16[144,256]{1,0:T(8,128)(2,1)S(1)}, bf16[144,256]{1,0:T(8,128)(2,1)S(1)}, u32[]{:S(2)}, u32[]{:S(2)}) collective-permute-start(bf16[144,256]{1,0:T(8,128)(2,1)S(1)} %get-tuple-element.62), channel_id=1, source_target_pairs={{4,8},{12,16},{20,24},{28,32},{36,40},{44,48},{52,56},{60,64},{68,... | collective-permute-start | bytes 221192 | tf_op jit(solution)/shard_map/ppermute | solution.py:415
  50.2 0.9 %shard_map.124 = bf16[256,128]{1,0:T(8,128)(2,1)} custom-call(bf16[512,512]{1,0:T(8,128)(2,1)S(1)} %get-tuple-element.54.w_ref, bf16[512,128]{1,0:T(8,128)(2,1)S(1)} %get-tuple-element.55.v_ref), custom_call_target="tpu_custom_call" | custom-call | flops 500000000 | bytes 800000 | tf_op jit(solution)/shard_map/pallas_call | solution.py:421
  51.1 7.6 %all-to-all-done.1.got_ref = bf16[64,4,384]{2,1,0:T(4,128)(2,1)S(1)} async-done(((bf16[64,4,384]{2,1,0:T(4,128)(2,1)}), bf16[64,4,384]{2,1,0:T(4,128)(2,1)S(1)}, u32[]{:S(2)}, u32[]{:S(2)}) %all-to-all-start.1) | async-done | bytes 196640 | tf_op jit(solution)/shard_map/all_to_all | solution.py:428
  58.7 0.9 %shard_map.125 = bf16[128,4,384]{2,1,0:T(4,128)(2,1)} custom-call(bf16[64,4,384]{2,1,0:T(4,128)(2,1)S(1)} %all-to-all-done.1.got_ref), custom_call_target="tpu_custom_call" | custom-call | bytes 500000 | tf_op jit(solution)/shard_map/pallas_call | solution.py:430
  59.6 7.6 %all-to-all-start.2 = ((bf16[128,4,384]{2,1,0:T(4,128)(2,1)}), bf16[128,4,384]{2,1,0:T(4,128)(2,1)S(1)}, u32[]{:S(2)}, u32[]{:S(2)}) async-start(bf16[128,4,384]{2,1,0:T(4,128)(2,1)} %shard_map.125), calls=%async_computation.2 | async-start | bytes 786432 | tf_op jit(solution)/shard_map/all_to_all | solution.py:444
  67.2 0.0 collective-permute-done.3.back_b_ref
  67.2 0.5 shard_map.126
  67.7 2.2 %collective-permute-start.4 = (bf16[256,128]{1,0:T(8,128)(2,1)S(1)}, bf16[256,128]{1,0:T(8,128)(2,1)S(1)}, u32[]{:S(2)}, u32[]{:S(2)}) collective-permute-start(bf16[256,128]{1,0:T(8,128)(2,1)S(1)} %get-tuple-element.63), channel_id=1, source_target_pairs={{0,1},{1,2},{2,3},{3,0},{4,5},{5,6},{6,7},{7,4},{8,9},{9,10},{10,1... | collective-permute-start | bytes 196616 | tf_op jit(solution)/shard_map/ppermute | solution.py:441
  69.9 3.7 %collective-permute-start.5 = (bf16[256,128]{1,0:T(8,128)(2,1)S(1)}, bf16[256,128]{1,0:T(8,128)(2,1)S(1)}, u32[]{:S(2)}, u32[]{:S(2)}) collective-permute-start(bf16[256,128]{1,0:T(8,128)(2,1)S(1)} %get-tuple-element.64), channel_id=1, source_target_pairs={{0,2},{1,3},{2,0},{3,1},{4,6},{5,7},{6,4},{7,5},{8,10},{9,11},{10,... | collective-permute-start | bytes 196616 | tf_op jit(solution)/shard_map/ppermute | solution.py:441
  73.6 2.5 %collective-permute-start.6 = (bf16[256,128]{1,0:T(8,128)(2,1)S(1)}, bf16[256,128]{1,0:T(8,128)(2,1)S(1)}, u32[]{:S(2)}, u32[]{:S(2)}) collective-permute-start(bf16[256,128]{1,0:T(8,128)(2,1)S(1)} %get-tuple-element.65), channel_id=1, source_target_pairs={{0,3},{1,0},{2,1},{3,2},{4,7},{5,4},{6,5},{7,6},{8,11},{9,8},{10,9... | collective-permute-start | bytes 196616 | tf_op jit(solution)/shard_map/ppermute | solution.py:441
  76.1 0.6 collective-permute-done.5.refs_3_
  76.7 2.4 %collective-permute-done.6.refs_4_ = bf16[256,128]{1,0:T(8,128)(2,1)S(1)} collective-permute-done((bf16[256,128]{1,0:T(8,128)(2,1)S(1)}, bf16[256,128]{1,0:T(8,128)(2,1)S(1)}, u32[]{:S(2)}, u32[]{:S(2)}) %collective-permute-start.6) | collective-permute-done | bytes 65568 | tf_op jit(solution)/shard_map/ppermute | solution.py:441
  79.1 6.1 %all-to-all-done.2 = bf16[128,4,384]{2,1,0:T(4,128)(2,1)S(1)} async-done(((bf16[128,4,384]{2,1,0:T(4,128)(2,1)}), bf16[128,4,384]{2,1,0:T(4,128)(2,1)S(1)}, u32[]{:S(2)}, u32[]{:S(2)}) %all-to-all-start.2) | async-done | bytes 393248 | tf_op jit(solution)/shard_map/all_to_all | solution.py:444
  85.2 1.0 %shard_map.127 = (f32[512,128]{1,0:T(8,128)}, f32[512,128]{1,0:T(8,128)}, f32[512,128]{1,0:T(8,128)}, bf16[256,128]{1,0:T(8,128)(2,1)}) custom-call(bf16[64,2,4,384]{3,2,1,0:T(4,128)(2,1)S(1)} %bitcast.3, f32[256,128]{1,0:T(8,128)S(1)} %get-tuple-element.67.refs_1_, bf16[256,128]{1,0:T(8,128)(2,1)S(1)} %collective-permute-done.4.refs_2_, ...), custom_call_target="tpu_custom_call" | custom-call | bytes 1500000 | tf_op jit(solution)/shard_map/pallas_call | solution.py:451
  (14 shorter events, 0.1 us)
Async XLA Ops:
  0.6 0.8 copy-start
  2.2 5.0 %copy-start.7 = (s32[2,9,1024]{2,0,1:T(2,128)S(1)}, s32[2,9,1024]{2,0,1:T(2,128)}, u32[]{:S(2)}) copy-start(s32[2,9,1024]{2,0,1:T(2,128)} %param.15) | copy-start | bytes 221188
  2.2 10.5 %all-to-all-start = ((bf16[4,256,128]{2,1,0:T(8,128)(2,1)}), bf16[4,256,128]{2,1,0:T(8,128)(2,1)S(1)}, u32[]{:S(2)}, u32[]{:S(2)}) async-start(bf16[4,256,128]{2,1,0:T(8,128)(2,1)} %shard_map.119), calls=%async_computation | async-start | bytes 524288 | tf_op jit(solution)/shard_map/all_to_all | solution.py:366
  7.2 0.7 copy-start.5
  7.9 14.0 %copy-start.1 = (bf16[512,128]{1,0:T(8,128)(2,1)S(1)}, bf16[512,128]{1,0:T(8,128)(2,1)}, u32[]{:S(2)}) copy-start(bf16[512,128]{1,0:T(8,128)(2,1)} %wk_ref.5) | copy-start | bytes 393220
  7.9 14.0 %copy-start.2 = (bf16[512,128]{1,0:T(8,128)(2,1)S(1)}, bf16[512,128]{1,0:T(8,128)(2,1)}, u32[]{:S(2)}) copy-start(bf16[512,128]{1,0:T(8,128)(2,1)} %wv_ref.5) | copy-start | bytes 393220
  7.9 14.0 %copy-start.3 = (bf16[512,128]{1,0:T(8,128)(2,1)S(1)}, bf16[512,128]{1,0:T(8,128)(2,1)}, u32[]{:S(2)}) copy-start(bf16[512,128]{1,0:T(8,128)(2,1)} %wq_ref.3) | copy-start | bytes 393220
  7.9 14.0 %copy-start.4 = (bf16[256,128]{1,0:T(8,128)(2,1)S(1)}, bf16[256,128]{1,0:T(8,128)(2,1)}, u32[]{:S(2)}) copy-start(bf16[256,128]{1,0:T(8,128)(2,1)} %up_ref.3) | copy-start | bytes 196612
  7.9 14.0 %copy-start.6 = (f32[2]{0:T(128)S(1)}, f32[2]{0:T(128)}, u32[]{:S(2)}) copy-start(f32[2]{0:T(128)} %scale_ref.3) | copy-start | bytes 28
  12.7 10.5 %collective-permute-start.1 = (bf16[4,256,128]{2,1,0:T(8,128)(2,1)S(1)}, bf16[4,256,128]{2,1,0:T(8,128)(2,1)S(1)}, u32[]{:S(2)}, u32[]{:S(2)}) collective-permute-start(bf16[4,256,128]{2,1,0:T(8,128)(2,1)S(1)} %all-to-all-done.x_ref), channel_id=1, source_target_pairs={{4,8},{12,16},{20,24},{28,32},{36,40},{44,48},{52,56},{60,64},{68,... | collective-permute-start | bytes 786440 | tf_op jit(solution)/shard_map/ppermute | solution.py:380
  17.9 5.3 %collective-permute-start = (bf16[4,256,128]{2,1,0:T(8,128)(2,1)S(1)}, bf16[4,256,128]{2,1,0:T(8,128)(2,1)S(1)}, u32[]{:S(2)}, u32[]{:S(2)}) collective-permute-start(bf16[4,256,128]{2,1,0:T(8,128)(2,1)S(1)} %all-to-all-done.x_ref), channel_id=1, source_target_pairs={{0,4},{4,0},{8,12},{12,8},{16,20},{20,16},{24,28},{28,24},{32,36},... | collective-permute-start | bytes 786440 | tf_op jit(solution)/shard_map/ppermute | solution.py:379
  25.8 3.4 %collective-permute-start.2 = (bf16[65,4,512]{2,1,0:T(4,128)(2,1)S(1)}, bf16[65,4,512]{2,1,0:T(4,128)(2,1)S(1)}, u32[]{:S(2)}, u32[]{:S(2)}) collective-permute-start(bf16[65,4,512]{2,1,0:T(4,128)(2,1)S(1)} %get-tuple-element.51), channel_id=1, source_target_pairs={{0,4},{4,0},{8,12},{12,8},{16,20},{20,16},{24,28},{28,24},{32,36},... | collective-permute-start | bytes 798728 | tf_op jit(solution)/shard_map/ppermute | solution.py:414
  30.0 28.7 %all-to-all-start.1 = ((bf16[64,4,384]{2,1,0:T(4,128)(2,1)}), bf16[64,4,384]{2,1,0:T(4,128)(2,1)S(1)}, u32[]{:S(2)}, u32[]{:S(2)}) async-start(bf16[64,4,384]{2,1,0:T(4,128)(2,1)} %shard_map.123), calls=%async_computation.1 | async-start | bytes 393216 | tf_op jit(solution)/shard_map/all_to_all | solution.py:428
  46.4 20.8 %collective-permute-start.3 = (bf16[144,256]{1,0:T(8,128)(2,1)S(1)}, bf16[144,256]{1,0:T(8,128)(2,1)S(1)}, u32[]{:S(2)}, u32[]{:S(2)}) collective-permute-start(bf16[144,256]{1,0:T(8,128)(2,1)S(1)} %get-tuple-element.62), channel_id=1, source_target_pairs={{4,8},{12,16},{20,24},{28,32},{36,40},{44,48},{52,56},{60,64},{68,... | collective-permute-start | bytes 221192 | tf_op jit(solution)/shard_map/ppermute | solution.py:415
  59.6 25.6 %all-to-all-start.2 = ((bf16[128,4,384]{2,1,0:T(4,128)(2,1)}), bf16[128,4,384]{2,1,0:T(4,128)(2,1)S(1)}, u32[]{:S(2)}, u32[]{:S(2)}) async-start(bf16[128,4,384]{2,1,0:T(4,128)(2,1)} %shard_map.125), calls=%async_computation.2 | async-start | bytes 786432 | tf_op jit(solution)/shard_map/all_to_all | solution.py:444
  67.7 8.4 %collective-permute-start.4 = (bf16[256,128]{1,0:T(8,128)(2,1)S(1)}, bf16[256,128]{1,0:T(8,128)(2,1)S(1)}, u32[]{:S(2)}, u32[]{:S(2)}) collective-permute-start(bf16[256,128]{1,0:T(8,128)(2,1)S(1)} %get-tuple-element.63), channel_id=1, source_target_pairs={{0,1},{1,2},{2,3},{3,0},{4,5},{5,6},{6,7},{7,4},{8,9},{9,10},{10,1... | collective-permute-start | bytes 196616 | tf_op jit(solution)/shard_map/ppermute | solution.py:441
  69.9 6.8 %collective-permute-start.5 = (bf16[256,128]{1,0:T(8,128)(2,1)S(1)}, bf16[256,128]{1,0:T(8,128)(2,1)S(1)}, u32[]{:S(2)}, u32[]{:S(2)}) collective-permute-start(bf16[256,128]{1,0:T(8,128)(2,1)S(1)} %get-tuple-element.64), channel_id=1, source_target_pairs={{0,2},{1,3},{2,0},{3,1},{4,6},{5,7},{6,4},{7,5},{8,10},{9,11},{10,... | collective-permute-start | bytes 196616 | tf_op jit(solution)/shard_map/ppermute | solution.py:441
  73.6 5.6 %collective-permute-start.6 = (bf16[256,128]{1,0:T(8,128)(2,1)S(1)}, bf16[256,128]{1,0:T(8,128)(2,1)S(1)}, u32[]{:S(2)}, u32[]{:S(2)}) collective-permute-start(bf16[256,128]{1,0:T(8,128)(2,1)S(1)} %get-tuple-element.65), channel_id=1, source_target_pairs={{0,3},{1,0},{2,1},{3,2},{4,7},{5,4},{6,5},{7,6},{8,11},{9,8},{10,9... | collective-permute-start | bytes 196616 | tf_op jit(solution)/shard_map/ppermute | solution.py:441
